TPU v7x, 32 devices: a whole 2x2x4 slice. The times are simulated.
32 devices in a mesh: grp: 2 (over y), comp: 4 (over z), space: 4 (over x, core).
Axes of the slice: x: 2, y: 2, z: 4, core: 2. Of those that a mesh axis runs over, the one named last changes fastest.
Arguments:
- spectrum: float32 [2304, 4096], P('comp', ('grp', 'space')), parts along dimension 1, may hold values from -6 to 6
- wave_speed: float32 [36], replicated, may hold values from 0.25 to 2
- current_east: float32 [4096], P(('grp', 'space')), parts along dimension 0, may hold values from -3 to 3
- current_north: float32 [4096], P(('grp', 'space')), parts along dimension 0, may hold values from -3 to 3
- substeps: int32 [2304], replicated, may hold values from 1 to 4, as said below
- neighbours: int32 [4, 4096], P(None, ('grp', 'space')), parts along dimension 1, may hold values from 0 to 767, as said below
- blocks: bfloat16 [64, 64, 64], replicated, may hold values from -0.75 to 0.75
- quad_index: int32 [4, 64], replicated, may hold values from 0 to 35
- strength: float32 [64], replicated, may hold values from -1 to 1
Outputs:
- spectrum_out: float32 [2304, 4096], P('comp', ('grp', 'space')), parts along dimension 1
There are 2 independent parts, one for each index of `grp`. A program takes and returns all parts, laid end to end along the dimension named above; an argument that names none is the same for every part. Nothing has to cross between parts.
Inputs may be any that keep to these rules, and one draw needn't show every extreme that they name: `substeps`: component 0 takes 4. `neighbours`: the entry of row r for the slab's point q (counted within its slab) is q + 128 + o, with -128 <= o <= -1 for rows 0 and 2 and 1 <= o <= 128 for rows 1 and 3.
All inputs are finite; a program needn't handle non-finite values.
Results may differ from a plain program's by a relative error of at most 0.00031.
Values sent between devices are 32-bit elements; how exact they have to be, the bound alone decides.
No kernel may reach another device: no remote copies, remote signals or barrier semaphores. Data moves between devices by JAX's collectives and lax.ppermute only.
A program may use at most 64 MiB of HBM per device.

v0:
```python
import math

import jax
import jax.numpy as jnp
from jax import lax
from jax.sharding import PartitionSpec as P

NF = 36
ND = 64
SUB = 4
HALO = 128


courant_scale = 0.4
courant_limit = 0.45
source_step = 0.1


def padded(cells, sides, width):
    for axis, dim in sides:
        count = lax.axis_size(axis)
        ends = count - 1
        head = lax.slice_in_dim(cells, 0, width, axis=dim)
        tail = lax.slice_in_dim(cells, cells.shape[dim] - width, cells.shape[dim], axis=dim)
        cells = jnp.concatenate(
            [
                lax.ppermute(tail, axis, [(i, (i + 1) % count) for i in range(ends)]),
                cells,
                lax.ppermute(head, axis, [((i + 1) % count, i) for i in range(ends)]),
            ],
            axis=dim,
        )
    return cells


def upwind(spectra, first_comp, substeps, wave_speed, current_east, current_north, neighbours):
    row_count = spectra.shape[0]
    components = first_comp + jnp.arange(row_count, dtype=jnp.int32)
    frequency = components // ND
    angles = ((components % ND).astype(jnp.float32) + 0.5) * (2.0 * math.pi / ND)
    matches = frequency[:, None] == jnp.arange(NF, dtype=jnp.int32)[None, :]
    group_speed = jnp.sum(jnp.where(matches, wave_speed[None, :], 0.0), axis=1)
    counts = lax.dynamic_slice_in_dim(substeps, first_comp, row_count)
    divisor = counts.astype(jnp.float32)[:, None]
    along_x = jnp.clip(
        ((group_speed * jnp.cos(angles))[:, None] + current_east[None, :])
        * courant_scale
        / divisor,
        -courant_limit,
        courant_limit,
    )
    along_y = jnp.clip(
        ((group_speed * jnp.sin(angles))[:, None] + current_north[None, :])
        * courant_scale
        / divisor,
        -courant_limit,
        courant_limit,
    )
    pos_x = jnp.maximum(along_x, 0.0)
    neg_x = jnp.minimum(along_x, 0.0)
    pos_y = jnp.maximum(along_y, 0.0)
    neg_y = jnp.minimum(along_y, 0.0)

    def sweep_once(repeat, values):
        extended = padded(values, (("space", 1),), HALO)
        west_value = jnp.take(extended, neighbours[0], axis=1)
        east_value = jnp.take(extended, neighbours[1], axis=1)
        south_value = jnp.take(extended, neighbours[2], axis=1)
        north_value = jnp.take(extended, neighbours[3], axis=1)
        updated = (
            values
            - pos_x * (values - west_value)
            - neg_x * (east_value - values)
            - pos_y * (values - south_value)
            - neg_y * (north_value - values)
        )
        return jnp.where(repeat < counts[:, None], updated, values)

    return lax.fori_loop(0, SUB, sweep_once, spectra)


def to_points(spectra, peers):
    row_count, columns = spectra.shape
    pieces = spectra.reshape(row_count, peers, columns // peers)
    arrived = lax.all_to_all(pieces, "comp", split_axis=1, concat_axis=0, tiled=True)
    return arrived.reshape(row_count * peers, columns // peers)


def to_components(points, peers):
    total_rows, columns = points.shape
    pieces = points.reshape(total_rows, 1, columns)
    arrived = lax.all_to_all(pieces, "comp", split_axis=0, concat_axis=1, tiled=True)
    return arrived.reshape(total_rows // peers, peers * columns)


def source_term(spectra, blocks, quad_index, strength):
    columns = spectra.shape[1]
    block_total = blocks.shape[0]
    group_size = math.gcd(block_total, 32)
    group_count = block_total // group_size
    spectra_grid = spectra.reshape(NF, ND, columns)
    rounded = spectra_grid.astype(jnp.bfloat16)
    block_sets = blocks.reshape(group_count, group_size, ND, ND)
    quad_sets = quad_index.reshape(4, group_count, group_size).transpose(1, 0, 2)
    weight_sets = strength.reshape(group_count, group_size)

    def accumulate(total, members):
        block_set, quad_set, weight_set = members
        first_rows = rounded[quad_set[0]]
        second = rounded[quad_set[1]]
        third_rows = spectra_grid[quad_set[2]]
        left_term = jnp.einsum(
            "jde,jep->jdp", block_set, first_rows, preferred_element_type=jnp.float32
        )
        right_term = jnp.einsum(
            "jed,jep->jdp", block_set, second, preferred_element_type=jnp.float32
        )
        product = (left_term * right_term * third_rows).astype(jnp.bfloat16)
        part_term = jnp.einsum(
            "jde,jep->jdp", block_set, product, preferred_element_type=jnp.float32
        )
        total = total.at[quad_set[3]].add(weight_set[:, None, None] * part_term)
        return (total, None)

    total, unused = lax.scan(
        accumulate, jnp.zeros((NF, ND, columns), jnp.float32), (block_sets, quad_sets, weight_sets)
    )
    return (spectra_grid + source_step * total).reshape(NF * ND, columns)


def shards(
    spectrum,
    wave_speed,
    current_east,
    current_north,
    substeps,
    neighbours,
    blocks,
    quad_index,
    strength,
):
    peers = lax.axis_size("comp")
    row_count = spectrum.shape[0]
    own_index = lax.axis_index("comp")
    first_comp = own_index * row_count
    spectra = spectrum
    spectra = upwind(
        spectra, first_comp, substeps, wave_speed, current_east, current_north, neighbours
    )
    points = source_term(to_points(spectra, peers), blocks, quad_index, strength)
    spectra = to_components(points, peers)
    return spectra


def solution(mesh):
    in_specs = (
        P("comp", ("grp", "space")),
        P(),
        P(("grp", "space")),
        P(("grp", "space")),
        P(),
        P(None, ("grp", "space")),
        P(),
        P(),
        P(),
    )
    out_specs = P("comp", ("grp", "space"))
    return jax.shard_map(shards, mesh=mesh, in_specs=in_specs, out_specs=out_specs, check_vma=False)
```

profile of v0, /device:TPU:0, one launch (start us, length us, event | category | flops | bytes accessed | tf_op | source)
XLA Modules:
  0.0 204.3 jit_solution(14900403641817318746)
XLA Ops:
  0.8 1.7 copy.31
  3.3 102.9 %while.26 = (s32[]{:T(128)}, f32[576,512]{0,1:T(8,128)S(1)}, s32[576]{0:T(1024)S(1)}, s32[4,512]{1,0:T(4,128)S(1)}, f32[512]{0:T(512)S(1)}, /*index=5*/f32[576]{...) while((s32[]{:T(128)}, f32[576,512]{0,1:T(8,128)S(1)}, ...), condition=%wide.region_2.4_spmd.clone.clone, body=%wide.region_1.3_spmd.clone.clone.sunk | while | flops 8575554 | bytes 24013112 | solution.py:79
  4.1 3.1 %collective-permute-start = (f32[576,128]{0,1:T(8,128)S(1)}, f32[576,128]{0,1:T(8,128)}, u32[]{:S(2)}, u32[]{:S(2)}) collective-permute-start(f32[576,128]{0,1:T(8,128)S(1)} %get-tuple-element.533), channel_id=1, source_target_pairs={{0,1},{1,2},{2,3},{4,5},{5,6},{6,7},{8,9},{9,10},{10,11},{12,13},{... | collective-permute-start | bytes 884744 | tf_op jit(solution)/shard_map/while/body/eval_jaxpr/ppermute | solution.py:27
  7.2 1.3 collective-permute-start.1
  9.7 2.7 %collective-permute-done.1 = f32[576,128]{0,1:T(8,128)} collective-permute-done((f32[576,128]{0,1:T(8,128)}, f32[576,128]{0,1:T(8,128)}, u32[]{:S(2)}, u32[]{:S(2)}) %collective-permute-start.1) | collective-permute-done | bytes 294944 | tf_op jit(solution)/shard_map/while/body/eval_jaxpr/ppermute | solution.py:29
  13.4 2.6 %gather_fusion.4 = f32[512,576]{1,0:T(8,128)} fusion(f32[576,768]{0,1:T(8,128)S(1)} %constant_dynamic-update-slice_fusion.8, s32[1024]{0:T(1024)S(1)} %get-tuple-element.538), kind=kCustom, calls=%fused_computation.5.clone.clone.1 | custom fusion | bytes 2361344 | tf_op jit(solution)/shard_map/while/body/eval_jaxpr/jit(_take)/gather | solution.py:68
  16.0 2.5 %gather_fusion.5 = f32[512,576]{1,0:T(8,128)} fusion(f32[576,768]{0,1:T(8,128)S(1)} %constant_dynamic-update-slice_fusion.8, s32[1024]{0:T(1024)S(1)} %get-tuple-element.541), kind=kCustom, calls=%fused_computation.4.clone.clone.1 | custom fusion | bytes 2361344 | tf_op jit(solution)/shard_map/while/body/eval_jaxpr/jit(_take)/gather | solution.py:67
  18.5 2.6 %gather_fusion.6 = f32[512,576]{1,0:T(8,128)} fusion(f32[576,768]{0,1:T(8,128)S(1)} %constant_dynamic-update-slice_fusion.8, s32[1024]{0:T(1024)S(1)} %get-tuple-element.542), kind=kCustom, calls=%fused_computation.clone.clone.1 | custom fusion | bytes 2361344 | tf_op jit(solution)/shard_map/while/body/eval_jaxpr/jit(_take)/gather | solution.py:66
  21.1 2.6 %gather_fusion.3 = f32[512,576]{1,0:T(8,128)} fusion(f32[576,768]{0,1:T(8,128)S(1)} %constant_dynamic-update-slice_fusion.8, s32[1024]{0:T(1024)S(1)} %get-tuple-element.537), kind=kCustom, calls=%fused_computation.6.clone.clone.1 | custom fusion | bytes 2361344 | tf_op jit(solution)/shard_map/while/body/eval_jaxpr/jit(_take)/gather | solution.py:69
  23.7 3.4 %fusion.68 = f32[576,512]{0,1:T(8,128)S(1)} fusion(f32[576,512]{0,1:T(8,128)S(1)} %get-tuple-element.558, f32[512,576]{1,0:T(8,128)} %gather_fusion.3, f32[512,576]{1,0:T(8,128)} %gather_fusion.4, f32[512,576]{1,0:T(8,128)} %gather_fusion.5, f32[512,576]{1,0:T(8,128)} %gather_fusion.6, f32[512]{0:T(512)S(1)} %get-tuple-element.574, ...), kind=kLoop, calls=%fused_computation.40.clone.1 | loop fusion | flops 8552448 | bytes 7091520 | tf_op jit(solution)/shard_map/while/body/eval_jaxpr/jit(_where)/select_n | solution.py:77
  27.8 8.0 %collective-permute-start = (f32[576,128]{0,1:T(8,128)S(1)}, f32[576,128]{0,1:T(8,128)}, u32[]{:S(2)}, u32[]{:S(2)}) collective-permute-start(f32[576,128]{0,1:T(8,128)S(1)} %get-tuple-element.533), channel_id=1, source_target_pairs={{0,1},{1,2},{2,3},{4,5},{5,6},{6,7},{8,9},{9,10},{10,11},{12,13},{... | collective-permute-start | bytes 884744 | tf_op jit(solution)/shard_map/while/body/eval_jaxpr/ppermute | solution.py:27
  38.3 1.3 collective-permute-done.1
  40.6 2.6 %gather_fusion.4 = f32[512,576]{1,0:T(8,128)} fusion(f32[576,768]{0,1:T(8,128)S(1)} %constant_dynamic-update-slice_fusion.8, s32[1024]{0:T(1024)S(1)} %get-tuple-element.538), kind=kCustom, calls=%fused_computation.5.clone.clone.1 | custom fusion | bytes 2361344 | tf_op jit(solution)/shard_map/while/body/eval_jaxpr/jit(_take)/gather | solution.py:68
  43.2 2.5 %gather_fusion.5 = f32[512,576]{1,0:T(8,128)} fusion(f32[576,768]{0,1:T(8,128)S(1)} %constant_dynamic-update-slice_fusion.8, s32[1024]{0:T(1024)S(1)} %get-tuple-element.541), kind=kCustom, calls=%fused_computation.4.clone.clone.1 | custom fusion | bytes 2361344 | tf_op jit(solution)/shard_map/while/body/eval_jaxpr/jit(_take)/gather | solution.py:67
  45.8 2.6 %gather_fusion.6 = f32[512,576]{1,0:T(8,128)} fusion(f32[576,768]{0,1:T(8,128)S(1)} %constant_dynamic-update-slice_fusion.8, s32[1024]{0:T(1024)S(1)} %get-tuple-element.542), kind=kCustom, calls=%fused_computation.clone.clone.1 | custom fusion | bytes 2361344 | tf_op jit(solution)/shard_map/while/body/eval_jaxpr/jit(_take)/gather | solution.py:66
  48.3 2.6 %gather_fusion.3 = f32[512,576]{1,0:T(8,128)} fusion(f32[576,768]{0,1:T(8,128)S(1)} %constant_dynamic-update-slice_fusion.8, s32[1024]{0:T(1024)S(1)} %get-tuple-element.537), kind=kCustom, calls=%fused_computation.6.clone.clone.1 | custom fusion | bytes 2361344 | tf_op jit(solution)/shard_map/while/body/eval_jaxpr/jit(_take)/gather | solution.py:69
  50.9 3.4 %fusion.68 = f32[576,512]{0,1:T(8,128)S(1)} fusion(f32[576,512]{0,1:T(8,128)S(1)} %get-tuple-element.558, f32[512,576]{1,0:T(8,128)} %gather_fusion.3, f32[512,576]{1,0:T(8,128)} %gather_fusion.4, f32[512,576]{1,0:T(8,128)} %gather_fusion.5, f32[512,576]{1,0:T(8,128)} %gather_fusion.6, f32[512]{0:T(512)S(1)} %get-tuple-element.574, ...), kind=kLoop, calls=%fused_computation.40.clone.1 | loop fusion | flops 8552448 | bytes 7091520 | tf_op jit(solution)/shard_map/while/body/eval_jaxpr/jit(_where)/select_n | solution.py:77
  55.0 6.8 %collective-permute-start = (f32[576,128]{0,1:T(8,128)S(1)}, f32[576,128]{0,1:T(8,128)}, u32[]{:S(2)}, u32[]{:S(2)}) collective-permute-start(f32[576,128]{0,1:T(8,128)S(1)} %get-tuple-element.533), channel_id=1, source_target_pairs={{0,1},{1,2},{2,3},{4,5},{5,6},{6,7},{8,9},{9,10},{10,11},{12,13},{... | collective-permute-start | bytes 884744 | tf_op jit(solution)/shard_map/while/body/eval_jaxpr/ppermute | solution.py:27
  64.3 1.3 collective-permute-done.1
  66.6 2.6 %gather_fusion.4 = f32[512,576]{1,0:T(8,128)} fusion(f32[576,768]{0,1:T(8,128)S(1)} %constant_dynamic-update-slice_fusion.8, s32[1024]{0:T(1024)S(1)} %get-tuple-element.538), kind=kCustom, calls=%fused_computation.5.clone.clone.1 | custom fusion | bytes 2361344 | tf_op jit(solution)/shard_map/while/body/eval_jaxpr/jit(_take)/gather | solution.py:68
  69.2 2.5 %gather_fusion.5 = f32[512,576]{1,0:T(8,128)} fusion(f32[576,768]{0,1:T(8,128)S(1)} %constant_dynamic-update-slice_fusion.8, s32[1024]{0:T(1024)S(1)} %get-tuple-element.541), kind=kCustom, calls=%fused_computation.4.clone.clone.1 | custom fusion | bytes 2361344 | tf_op jit(solution)/shard_map/while/body/eval_jaxpr/jit(_take)/gather | solution.py:67
  71.8 2.6 %gather_fusion.6 = f32[512,576]{1,0:T(8,128)} fusion(f32[576,768]{0,1:T(8,128)S(1)} %constant_dynamic-update-slice_fusion.8, s32[1024]{0:T(1024)S(1)} %get-tuple-element.542), kind=kCustom, calls=%fused_computation.clone.clone.1 | custom fusion | bytes 2361344 | tf_op jit(solution)/shard_map/while/body/eval_jaxpr/jit(_take)/gather | solution.py:66
  74.3 2.6 %gather_fusion.3 = f32[512,576]{1,0:T(8,128)} fusion(f32[576,768]{0,1:T(8,128)S(1)} %constant_dynamic-update-slice_fusion.8, s32[1024]{0:T(1024)S(1)} %get-tuple-element.537), kind=kCustom, calls=%fused_computation.6.clone.clone.1 | custom fusion | bytes 2361344 | tf_op jit(solution)/shard_map/while/body/eval_jaxpr/jit(_take)/gather | solution.py:69
  76.9 3.4 %fusion.68 = f32[576,512]{0,1:T(8,128)S(1)} fusion(f32[576,512]{0,1:T(8,128)S(1)} %get-tuple-element.558, f32[512,576]{1,0:T(8,128)} %gather_fusion.3, f32[512,576]{1,0:T(8,128)} %gather_fusion.4, f32[512,576]{1,0:T(8,128)} %gather_fusion.5, f32[512,576]{1,0:T(8,128)} %gather_fusion.6, f32[512]{0:T(512)S(1)} %get-tuple-element.574, ...), kind=kLoop, calls=%fused_computation.40.clone.1 | loop fusion | flops 8552448 | bytes 7091520 | tf_op jit(solution)/shard_map/while/body/eval_jaxpr/jit(_where)/select_n | solution.py:77
  81.0 6.8 %collective-permute-start = (f32[576,128]{0,1:T(8,128)S(1)}, f32[576,128]{0,1:T(8,128)}, u32[]{:S(2)}, u32[]{:S(2)}) collective-permute-start(f32[576,128]{0,1:T(8,128)S(1)} %get-tuple-element.533), channel_id=1, source_target_pairs={{0,1},{1,2},{2,3},{4,5},{5,6},{6,7},{8,9},{9,10},{10,11},{12,13},{... | collective-permute-start | bytes 884744 | tf_op jit(solution)/shard_map/while/body/eval_jaxpr/ppermute | solution.py:27
  90.3 1.3 collective-permute-done.1
  92.7 2.6 %gather_fusion.4 = f32[512,576]{1,0:T(8,128)} fusion(f32[576,768]{0,1:T(8,128)S(1)} %constant_dynamic-update-slice_fusion.8, s32[1024]{0:T(1024)S(1)} %get-tuple-element.538), kind=kCustom, calls=%fused_computation.5.clone.clone.1 | custom fusion | bytes 2361344 | tf_op jit(solution)/shard_map/while/body/eval_jaxpr/jit(_take)/gather | solution.py:68
  95.2 2.5 %gather_fusion.5 = f32[512,576]{1,0:T(8,128)} fusion(f32[576,768]{0,1:T(8,128)S(1)} %constant_dynamic-update-slice_fusion.8, s32[1024]{0:T(1024)S(1)} %get-tuple-element.541), kind=kCustom, calls=%fused_computation.4.clone.clone.1 | custom fusion | bytes 2361344 | tf_op jit(solution)/shard_map/while/body/eval_jaxpr/jit(_take)/gather | solution.py:67
  97.8 2.6 %gather_fusion.6 = f32[512,576]{1,0:T(8,128)} fusion(f32[576,768]{0,1:T(8,128)S(1)} %constant_dynamic-update-slice_fusion.8, s32[1024]{0:T(1024)S(1)} %get-tuple-element.542), kind=kCustom, calls=%fused_computation.clone.clone.1 | custom fusion | bytes 2361344 | tf_op jit(solution)/shard_map/while/body/eval_jaxpr/jit(_take)/gather | solution.py:66
  100.3 2.6 %gather_fusion.3 = f32[512,576]{1,0:T(8,128)} fusion(f32[576,768]{0,1:T(8,128)S(1)} %constant_dynamic-update-slice_fusion.8, s32[1024]{0:T(1024)S(1)} %get-tuple-element.537), kind=kCustom, calls=%fused_computation.6.clone.clone.1 | custom fusion | bytes 2361344 | tf_op jit(solution)/shard_map/while/body/eval_jaxpr/jit(_take)/gather | solution.py:69
  102.9 3.4 %fusion.68 = f32[576,512]{0,1:T(8,128)S(1)} fusion(f32[576,512]{0,1:T(8,128)S(1)} %get-tuple-element.558, f32[512,576]{1,0:T(8,128)} %gather_fusion.3, f32[512,576]{1,0:T(8,128)} %gather_fusion.4, f32[512,576]{1,0:T(8,128)} %gather_fusion.5, f32[512,576]{1,0:T(8,128)} %gather_fusion.6, f32[512]{0:T(512)S(1)} %get-tuple-element.574, ...), kind=kLoop, calls=%fused_computation.40.clone.1 | loop fusion | flops 8552448 | bytes 7091520 | tf_op jit(solution)/shard_map/while/body/eval_jaxpr/jit(_where)/select_n | solution.py:77
  106.3 1.4 copy.33
  107.7 5.0 %all-to-all-start = ((f32[576,4,128]{2,0,1:T(8,128)}), f32[576,4,128]{2,0,1:T(8,128)}, u32[]{:S(2)}, u32[]{:S(2)}) async-start(f32[576,4,128]{2,0,1:T(8,128)} %copy.33), calls=%async_computation | async-start | bytes 2359296 | tf_op jit(solution)/shard_map/all_to_all | solution.py:85
  112.9 28.8 %all-to-all-done = f32[576,4,128]{2,0,1:T(8,128)} async-done(((f32[576,4,128]{2,0,1:T(8,128)}), f32[576,4,128]{2,0,1:T(8,128)}, u32[]{:S(2)}, u32[]{:S(2)}) %all-to-all-start) | async-done | bytes 1179680 | tf_op jit(solution)/shard_map/all_to_all | solution.py:85
  141.7 1.4 convert_element_type.21
  144.2 24.0 %while.25 = (s32[]{:T(128)}, f32[36,64,128]{2,1,0:T(8,128)}, s32[2,4,32]{2,0,1:T(2,128)S(1)}, f32[2,32]{1,0:T(2,128)S(1)}, bf16[2,32,64,64]{3,2,1,0:T(8,128)(2,1...) while((s32[]{:T(128)}, f32[36,64,128]{2,1,0:T(8,128)}, ...), condition=%wide.region_5.7_spmd, body=%wide.region_3.6_spmd.sunk | while | flops 101977472 | bytes 18891668 | solution.py:125
  144.3 1.4 gather_fusion.2
  145.7 1.9 gather_fusion
  148.2 1.3 fusion.64
  149.6 1.8 convolution_multiply_fusion.3
  151.4 4.8 %scatter_fusion = f32[36,64,128]{2,1,0:T(8,128)} fusion(f32[36,64,128]{2,1,0:T(8,128)} %get-tuple-element.586, s32[32]{0:T(128)S(1)} %get-tuple-element.518, f32[32,64,128]{2,1,0:T(8,128)S(1)} %convolution_multiply_fusion.3), kind=kCustom, calls=%fused_computation.7.clone.1 | custom fusion | flops 262144 | bytes 3145856 | tf_op jit(solution)/shard_map/while/body/eval_jaxpr/scatter-add | solution.py:122
  156.3 1.4 gather_fusion.2
  157.7 1.9 gather_fusion
  160.2 1.3 fusion.64
  161.6 1.8 convolution_multiply_fusion.3
  163.5 4.8 %scatter_fusion = f32[36,64,128]{2,1,0:T(8,128)} fusion(f32[36,64,128]{2,1,0:T(8,128)} %get-tuple-element.586, s32[32]{0:T(128)S(1)} %get-tuple-element.518, f32[32,64,128]{2,1,0:T(8,128)S(1)} %convolution_multiply_fusion.3), kind=kCustom, calls=%fused_computation.7.clone.1 | custom fusion | flops 262144 | bytes 3145856 | tf_op jit(solution)/shard_map/while/body/eval_jaxpr/scatter-add | solution.py:122
  168.2 1.8 multiply_add_fusion
  170.1 32.4 %all_to_all.30 = f32[2304,1,128]{2,1,0:T(1,128)S(1)} all-to-all(f32[2304,1,128]{2,1,0:T(1,128)S(1)} %bitcast.116), channel_id=1, replica_groups=mesh['grp'=2,'comp'=4,'space'=4] {'comp'}, dimensions={0} | all-to-all | bytes 2359296 | tf_op jit(solution)/shard_map/all_to_all | solution.py:92
  (102 shorter events, 21.7 us)
Async XLA Ops:
  0.0 3.3 %copy-start.3 = (f32[512]{0:T(512)S(1)}, f32[512]{0:T(512)}, u32[]{:S(2)}) copy-start(f32[512]{0:T(512)} %param.17) | copy-start | bytes 6148
  0.0 3.3 %copy-start.4 = (f32[512]{0:T(512)S(1)}, f32[512]{0:T(512)}, u32[]{:S(2)}) copy-start(f32[512]{0:T(512)} %param.18) | copy-start | bytes 6148
  0.0 3.3 %copy-start.2 = (s32[4,512]{1,0:T(4,128)S(1)}, s32[4,512]{1,0:T(4,128)}, u32[]{:S(2)}) copy-start(s32[4,512]{1,0:T(4,128)} %param.20) | copy-start | bytes 24580
  4.1 4.5 %collective-permute-start = (f32[576,128]{0,1:T(8,128)S(1)}, f32[576,128]{0,1:T(8,128)}, u32[]{:S(2)}, u32[]{:S(2)}) collective-permute-start(f32[576,128]{0,1:T(8,128)S(1)} %get-tuple-element.533), channel_id=1, source_target_pairs={{0,1},{1,2},{2,3},{4,5},{5,6},{6,7},{8,9},{9,10},{10,11},{12,13},{... | collective-permute-start | bytes 884744 | tf_op jit(solution)/shard_map/while/body/eval_jaxpr/ppermute | solution.py:27
  7.2 5.3 %collective-permute-start.1 = (f32[576,128]{0,1:T(8,128)}, f32[576,128]{0,1:T(8,128)}, u32[]{:S(2)}, u32[]{:S(2)}) collective-permute-start(f32[576,128]{0,1:T(8,128)} %get-tuple-element.534), channel_id=1, source_target_pairs={{1,0},{2,1},{3,2},{5,4},{6,5},{7,6},{9,8},{10,9},{11,10},{13,12},{... | collective-permute-start | bytes 884744 | tf_op jit(solution)/shard_map/while/body/eval_jaxpr/ppermute | solution.py:29
  27.8 9.4 %collective-permute-start = (f32[576,128]{0,1:T(8,128)S(1)}, f32[576,128]{0,1:T(8,128)}, u32[]{:S(2)}, u32[]{:S(2)}) collective-permute-start(f32[576,128]{0,1:T(8,128)S(1)} %get-tuple-element.533), channel_id=1, source_target_pairs={{0,1},{1,2},{2,3},{4,5},{5,6},{6,7},{8,9},{9,10},{10,11},{12,13},{... | collective-permute-start | bytes 884744 | tf_op jit(solution)/shard_map/while/body/eval_jaxpr/ppermute | solution.py:27
  35.8 3.9 %collective-permute-start.1 = (f32[576,128]{0,1:T(8,128)}, f32[576,128]{0,1:T(8,128)}, u32[]{:S(2)}, u32[]{:S(2)}) collective-permute-start(f32[576,128]{0,1:T(8,128)} %get-tuple-element.534), channel_id=1, source_target_pairs={{1,0},{2,1},{3,2},{5,4},{6,5},{7,6},{9,8},{10,9},{11,10},{13,12},{... | collective-permute-start | bytes 884744 | tf_op jit(solution)/shard_map/while/body/eval_jaxpr/ppermute | solution.py:29
  55.0 8.2 %collective-permute-start = (f32[576,128]{0,1:T(8,128)S(1)}, f32[576,128]{0,1:T(8,128)}, u32[]{:S(2)}, u32[]{:S(2)}) collective-permute-start(f32[576,128]{0,1:T(8,128)S(1)} %get-tuple-element.533), channel_id=1, source_target_pairs={{0,1},{1,2},{2,3},{4,5},{5,6},{6,7},{8,9},{9,10},{10,11},{12,13},{... | collective-permute-start | bytes 884744 | tf_op jit(solution)/shard_map/while/body/eval_jaxpr/ppermute | solution.py:27
  61.8 3.9 %collective-permute-start.1 = (f32[576,128]{0,1:T(8,128)}, f32[576,128]{0,1:T(8,128)}, u32[]{:S(2)}, u32[]{:S(2)}) collective-permute-start(f32[576,128]{0,1:T(8,128)} %get-tuple-element.534), channel_id=1, source_target_pairs={{1,0},{2,1},{3,2},{5,4},{6,5},{7,6},{9,8},{10,9},{11,10},{13,12},{... | collective-permute-start | bytes 884744 | tf_op jit(solution)/shard_map/while/body/eval_jaxpr/ppermute | solution.py:29
  81.0 8.2 %collective-permute-start = (f32[576,128]{0,1:T(8,128)S(1)}, f32[576,128]{0,1:T(8,128)}, u32[]{:S(2)}, u32[]{:S(2)}) collective-permute-start(f32[576,128]{0,1:T(8,128)S(1)} %get-tuple-element.533), channel_id=1, source_target_pairs={{0,1},{1,2},{2,3},{4,5},{5,6},{6,7},{8,9},{9,10},{10,11},{12,13},{... | collective-permute-start | bytes 884744 | tf_op jit(solution)/shard_map/while/body/eval_jaxpr/ppermute | solution.py:27
  87.8 3.9 %collective-permute-start.1 = (f32[576,128]{0,1:T(8,128)}, f32[576,128]{0,1:T(8,128)}, u32[]{:S(2)}, u32[]{:S(2)}) collective-permute-start(f32[576,128]{0,1:T(8,128)} %get-tuple-element.534), channel_id=1, source_target_pairs={{1,0},{2,1},{3,2},{5,4},{6,5},{7,6},{9,8},{10,9},{11,10},{13,12},{... | collective-permute-start | bytes 884744 | tf_op jit(solution)/shard_map/while/body/eval_jaxpr/ppermute | solution.py:29
  107.7 5.0 %copy-start.5 = (s32[4,64]{1,0:T(4,128)S(1)}, s32[4,64]{1,0:T(4,128)}, u32[]{:S(2)}) copy-start(s32[4,64]{1,0:T(4,128)} %param.22) | copy-start | bytes 3076
  107.7 5.1 %copy-start.6 = (f32[64]{0:T(128)S(1)}, f32[64]{0:T(128)}, u32[]{:S(2)}) copy-start(f32[64]{0:T(128)} %param.23) | copy-start | bytes 772
  107.7 34.0 %all-to-all-start = ((f32[576,4,128]{2,0,1:T(8,128)}), f32[576,4,128]{2,0,1:T(8,128)}, u32[]{:S(2)}, u32[]{:S(2)}) async-start(f32[576,4,128]{2,0,1:T(8,128)} %copy.33), calls=%async_computation | async-start | bytes 2359296 | tf_op jit(solution)/shard_map/all_to_all | solution.py:85
  144.2 3.4 %copy-start = (bf16[36,64,128]{2,1,0:T(8,128)(2,1)}, bf16[36,64,128]{2,1,0:T(8,128)(2,1)S(1)}, u32[]{:S(2)}) copy-start(bf16[36,64,128]{2,1,0:T(8,128)(2,1)S(1)} %get-tuple-element.598) | copy-start | bytes 1769476 | tf_op jit(solution)/shard_map/while
  151.4 4.8 %copy-start.1 = (bf16[36,64,128]{2,1,0:T(8,128)(2,1)S(1)}, bf16[36,64,128]{2,1,0:T(8,128)(2,1)}, u32[]{:S(2)}) copy-start(bf16[36,64,128]{2,1,0:T(8,128)(2,1)} %copy-done) | copy-start | bytes 1769476 | tf_op jit(solution)/shard_map/while
  156.2 3.4 %copy-start = (bf16[36,64,128]{2,1,0:T(8,128)(2,1)}, bf16[36,64,128]{2,1,0:T(8,128)(2,1)S(1)}, u32[]{:S(2)}) copy-start(bf16[36,64,128]{2,1,0:T(8,128)(2,1)S(1)} %get-tuple-element.598) | copy-start | bytes 1769476 | tf_op jit(solution)/shard_map/while
  163.4 4.8 %copy-start.1 = (bf16[36,64,128]{2,1,0:T(8,128)(2,1)S(1)}, bf16[36,64,128]{2,1,0:T(8,128)(2,1)}, u32[]{:S(2)}) copy-start(bf16[36,64,128]{2,1,0:T(8,128)(2,1)} %copy-done) | copy-start | bytes 1769476 | tf_op jit(solution)/shard_map/while
where the time goes:
time: 206 us; the launch traced here: 204 us
  local copies, waits for them, and re-layouts  66.6 us (32%)
  waiting for transfers between devices  35.5 us (17%)
  starting transfers between devices  34.7 us (17%)
  blocking collectives  32.4 us (16%)
  other arithmetic  28 us (14%)
  matrix products  6.35 us (3%)
    all_to_all x1, blocking collectives, to_components(): lax.all_to_all(pieces, 'comp', split_axis=0, concat_axis=1, tiled=True)  32.4 us
    all_to_all x1, waiting for transfers between devices, to_points(): lax.all_to_all(pieces, 'comp', split_axis=1, concat_axis=0, tiled=True)  28.8 us
    ppermute x4, starting transfers between devices, padded(): lax.ppermute(tail, axis, [(i, (i + 1) % count) for i in range(ends)])  24.6 us
    select_n x4, other arithmetic, sweep_once(): return jnp.where(repeat < counts[:, None], updated, values)  13.4 us
    gather x4, local copies, waits for them, and re-layouts, sweep_once(): south_value = jnp.take(extended, neighbours[2], axis=1)  10.3 us
    gather x4, local copies, waits for them, and re-layouts, sweep_once(): north_value = jnp.take(extended, neighbours[3], axis=1)  10.2 us
    gather x4, local copies, waits for them, and re-layouts, sweep_once(): west_value = jnp.take(extended, neighbours[0], axis=1)  10.2 us
    gather x4, local copies, waits for them, and re-layouts, sweep_once(): east_value = jnp.take(extended, neighbours[1], axis=1)  10.2 us
  transfers between devices with their start and end apart: 9, of which 5 were waited for; matrix products, arithmetic and copies ran while one was open for 2% of the time, Pallas kernels for 0%

commit v1 on v0

v1 whole, which is shorter than its diff:
```python
import functools
import math

import jax
import jax.numpy as jnp
from jax import lax
from jax.experimental import pallas as pl
from jax.experimental.pallas import tpu as pltpu
from jax.sharding import PartitionSpec as P

NF = 36
ND = 64
SUB = 4
HALO = 128
DEEP = SUB * HALO
LANES = 128
TILES = DEEP // LANES

courant_scale = 0.4
courant_limit = 0.45
source_step = 0.1

VMEM = pl.BlockSpec(memory_space=pltpu.VMEM)
SMEM = pl.BlockSpec(memory_space=pltpu.SMEM)
PARAMS = pltpu.CompilerParams(vmem_limit_bytes=56 << 20)


def split(values):
    high = values.astype(jnp.bfloat16)
    return high, (values - high.astype(jnp.float32)).astype(jnp.bfloat16)


def lane_tile(t, width=1):
    return pl.ds(pl.multiple_of(t * LANES, LANES), width * LANES)


def propagate_kernel(turn, left, own, right, table, rows, *refs):
    outs, (field, parts, courant, pick) = refs[:TILES], refs[TILES:]
    count = own.shape[0]
    total = 3 * TILES
    position = lax.broadcasted_iota(jnp.int32, (2 * LANES, LANES), 0).astype(jnp.float32)

    def build(t, carry):
        cols = lane_tile(t)
        for side in range(2):
            for d in range(2):
                chosen = position == table[2 * d + side : 2 * d + side + 1, cols]
                pick[t, side, :, d * LANES : (d + 1) * LANES] = jnp.where(chosen, 1.0, 0.0).astype(jnp.bfloat16)
        return carry

    lax.fori_loop(1, total - 1, build, 0)
    for j, ref in enumerate((left, own, right)):
        cols = slice(j * DEEP, (j + 1) * DEEP)
        values = ref[...]
        field[:, cols] = values
        parts[0, :count, cols], parts[0, count:, cols] = split(values)
    east, north, inverse, substeps = (jnp.broadcast_to(rows[:, c : c + 1], (count, LANES)) for c in range(4))

    def courants(t, carry):
        cols = lane_tile(t)
        limit = table[6:7, cols]
        courant[t, 0] = jnp.clip(east + inverse * table[4:5, cols], -limit, limit)
        courant[t, 1] = jnp.clip(north + inverse * table[5:6, cols], -limit, limit)
        return carry

    lax.fori_loop(1, total - 1, courants, 0)
    for s in range(SUB):
        source, target = s % 2, 1 - s % 2

        def sweep(t, carry):
            behind = jnp.dot(parts[source, :, lane_tile(t - 1, 2)], pick[t, 0], preferred_element_type=jnp.float32)
            ahead = jnp.dot(parts[source, :, lane_tile(t, 2)], pick[t, 1], preferred_element_type=jnp.float32)
            behind = behind[:count] + behind[count:]
            ahead = ahead[:count] + ahead[count:]
            cols = lane_tile(t)
            values = field[:, cols]
            updated = values
            for d in range(2):
                speed = courant[t, d]
                half = slice(d * LANES, (d + 1) * LANES)
                upwind = jnp.where(speed > 0, behind[:, half], ahead[:, half])
                updated = updated - jnp.abs(speed) * (values - upwind)
            if s:
                updated = jnp.where(substeps > s, updated, values)
            field[:, cols] = updated
            if s < SUB - 1:
                parts[target, :count, cols], parts[target, count:, cols] = split(updated)
            return carry

        lax.fori_loop(s + 1, total - 1 - s, sweep, 0)
    for m, out in enumerate(outs):
        tile = lax.rem(turn[0] + m, TILES)
        out[...] = field[:, lane_tile(tile + TILES)]


def propagate(turn, left, own, right, table, rows):
    count = own.shape[0]
    return pl.pallas_call(
        propagate_kernel,
        out_shape=[jax.ShapeDtypeStruct((count, LANES), jnp.float32)] * TILES,
        in_specs=[SMEM] + [VMEM] * 5,
        out_specs=[VMEM] * TILES,
        scratch_shapes=[
            pltpu.VMEM((count, 3 * DEEP), jnp.float32),
            pltpu.VMEM((2, 2 * count, 3 * DEEP), jnp.bfloat16),
            pltpu.VMEM((3 * TILES, 2, count, LANES), jnp.float32),
            pltpu.VMEM((3 * TILES, 2, 2 * LANES, 2 * LANES), jnp.bfloat16),
        ],
        compiler_params=PARAMS,
        name="propagate",
    )(turn, left, own, right, table, rows)


def source_kernel(starts, step, arrived, quad, strength, turn, blocks, turned, *refs):
    ins, outs, (field, rounded, total) = refs[:arrived], refs[arrived:-3], refs[-3:]
    peers = len(outs)
    row_count = field.shape[0] // peers
    for m, group in enumerate(starts):
        base = lax.rem(turn[0] + peers - m, peers) * row_count
        for offset, ref in zip(group, ins[m * len(group) : (m + 1) * len(group)]):
            rows = pl.ds(pl.multiple_of(base + offset, 16), ref.shape[0])
            values = ref[...]
            field[rows, :] = values
            total[rows, :] = values
            rounded[rows, :] = values.astype(jnp.bfloat16)

    def rows_of(f):
        return pl.ds(pl.multiple_of(f * ND, ND), ND)

    def some(g, carry):
        products = []
        for k in range(step):
            j = g * step + k
            left = jnp.dot(blocks[j], rounded[rows_of(quad[0, j]), :], preferred_element_type=jnp.float32)
            right = jnp.dot(turned[j], rounded[rows_of(quad[1, j]), :], preferred_element_type=jnp.float32)
            products.append((left * right * field[rows_of(quad[2, j]), :]).astype(jnp.bfloat16))
        for k in range(step):
            j = g * step + k
            part = jnp.dot(blocks[j], products[k], preferred_element_type=jnp.float32)
            rows = rows_of(quad[3, j])
            total[rows, :] += (source_step * strength[j]) * part
        return carry

    lax.fori_loop(0, blocks.shape[0] // step, some, 0)
    for m, out in enumerate(outs):
        base = lax.rem(turn[0] + m, peers) * row_count
        out[...] = total[pl.ds(pl.multiple_of(base, 8), row_count), :]


def source_term(turn, pieces, starts, quad_index, strength, blocks, turned, peers):
    columns = pieces[0].shape[1]
    row_count = NF * ND // peers
    step = math.gcd(blocks.shape[0], 8)
    return pl.pallas_call(
        functools.partial(source_kernel, starts, step, len(pieces)),
        out_shape=[jax.ShapeDtypeStruct((row_count, columns), jnp.float32)] * peers,
        in_specs=[SMEM] * 3 + [VMEM] * (2 + len(pieces)),
        out_specs=[VMEM] * peers,
        scratch_shapes=[
            pltpu.VMEM((NF * ND, columns), jnp.float32),
            pltpu.VMEM((NF * ND, columns), jnp.bfloat16),
            pltpu.VMEM((NF * ND, columns), jnp.float32),
        ],
        compiler_params=PARAMS,
        name="source",
    )(quad_index, strength, turn, blocks, turned, *pieces)


def gather_kernel(turn, *refs):
    ins, out = refs[:-1], refs[-1]
    peers = len(ins)
    for m, ref in enumerate(ins):
        tile = lax.rem(turn[0] + peers - m, peers)
        out[:, lane_tile(tile)] = ref[...]


def gather_columns(turn, pieces):
    rows, columns = pieces[0].shape
    return pl.pallas_call(
        gather_kernel,
        out_shape=jax.ShapeDtypeStruct((rows, columns * len(pieces)), jnp.float32),
        in_specs=[SMEM] + [VMEM] * len(pieces),
        out_specs=VMEM,
        compiler_params=PARAMS,
        name="columns",
    )(turn, *pieces)


def from_sides(cells, width):
    count = lax.axis_size("space")
    head, tail = cells[:, :width], cells[:, cells.shape[1] - width :]
    before = lax.ppermute(tail, "space", [(i, i + 1) for i in range(count - 1)])
    after = lax.ppermute(head, "space", [(i + 1, i) for i in range(count - 1)])
    return before, after


def point_table(neighbours, current_east, current_north):
    columns = neighbours.shape[1]
    tile = jnp.arange(columns, dtype=jnp.int32) // LANES * LANES
    west, east, south, north = neighbours
    return jnp.stack(
        [
            (west - tile).astype(jnp.float32),
            (east - tile - LANES).astype(jnp.float32),
            (south - tile).astype(jnp.float32),
            (north - tile - LANES).astype(jnp.float32),
            current_east,
            current_north,
            jnp.full((columns,), courant_limit, jnp.float32),
            jnp.zeros((columns,), jnp.float32),
        ]
    )


def row_table(first_comp, row_count, substeps, wave_speed):
    angles = (jnp.arange(ND, dtype=jnp.float32) + 0.5) * (2.0 * math.pi / ND)
    inverse = courant_scale / substeps.astype(jnp.float32)
    speed = wave_speed[:, None]
    along = [(speed * turn(angles)[None, :]).reshape(NF * ND) * inverse for turn in (jnp.cos, jnp.sin)]
    table = jnp.stack(along + [inverse, substeps.astype(jnp.float32)], axis=1)
    return lax.dynamic_slice_in_dim(table, first_comp, row_count)


def cuts_of(row_count):
    if row_count % 192:
        return [(0, row_count)]
    first = 192
    return [(0, first), (first, row_count)] if row_count > first else [(0, row_count)]


def shards(
    spectrum,
    wave_speed,
    current_east,
    current_north,
    substeps,
    neighbours,
    blocks,
    quad_index,
    strength,
):
    peers = lax.axis_size("comp")
    row_count, columns = spectrum.shape
    own_index = lax.axis_index("comp").astype(jnp.int32)
    turn = own_index.reshape(1)
    table = point_table(neighbours, current_east, current_north)
    table = jnp.concatenate([from_sides(table, DEEP)[0], table, from_sides(table, DEEP)[1]], axis=1)
    rows = row_table(own_index * row_count, row_count, substeps, wave_speed)
    turned = blocks.swapaxes(1, 2)
    if columns == DEEP and peers == TILES:
        cuts = cuts_of(row_count)
        sent = [[] for _ in range(peers)]
        for low, high in cuts:
            chunk = spectrum[low:high]
            before, after = from_sides(chunk, DEEP)
            moved = propagate(turn, before, chunk, after, table, rows[low:high])
            for m in range(peers):
                piece = moved[m]
                if m:
                    piece = lax.ppermute(piece, "comp", [(i, (i + m) % peers) for i in range(peers)])
                sent[m].append(piece)
        pieces = [piece for group in sent for piece in group]
        starts = [[low for low, high in cuts]] * peers
        results = source_term(turn, pieces, starts, quad_index, strength, blocks, turned, peers)
        back = [
            lax.ppermute(piece, "comp", [(i, (i + m) % peers) for i in range(peers)]) if m else piece
            for m, piece in enumerate(results)
        ]
        return gather_columns(turn, back)
    still = jnp.zeros((1,), jnp.int32)
    extra = -row_count % 16
    chunk = jnp.pad(spectrum, ((0, extra), (0, 0)))
    rows = jnp.pad(rows, ((0, extra), (0, 0)))
    before, after = from_sides(chunk, DEEP)
    wide = jnp.concatenate([before, chunk, after], axis=1)
    tiles = []
    for first in range(0, columns, DEEP):
        near = [wide[:, first + j * DEEP : first + (j + 1) * DEEP] for j in range(3)]
        tiles += propagate(still, *near, table[:, first : first + 3 * DEEP], rows)
    grid = jnp.concatenate(tiles, axis=1)[:row_count].reshape(row_count, peers, columns // peers).swapaxes(0, 1)
    arrived = lax.all_to_all(grid, "comp", 0, 0, tiled=True)
    arrived = arrived.reshape(NF * ND, columns // peers)
    (results,) = source_term(still, [arrived], [[0]], quad_index, strength, blocks, turned, 1)
    results = results.reshape(peers, row_count, columns // peers)
    back = lax.all_to_all(results, "comp", 0, 0, tiled=True)
    return back.swapaxes(0, 1).reshape(row_count, columns)


def solution(mesh):
    in_specs = (
        P("comp", ("grp", "space")),
        P(),
        P(("grp", "space")),
        P(("grp", "space")),
        P(),
        P(None, ("grp", "space")),
        P(),
        P(),
        P(),
    )
    out_specs = P("comp", ("grp", "space"))
    return jax.shard_map(shards, mesh=mesh, in_specs=in_specs, out_specs=out_specs, check_vma=False)
```

time: 206 us -> 121 us (0.59)
  the two profiles are of different devices: /device:TPU:0 before, /device:TPU:13 now
where the time goes in v1:
time: 121 us; the launch traced here: 119 us
  waiting for transfers between devices  45 us (37%)
  Pallas kernels  35.1 us (29%)
  starting transfers between devices  28.1 us (23%)
  local copies, waits for them, and re-layouts  9.5 us (8%)
    ppermute x9, waiting for transfers between devices, shards(): lax.ppermute(piece, 'comp', [(i, (i + m) % peers) for i in range(peers)])  42.3 us
    pallas_call x2, Pallas kernels, propagate(): pl.pallas_call(propagate_kernel, out_shape=[jax.ShapeDtypeStruct((count,...  26.8 us
    ppermute x9, starting transfers between devices, shards(): lax.ppermute(piece, 'comp', [(i, (i + m) % peers) for i in range(peers)])  11.4 us
    ppermute x3, starting transfers between devices, from_sides(): before = lax.ppermute(tail, 'space', [(i, i + 1) for i in range(count - 1)])  11 us
    unnamed x43, local copies, waits for them, and re-layouts  6.94 us
    pallas_call x1, Pallas kernels, source_term(): pl.pallas_call(functools.partial(source_kernel, starts, step, len(pieces)...  5.92 us
    ppermute x3, starting transfers between devices, from_sides(): after = lax.ppermute(head, 'space', [(i + 1, i) for i in range(count - 1)])  5.75 us
  transfers between devices with their start and end apart: 15, of which 7 were waited for; matrix products, arithmetic and copies ran while one was open for 4% of the time, Pallas kernels for 23%

profile of v1, /device:TPU:13, one launch (start us, length us, event | category | flops | bytes accessed | tf_op | source)
XLA Modules:
  0.0 118.9 jit_solution(1421451437272469646)
XLA Ops:
  0.0 1.2 %slice.14.own = f32[384,512]{1,0:T(8,128)S(1)} slice(f32[576,512]{1,0:T(8,128)} %param.9), slice={[192:576], [0:512]} | slice | bytes 1572864 | tf_op jit(solution)/shard_map/slice | solution.py:254
  1.3 3.7 %collective-permute-start.4 = (f32[384,512]{1,0:T(8,128)S(1)}, f32[384,512]{1,0:T(8,128)S(1)}, u32[]{:S(2)}, u32[]{:S(2)}) collective-permute-start(f32[384,512]{1,0:T(8,128)S(1)} %slice.14.own), channel_id=1, source_target_pairs={{0,1},{1,2},{2,3},{4,5},{5,6},{6,7},{8,9},{9,10},{10,11},{12,13},{... | collective-permute-start | bytes 2359304 | tf_op jit(solution)/shard_map/ppermute | solution.py:192
  5.0 1.9 %collective-permute-start.5 = (f32[384,512]{1,0:T(8,128)S(1)}, f32[384,512]{1,0:T(8,128)S(1)}, u32[]{:S(2)}, u32[]{:S(2)}) collective-permute-start(f32[384,512]{1,0:T(8,128)S(1)} %slice.14.own), channel_id=1, source_target_pairs={{1,0},{2,1},{3,2},{5,4},{6,5},{7,6},{9,8},{10,9},{11,10},{13,12},{... | collective-permute-start | bytes 2359304 | tf_op jit(solution)/shard_map/ppermute | solution.py:193
  6.9 1.0 slice.12.own
  7.9 3.6 %collective-permute-start = (f32[192,512]{1,0:T(8,128)S(1)}, f32[192,512]{1,0:T(8,128)S(1)}, u32[]{:S(2)}, u32[]{:S(2)}) collective-permute-start(f32[192,512]{1,0:T(8,128)S(1)} %slice.12.own), channel_id=1, source_target_pairs={{0,1},{1,2},{2,3},{4,5},{5,6},{6,7},{8,9},{9,10},{10,11},{12,13},{... | collective-permute-start | bytes 1179656 | tf_op jit(solution)/shard_map/ppermute | solution.py:192
  11.6 1.9 %collective-permute-start.1 = (f32[192,512]{1,0:T(8,128)S(1)}, f32[192,512]{1,0:T(8,128)}, u32[]{:S(2)}, u32[]{:S(2)}) collective-permute-start(f32[192,512]{1,0:T(8,128)S(1)} %slice.12.own), channel_id=1, source_target_pairs={{1,0},{2,1},{3,2},{5,4},{6,5},{7,6},{9,8},{10,9},{11,10},{13,12},{... | collective-permute-start | bytes 1179656 | tf_op jit(solution)/shard_map/ppermute | solution.py:193
  13.6 3.6 %collective-permute-start.2 = (f32[8,512]{1,0:T(8,128)S(1)}, f32[8,512]{1,0:T(8,128)S(1)}, u32[]{:S(2)}, u32[]{:S(2)}) collective-permute-start(f32[8,512]{1,0:T(8,128)S(1)} %stack.30), channel_id=1, source_target_pairs={{0,1},{1,2},{2,3},{4,5},{5,6},{6,7},{8,9},{9,10},{10,11},{12,13},{... | collective-permute-start | bytes 49160 | tf_op jit(solution)/shard_map/ppermute | solution.py:192
  17.3 0.1 broadcast_multiply_fusion
  17.4 0.1 mul.81
  17.5 0.1 mul.85
  17.7 0.6 collective-permute-done.2
  18.3 1.9 %collective-permute-start.3 = (f32[8,512]{1,0:T(8,128)S(1)}, f32[8,512]{1,0:T(8,128)S(1)}, u32[]{:S(2)}, u32[]{:S(2)}) collective-permute-start(f32[8,512]{1,0:T(8,128)S(1)} %stack.30), channel_id=1, source_target_pairs={{1,0},{2,1},{3,2},{5,4},{6,5},{7,6},{9,8},{10,9},{11,10},{13,12},{... | collective-permute-start | bytes 49160 | tf_op jit(solution)/shard_map/ppermute | solution.py:193
  20.2 0.1 fusion.2
  20.3 0.1 slice.17
  20.4 0.8 copy.20.rows
  21.2 0.8 copy.19.rows
  22.0 2.1 %collective-permute-done.3 = f32[8,512]{1,0:T(8,128)S(1)} collective-permute-done((f32[8,512]{1,0:T(8,128)S(1)}, f32[8,512]{1,0:T(8,128)S(1)}, u32[]{:S(2)}, u32[]{:S(2)}) %collective-permute-start.3) | collective-permute-done | bytes 16416 | tf_op jit(solution)/shard_map/ppermute | solution.py:193
  24.1 0.6 pad_maximum_fusion.table
  24.7 0.7 copy-done.5
  25.4 11.2 %propagate.2 = (f32[192,128]{1,0:T(8,128)}, f32[192,128]{1,0:T(8,128)}, f32[192,128]{1,0:T(8,128)}, f32[192,128]{1,0:T(8,128)}) custom-call(s32[1]{0:T(128)} %bitcast.turn, f32[192,512]{1,0:T(8,128)} %copy-done.5, f32[192,512]{1,0:T(8,128)} %copy-done.2, f32[192,512]{1,0:T(8,128)} %collective-permute-done.1.right, f32[8,1536]{1,0:T(8,128)} %pad_maximum_fusion.table, ...), custom_call_target="tpu_custom_call" | custom-call | tf_op jit(solution)/shard_map/propagate/pallas_call | solution.py:98
  36.7 0.2 collective-permute-start.10
  36.9 0.0 collective-permute-done.4.left
  36.9 0.0 collective-permute-done.5.right
  36.9 0.9 copy-done.3
  37.8 0.9 copy-done.4
  38.7 15.6 %propagate.3 = (f32[384,128]{1,0:T(8,128)}, f32[384,128]{1,0:T(8,128)}, f32[384,128]{1,0:T(8,128)}, f32[384,128]{1,0:T(8,128)}) custom-call(s32[1]{0:T(128)} %bitcast.turn, f32[384,512]{1,0:T(8,128)} %copy-done.3, f32[384,512]{1,0:T(8,128)} %copy-done.1, f32[384,512]{1,0:T(8,128)} %copy-done.4, f32[8,1536]{1,0:T(8,128)} %pad_maximum_fusion.table, ...), custom_call_target="tpu_custom_call" | custom-call | tf_op jit(solution)/shard_map/propagate/pallas_call | solution.py:98
  54.2 3.3 %collective-permute-start.11 = (f32[384,128]{1,0:T(8,128)}, f32[384,128]{1,0:T(8,128)S(1)}, u32[]{:S(2)}, u32[]{:S(2)}) collective-permute-start(f32[384,128]{1,0:T(8,128)} %get-tuple-element.24), channel_id=1, source_target_pairs={{0,12},{4,0},{8,4},{12,8},{1,13},{5,1},{9,5},{13,9},{2,14},{6,2},{... | collective-permute-start | bytes 589832 | tf_op jit(solution)/shard_map/ppermute | solution.py:260
  57.5 0.0 collective-permute-start.7
  57.5 2.3 %collective-permute-start.9 = (f32[384,128]{1,0:T(8,128)}, f32[384,128]{1,0:T(8,128)S(1)}, u32[]{:S(2)}, u32[]{:S(2)}) collective-permute-start(f32[384,128]{1,0:T(8,128)} %get-tuple-element.22), channel_id=1, source_target_pairs={{0,8},{4,12},{8,0},{12,4},{1,9},{5,13},{9,1},{13,5},{2,10},{6,14},... | collective-permute-start | bytes 589832 | tf_op jit(solution)/shard_map/ppermute | solution.py:260
  59.8 0.4 collective-permute-start.6
  60.2 0.0 collective-permute-done.10.refs_6_
  60.2 0.9 collective-permute-start.8
  61.1 1.3 %copy.16 = bf16[64,64,64]{1,2,0:T(8,128)(2,1)} copy(bf16[64,64,64]{2,1,0:T(8,128)(2,1)S(1)} %copy-done) | data formatting | bytes 1048576 | tf_op args[6]
  62.4 15.0 %collective-permute-done.6.refs_2_ = f32[192,128]{1,0:T(8,128)S(1)} collective-permute-done((f32[192,128]{1,0:T(8,128)}, f32[192,128]{1,0:T(8,128)S(1)}, u32[]{:S(2)}, u32[]{:S(2)}) %collective-permute-start.6) | collective-permute-done | bytes 98336 | tf_op jit(solution)/shard_map/ppermute | solution.py:260
  77.4 2.0 %collective-permute-done.8.refs_4_ = f32[192,128]{1,0:T(8,128)S(1)} collective-permute-done((f32[192,128]{1,0:T(8,128)}, f32[192,128]{1,0:T(8,128)S(1)}, u32[]{:S(2)}, u32[]{:S(2)}) %collective-permute-start.8) | collective-permute-done | bytes 98336 | tf_op jit(solution)/shard_map/ppermute | solution.py:260
  79.5 0.0 collective-permute-done.9.refs_5_
  79.5 0.6 copy-done.14
  80.1 0.1 copy-done.9
  80.2 0.1 copy-done.10
  80.3 0.0 copy-done.11
  80.3 5.9 %source.1 = (f32[576,128]{1,0:T(8,128)}, f32[576,128]{1,0:T(8,128)}, f32[576,128]{1,0:T(8,128)}, f32[576,128]{1,0:T(8,128)}) custom-call(s32[4,64]{1,0:T(4,128)} %quad.1, f32[64]{0:T(128)} %strength.1, s32[1]{0:T(128)} %bitcast.turn, bf16[64,64,64]{2,1,0:T(8,128)(2,1)} %blocks.1, bf16[64,64,64]{2,1,0:T(8,128)(2,1)} %bitcast.4, ...), custom_call_target="tpu_custom_call" | custom-call | tf_op jit(solution)/shard_map/source/pallas_call | solution.py:154
  86.2 2.9 %collective-permute-start.13 = (f32[576,128]{1,0:T(8,128)}, f32[576,128]{1,0:T(8,128)S(1)}, u32[]{:S(2)}, u32[]{:S(2)}) collective-permute-start(f32[576,128]{1,0:T(8,128)} %get-tuple-element.27), channel_id=1, source_target_pairs={{0,8},{4,12},{8,0},{12,4},{1,9},{5,13},{9,1},{13,5},{2,10},{6,14},... | collective-permute-start | bytes 884744 | tf_op jit(solution)/shard_map/ppermute | solution.py:266
  89.2 1.4 %collective-permute-start.14 = (f32[576,128]{1,0:T(8,128)}, f32[576,128]{1,0:T(8,128)S(1)}, u32[]{:S(2)}, u32[]{:S(2)}) collective-permute-start(f32[576,128]{1,0:T(8,128)} %get-tuple-element.28), channel_id=1, source_target_pairs={{0,12},{4,0},{8,4},{12,8},{1,13},{5,1},{9,5},{13,9},{2,14},{6,2},{... | collective-permute-start | bytes 884744 | tf_op jit(solution)/shard_map/ppermute | solution.py:266
  90.6 4.2 %collective-permute-done.12.refs_1_ = f32[576,128]{1,0:T(8,128)S(1)} collective-permute-done((f32[576,128]{1,0:T(8,128)}, f32[576,128]{1,0:T(8,128)S(1)}, u32[]{:S(2)}, u32[]{:S(2)}) %collective-permute-start.12) | collective-permute-done | bytes 294944 | tf_op jit(solution)/shard_map/ppermute | solution.py:266
  94.8 16.8 %collective-permute-done.13.refs_2_ = f32[576,128]{1,0:T(8,128)S(1)} collective-permute-done((f32[576,128]{1,0:T(8,128)}, f32[576,128]{1,0:T(8,128)S(1)}, u32[]{:S(2)}, u32[]{:S(2)}) %collective-permute-start.13) | collective-permute-done | bytes 294944 | tf_op jit(solution)/shard_map/ppermute | solution.py:266
  111.6 4.2 %collective-permute-done.14.refs_3_ = f32[576,128]{1,0:T(8,128)S(1)} collective-permute-done((f32[576,128]{1,0:T(8,128)}, f32[576,128]{1,0:T(8,128)S(1)}, u32[]{:S(2)}, u32[]{:S(2)}) %collective-permute-start.14) | collective-permute-done | bytes 294944 | tf_op jit(solution)/shard_map/ppermute | solution.py:266
  115.8 0.7 copy-done.8
  116.5 2.4 %columns.1 = f32[576,512]{1,0:T(8,128)} custom-call(s32[1]{0:T(128)} %bitcast.turn, f32[576,128]{1,0:T(8,128)} %get-tuple-element.25.refs_0_, f32[576,128]{1,0:T(8,128)} %copy-done.6, f32[576,128]{1,0:T(8,128)} %copy-done.7, f32[576,128]{1,0:T(8,128)} %copy-done.8), custom_call_target="tpu_custom_call" | custom-call | tf_op jit(solution)/shard_map/columns/pallas_call | solution.py:179
  (49 shorter events, 0.2 us)
Async XLA Ops:
  0.0 13.5 %copy-start.16 = (s32[4,512]{1,0:T(4,128)S(1)}, s32[4,512]{1,0:T(4,128)}, u32[]{:S(2)}) copy-start(s32[4,512]{1,0:T(4,128)} %param.14) | copy-start | bytes 24580
  0.0 13.6 %copy-start.17 = (f32[512]{0:T(512)S(1)}, f32[512]{0:T(512)}, u32[]{:S(2)}) copy-start(f32[512]{0:T(512)} %param.11) | copy-start | bytes 6148
  0.0 13.6 %copy-start.18 = (f32[512]{0:T(512)S(1)}, f32[512]{0:T(512)}, u32[]{:S(2)}) copy-start(f32[512]{0:T(512)} %param.12) | copy-start | bytes 6148
  0.0 17.3 %copy-start.19 = (f32[36]{0:T(128)S(1)}, f32[36]{0:T(128)}, u32[]{:S(2)}) copy-start(f32[36]{0:T(128)} %param.10) | copy-start | bytes 436
  0.0 17.5 %copy-start.15 = (s32[2304]{0:T(1024)S(1)}, s32[2304]{0:T(1024)}, u32[]{:S(2)}) copy-start(s32[2304]{0:T(1024)} %param.13) | copy-start | bytes 27652
  1.3 35.4 %copy-start.1 = (f32[384,512]{1,0:T(8,128)}, f32[384,512]{1,0:T(8,128)S(1)}, u32[]{:S(2)}) copy-start(f32[384,512]{1,0:T(8,128)S(1)} %slice.14.own) | copy-start | bytes 2359300
  1.3 35.6 %collective-permute-start.4 = (f32[384,512]{1,0:T(8,128)S(1)}, f32[384,512]{1,0:T(8,128)S(1)}, u32[]{:S(2)}, u32[]{:S(2)}) collective-permute-start(f32[384,512]{1,0:T(8,128)S(1)} %slice.14.own), channel_id=1, source_target_pairs={{0,1},{1,2},{2,3},{4,5},{5,6},{6,7},{8,9},{9,10},{10,11},{12,13},{... | collective-permute-start | bytes 2359304 | tf_op jit(solution)/shard_map/ppermute | solution.py:192
  5.0 31.9 %collective-permute-start.5 = (f32[384,512]{1,0:T(8,128)S(1)}, f32[384,512]{1,0:T(8,128)S(1)}, u32[]{:S(2)}, u32[]{:S(2)}) collective-permute-start(f32[384,512]{1,0:T(8,128)S(1)} %slice.14.own), channel_id=1, source_target_pairs={{1,0},{2,1},{3,2},{5,4},{6,5},{7,6},{9,8},{10,9},{11,10},{13,12},{... | collective-permute-start | bytes 2359304 | tf_op jit(solution)/shard_map/ppermute | solution.py:193
  7.9 16.8 %copy-start.2 = (f32[192,512]{1,0:T(8,128)}, f32[192,512]{1,0:T(8,128)S(1)}, u32[]{:S(2)}) copy-start(f32[192,512]{1,0:T(8,128)S(1)} %slice.12.own) | copy-start | bytes 1179652
  7.9 16.7 %collective-permute-start = (f32[192,512]{1,0:T(8,128)S(1)}, f32[192,512]{1,0:T(8,128)S(1)}, u32[]{:S(2)}, u32[]{:S(2)}) collective-permute-start(f32[192,512]{1,0:T(8,128)S(1)} %slice.12.own), channel_id=1, source_target_pairs={{0,1},{1,2},{2,3},{4,5},{5,6},{6,7},{8,9},{9,10},{10,11},{12,13},{... | collective-permute-start | bytes 1179656 | tf_op jit(solution)/shard_map/ppermute | solution.py:192
  11.6 13.1 %collective-permute-start.1 = (f32[192,512]{1,0:T(8,128)S(1)}, f32[192,512]{1,0:T(8,128)}, u32[]{:S(2)}, u32[]{:S(2)}) collective-permute-start(f32[192,512]{1,0:T(8,128)S(1)} %slice.12.own), channel_id=1, source_target_pairs={{1,0},{2,1},{3,2},{5,4},{6,5},{7,6},{9,8},{10,9},{11,10},{13,12},{... | collective-permute-start | bytes 1179656 | tf_op jit(solution)/shard_map/ppermute | solution.py:193
  13.6 4.6 %collective-permute-start.2 = (f32[8,512]{1,0:T(8,128)S(1)}, f32[8,512]{1,0:T(8,128)S(1)}, u32[]{:S(2)}, u32[]{:S(2)}) collective-permute-start(f32[8,512]{1,0:T(8,128)S(1)} %stack.30), channel_id=1, source_target_pairs={{0,1},{1,2},{2,3},{4,5},{5,6},{6,7},{8,9},{9,10},{10,11},{12,13},{... | collective-permute-start | bytes 49160 | tf_op jit(solution)/shard_map/ppermute | solution.py:192
  18.3 5.8 %collective-permute-start.3 = (f32[8,512]{1,0:T(8,128)S(1)}, f32[8,512]{1,0:T(8,128)S(1)}, u32[]{:S(2)}, u32[]{:S(2)}) collective-permute-start(f32[8,512]{1,0:T(8,128)S(1)} %stack.30), channel_id=1, source_target_pairs={{1,0},{2,1},{3,2},{5,4},{6,5},{7,6},{9,8},{10,9},{11,10},{13,12},{... | collective-permute-start | bytes 49160 | tf_op jit(solution)/shard_map/ppermute | solution.py:193
  24.7 0.7 copy-start.5
  36.7 24.4 %copy-start = (bf16[64,64,64]{2,1,0:T(8,128)(2,1)S(1)}, bf16[64,64,64]{2,1,0:T(8,128)(2,1)}, u32[]{:S(2)}) copy-start(bf16[64,64,64]{2,1,0:T(8,128)(2,1)} %blocks.1) | copy-start | bytes 1572868
  36.7 23.5 %collective-permute-start.10 = (f32[192,128]{1,0:T(8,128)}, f32[192,128]{1,0:T(8,128)S(1)}, u32[]{:S(2)}, u32[]{:S(2)}) collective-permute-start(f32[192,128]{1,0:T(8,128)} %get-tuple-element.23), channel_id=1, source_target_pairs={{0,12},{4,0},{8,4},{12,8},{1,13},{5,1},{9,5},{13,9},{2,14},{6,2},{... | collective-permute-start | bytes 294920 | tf_op jit(solution)/shard_map/ppermute | solution.py:260
  36.9 0.9 copy-start.3
  37.8 0.9 copy-start.4
  54.2 25.2 %collective-permute-start.11 = (f32[384,128]{1,0:T(8,128)}, f32[384,128]{1,0:T(8,128)S(1)}, u32[]{:S(2)}, u32[]{:S(2)}) collective-permute-start(f32[384,128]{1,0:T(8,128)} %get-tuple-element.24), channel_id=1, source_target_pairs={{0,12},{4,0},{8,4},{12,8},{1,13},{5,1},{9,5},{13,9},{2,14},{6,2},{... | collective-permute-start | bytes 589832 | tf_op jit(solution)/shard_map/ppermute | solution.py:260
  57.5 21.9 %collective-permute-start.7 = (f32[384,128]{1,0:T(8,128)}, f32[384,128]{1,0:T(8,128)S(1)}, u32[]{:S(2)}, u32[]{:S(2)}) collective-permute-start(f32[384,128]{1,0:T(8,128)} %get-tuple-element.20), channel_id=1, source_target_pairs={{0,4},{4,8},{8,12},{12,0},{1,5},{5,9},{9,13},{13,1},{2,6},{6,10},{... | collective-permute-start | bytes 589832 | tf_op jit(solution)/shard_map/ppermute | solution.py:260
  57.5 22.0 %collective-permute-start.9 = (f32[384,128]{1,0:T(8,128)}, f32[384,128]{1,0:T(8,128)S(1)}, u32[]{:S(2)}, u32[]{:S(2)}) collective-permute-start(f32[384,128]{1,0:T(8,128)} %get-tuple-element.22), channel_id=1, source_target_pairs={{0,8},{4,12},{8,0},{12,4},{1,9},{5,13},{9,1},{13,5},{2,10},{6,14},... | collective-permute-start | bytes 589832 | tf_op jit(solution)/shard_map/ppermute | solution.py:260
  59.8 17.6 %collective-permute-start.6 = (f32[192,128]{1,0:T(8,128)}, f32[192,128]{1,0:T(8,128)S(1)}, u32[]{:S(2)}, u32[]{:S(2)}) collective-permute-start(f32[192,128]{1,0:T(8,128)} %get-tuple-element.19), channel_id=1, source_target_pairs={{0,4},{4,8},{8,12},{12,0},{1,5},{5,9},{9,13},{13,1},{2,6},{6,10},{... | collective-permute-start | bytes 294920 | tf_op jit(solution)/shard_map/ppermute | solution.py:260
  60.2 19.3 %copy-start.12 = (f32[192,128]{1,0:T(8,128)}, f32[192,128]{1,0:T(8,128)S(1)}, u32[]{:S(2)}) copy-start(f32[192,128]{1,0:T(8,128)S(1)} %collective-permute-done.10.refs_6_) | copy-start | bytes 294916
  60.2 19.3 %collective-permute-start.8 = (f32[192,128]{1,0:T(8,128)}, f32[192,128]{1,0:T(8,128)S(1)}, u32[]{:S(2)}, u32[]{:S(2)}) collective-permute-start(f32[192,128]{1,0:T(8,128)} %get-tuple-element.21), channel_id=1, source_target_pairs={{0,8},{4,12},{8,0},{12,4},{1,9},{5,13},{9,1},{13,5},{2,10},{6,14},... | collective-permute-start | bytes 294920 | tf_op jit(solution)/shard_map/ppermute | solution.py:260
  77.4 2.1 %copy-start.13 = (f32[192,128]{1,0:T(8,128)}, f32[192,128]{1,0:T(8,128)S(1)}, u32[]{:S(2)}) copy-start(f32[192,128]{1,0:T(8,128)S(1)} %collective-permute-done.6.refs_2_) | copy-start | bytes 294916
  79.5 0.6 copy-start.14
  79.5 0.7 copy-start.9
  79.5 0.8 copy-start.10
  79.5 0.8 copy-start.11
  86.2 8.5 %collective-permute-start.12 = (f32[576,128]{1,0:T(8,128)}, f32[576,128]{1,0:T(8,128)S(1)}, u32[]{:S(2)}, u32[]{:S(2)}) collective-permute-start(f32[576,128]{1,0:T(8,128)} %get-tuple-element.26), channel_id=1, source_target_pairs={{0,4},{4,8},{8,12},{12,0},{1,5},{5,9},{9,13},{13,1},{2,6},{6,10},{... | collective-permute-start | bytes 884744 | tf_op jit(solution)/shard_map/ppermute | solution.py:266
  86.2 25.4 %collective-permute-start.13 = (f32[576,128]{1,0:T(8,128)}, f32[576,128]{1,0:T(8,128)S(1)}, u32[]{:S(2)}, u32[]{:S(2)}) collective-permute-start(f32[576,128]{1,0:T(8,128)} %get-tuple-element.27), channel_id=1, source_target_pairs={{0,8},{4,12},{8,0},{12,4},{1,9},{5,13},{9,1},{13,5},{2,10},{6,14},... | collective-permute-start | bytes 884744 | tf_op jit(solution)/shard_map/ppermute | solution.py:266
  89.2 26.6 %collective-permute-start.14 = (f32[576,128]{1,0:T(8,128)}, f32[576,128]{1,0:T(8,128)S(1)}, u32[]{:S(2)}, u32[]{:S(2)}) collective-permute-start(f32[576,128]{1,0:T(8,128)} %get-tuple-element.28), channel_id=1, source_target_pairs={{0,12},{4,0},{8,4},{12,8},{1,13},{5,1},{9,5},{13,9},{2,14},{6,2},{... | collective-permute-start | bytes 884744 | tf_op jit(solution)/shard_map/ppermute | solution.py:266
  94.8 21.0 %copy-start.6 = (f32[576,128]{1,0:T(8,128)}, f32[576,128]{1,0:T(8,128)S(1)}, u32[]{:S(2)}) copy-start(f32[576,128]{1,0:T(8,128)S(1)} %collective-permute-done.12.refs_1_) | copy-start | bytes 884740
  111.6 4.2 %copy-start.7 = (f32[576,128]{1,0:T(8,128)}, f32[576,128]{1,0:T(8,128)S(1)}, u32[]{:S(2)}) copy-start(f32[576,128]{1,0:T(8,128)S(1)} %collective-permute-done.13.refs_2_) | copy-start | bytes 884740
  115.8 0.7 copy-start.8

commit v2 on v1

v2 whole, which is shorter than its diff:
```python
import functools
import math

import jax
import jax.numpy as jnp
from jax import lax
from jax.experimental import pallas as pl
from jax.experimental.pallas import tpu as pltpu
from jax.sharding import PartitionSpec as P

NF = 36
ND = 64
SUB = 4
HALO = 128
DEEP = SUB * HALO
LANES = 128
TILES = DEEP // LANES

courant_scale = 0.4
courant_limit = 0.45
source_step = 0.1

VMEM = pl.BlockSpec(memory_space=pltpu.VMEM)
SMEM = pl.BlockSpec(memory_space=pltpu.SMEM)
ANY = pl.BlockSpec(memory_space=pl.ANY)
PARAMS = pltpu.CompilerParams(vmem_limit_bytes=56 << 20)


def split(values):
    high = values.astype(jnp.bfloat16)
    return high, (values - high.astype(jnp.float32)).astype(jnp.bfloat16)


def lane_tile(t, width=1):
    if isinstance(t, int):
        return slice(t * LANES, (t + width) * LANES)
    return pl.ds(pl.multiple_of(t * LANES, LANES), width * LANES)


def copy_all(pairs, flags):
    copies = [pltpu.make_async_copy(source, target, flags.at[i]) for i, (source, target) in enumerate(pairs)]
    for copy in copies:
        copy.start()
    return copies


def propagate_kernel(first, low, turn, rows, *refs):
    tables, sides, outs = refs[:3], refs[3:6], refs[6 : 6 + TILES]
    table, field, parts_a, parts_b, along_x, along_y, behind_pick, ahead_pick, flags = refs[6 + TILES :]
    parts = (parts_a, parts_b)
    count = field.shape[0]
    total = 3 * TILES
    pairs = [(ref.at[0:8, :], table.at[:, j * DEEP : (j + 1) * DEEP]) for j, ref in enumerate(tables)]
    pairs += [(ref.at[first : first + count, :], field.at[:, j * DEEP : (j + 1) * DEEP]) for j, ref in enumerate(sides)]
    copies = copy_all(pairs, flags)
    columns = jnp.transpose(rows[...])[low : low + count]
    east, north, inverse, substeps = (jnp.broadcast_to(columns[:, c : c + 1], (count, LANES)) for c in range(4))
    position = lax.broadcasted_iota(jnp.int32, (2 * LANES, LANES), 0).astype(jnp.float32)
    for copy in copies:
        copy.wait()
    parts_a[:count], parts_a[count:] = split(field[...])
    for s in range(SUB):
        source, target = parts[s % 2], parts[1 - s % 2]
        for t in range(s + 1, total - 1 - s):
            cols = lane_tile(t)
            if s == 0:
                for pick, side in ((behind_pick, 0), (ahead_pick, 1)):
                    for d in range(2):
                        chosen = position == table[2 * d + side : 2 * d + side + 1, cols]
                        pick[t, :, lane_tile(d)] = jnp.where(chosen, 1.0, 0.0).astype(jnp.bfloat16)
                limit = table[6:7, cols]
                along_x[t] = jnp.clip(east + inverse * table[4:5, cols], -limit, limit)
                along_y[t] = jnp.clip(north + inverse * table[5:6, cols], -limit, limit)
            behind = jnp.dot(source[:, lane_tile(t - 1, 2)], behind_pick[t], preferred_element_type=jnp.float32)
            ahead = jnp.dot(source[:, lane_tile(t, 2)], ahead_pick[t], preferred_element_type=jnp.float32)
            behind = behind[:count] + behind[count:]
            ahead = ahead[:count] + ahead[count:]
            values = field[:, cols]
            updated = values
            for d, along in enumerate((along_x, along_y)):
                speed = along[t]
                upwind = jnp.where(speed > 0, behind[:, lane_tile(d)], ahead[:, lane_tile(d)])
                updated = updated - jnp.abs(speed) * (values - upwind)
            if s:
                updated = jnp.where(substeps > s, updated, values)
            field[:, cols] = updated
            if s < SUB - 1:
                target[:count, cols], target[count:, cols] = split(updated)
    pairs = [
        (field.at[:, lane_tile(lax.rem(turn[0] + m, TILES) + TILES)], out) for m, out in enumerate(outs)
    ]
    for copy in copy_all(pairs, flags):
        copy.wait()


def propagate(turn, rows, tables, sides, first, low, count):
    total = 3 * TILES
    return pl.pallas_call(
        functools.partial(propagate_kernel, first, low),
        out_shape=[jax.ShapeDtypeStruct((count, LANES), jnp.float32)] * TILES,
        in_specs=[SMEM, VMEM] + [ANY] * 6,
        out_specs=[ANY] * TILES,
        scratch_shapes=[
            pltpu.VMEM((8, 3 * DEEP), jnp.float32),
            pltpu.VMEM((count, 3 * DEEP), jnp.float32),
            pltpu.VMEM((2 * count, 3 * DEEP), jnp.bfloat16),
            pltpu.VMEM((2 * count, 3 * DEEP), jnp.bfloat16),
            pltpu.VMEM((total, count, LANES), jnp.float32),
            pltpu.VMEM((total, count, LANES), jnp.float32),
            pltpu.VMEM((total, 2 * LANES, 2 * LANES), jnp.bfloat16),
            pltpu.VMEM((total, 2 * LANES, 2 * LANES), jnp.bfloat16),
            pltpu.SemaphoreType.DMA((6,)),
        ],
        compiler_params=PARAMS,
        name="propagate",
    )(turn, rows, *tables, *sides)


def source_kernel(starts, step, arrived, quad, strength, turn, blocks, turned, *refs):
    ins, outs, (field, rounded, total, flags) = refs[:arrived], refs[arrived:-4], refs[-4:]
    peers = len(outs)
    row_count = field.shape[0] // peers
    pairs = []
    for m, group in enumerate(starts):
        base = lax.rem(turn[0] + peers - m, peers) * row_count
        for offset, ref in zip(group, ins[m * len(group) : (m + 1) * len(group)]):
            pairs.append((ref, field.at[pl.ds(pl.multiple_of(base + offset, 8), ref.shape[0]), :]))
    for copy in copy_all(pairs, flags):
        copy.wait()
    values = field[...]
    total[...] = values
    rounded[...] = values.astype(jnp.bfloat16)

    def rows_of(f):
        return pl.ds(pl.multiple_of(f * ND, ND), ND)

    def some(g, carry):
        products = []
        for k in range(step):
            j = g * step + k
            left = jnp.dot(blocks[j], rounded[rows_of(quad[0, j]), :], preferred_element_type=jnp.float32)
            right = jnp.dot(turned[j], rounded[rows_of(quad[1, j]), :], preferred_element_type=jnp.float32)
            products.append((left * right * field[rows_of(quad[2, j]), :]).astype(jnp.bfloat16))
        for k in range(step):
            j = g * step + k
            part = jnp.dot(blocks[j], products[k], preferred_element_type=jnp.float32)
            rows = rows_of(quad[3, j])
            total[rows, :] += (source_step * strength[j]) * part
        return carry

    lax.fori_loop(0, blocks.shape[0] // step, some, 0)
    pairs = []
    for m, out in enumerate(outs):
        base = lax.rem(turn[0] + m, peers) * row_count
        pairs.append((total.at[pl.ds(pl.multiple_of(base, 8), row_count), :], out))
    for copy in copy_all(pairs, flags):
        copy.wait()


def source_term(turn, pieces, starts, quad_index, strength, blocks, turned, peers):
    columns = pieces[0].shape[1]
    row_count = NF * ND // peers
    step = math.gcd(blocks.shape[0], 8)
    return pl.pallas_call(
        functools.partial(source_kernel, starts, step, len(pieces)),
        out_shape=[jax.ShapeDtypeStruct((row_count, columns), jnp.float32)] * peers,
        in_specs=[SMEM] * 3 + [VMEM] * 2 + [ANY] * len(pieces),
        out_specs=[ANY] * peers,
        scratch_shapes=[
            pltpu.VMEM((NF * ND, columns), jnp.float32),
            pltpu.VMEM((NF * ND, columns), jnp.bfloat16),
            pltpu.VMEM((NF * ND, columns), jnp.float32),
            pltpu.SemaphoreType.DMA((max(len(pieces), peers),)),
        ],
        compiler_params=PARAMS,
        name="source",
    )(quad_index, strength, turn, blocks, turned, *pieces)


def gather_kernel(turn, *refs):
    ins, out, flags = refs[:-2], refs[-2], refs[-1]
    peers = len(ins)
    pairs = [(ref, out.at[:, lane_tile(lax.rem(turn[0] + peers - m, peers))]) for m, ref in enumerate(ins)]
    for copy in copy_all(pairs, flags):
        copy.wait()


def gather_columns(turn, pieces):
    rows, columns = pieces[0].shape
    return pl.pallas_call(
        gather_kernel,
        out_shape=jax.ShapeDtypeStruct((rows, columns * len(pieces)), jnp.float32),
        in_specs=[SMEM] + [ANY] * len(pieces),
        out_specs=ANY,
        scratch_shapes=[pltpu.SemaphoreType.DMA((len(pieces),))],
        compiler_params=PARAMS,
        name="columns",
    )(turn, *pieces)


def from_sides(cells, width):
    count = lax.axis_size("space")
    head, tail = cells[:, :width], cells[:, cells.shape[1] - width :]
    before = lax.ppermute(tail, "space", [(i, i + 1) for i in range(count - 1)])
    after = lax.ppermute(head, "space", [(i + 1, i) for i in range(count - 1)])
    return before, after


def point_table(neighbours, current_east, current_north):
    columns = neighbours.shape[1]
    tile = jnp.arange(columns, dtype=jnp.int32) // LANES * LANES
    west, east, south, north = neighbours
    return jnp.stack(
        [
            (west - tile).astype(jnp.float32),
            (east - tile - LANES).astype(jnp.float32),
            (south - tile).astype(jnp.float32),
            (north - tile - LANES).astype(jnp.float32),
            current_east,
            current_north,
            jnp.full((columns,), courant_limit, jnp.float32),
            jnp.zeros((columns,), jnp.float32),
        ]
    )


def row_table(first_comp, row_count, substeps, wave_speed):
    angles = (jnp.arange(ND, dtype=jnp.float32) + 0.5) * (2.0 * math.pi / ND)
    inverse = courant_scale / substeps.astype(jnp.float32)
    speed = wave_speed[:, None]
    along = [(speed * wave(angles)[None, :]).reshape(NF * ND) * inverse for wave in (jnp.cos, jnp.sin)]
    table = jnp.stack(along + [inverse, substeps.astype(jnp.float32)])
    own = lax.dynamic_slice_in_dim(table, first_comp, row_count, axis=1)
    return jnp.pad(own, ((0, 4), (0, -row_count % LANES)))


def cuts_of(row_count):
    middle = row_count // 2 // 16 * 16
    return [(0, middle), (middle, row_count)]


def shards(
    spectrum,
    wave_speed,
    current_east,
    current_north,
    substeps,
    neighbours,
    blocks,
    quad_index,
    strength,
):
    peers = lax.axis_size("comp")
    row_count, columns = spectrum.shape
    own_index = lax.axis_index("comp").astype(jnp.int32)
    turn = own_index.reshape(1)
    table = point_table(neighbours, current_east, current_north)
    rows = row_table(own_index * row_count, row_count, substeps, wave_speed)
    turned = blocks.swapaxes(1, 2)
    if columns == DEEP and peers == TILES and row_count % 16 == 0:
        cuts = cuts_of(row_count)
        sent = [[] for _ in range(peers)]
        tables, moved = None, None
        for low, high in cuts:
            chunk = spectrum[low:high]
            if tables is None:
                chunk = jnp.concatenate([table, chunk])
            else:
                chunk, *tables = lax.optimization_barrier((chunk, *tables))
            before, after = from_sides(chunk, DEEP)
            sides = (before, chunk, after)
            first = 0 if tables else 8
            tables = tables or sides
            moved = propagate(turn, rows, tables, sides, first, low, high - low)
            if sent[1]:
                arrived = [group[-1] for group in sent[1:]]
                held = lax.optimization_barrier((*moved, *arrived))
                moved = held[:peers]
                for group, piece in zip(sent[1:], held[peers:]):
                    group[-1] = piece
            for m in range(peers):
                piece = moved[m]
                if m:
                    piece = lax.ppermute(piece, "comp", [(i, (i + m) % peers) for i in range(peers)])
                sent[m].append(piece)
        pieces = [piece for group in sent for piece in group]
        starts = [[low for low, high in cuts]] * peers
        results = source_term(turn, pieces, starts, quad_index, strength, blocks, turned, peers)
        back = [
            lax.ppermute(piece, "comp", [(i, (i + m) % peers) for i in range(peers)]) if m else piece
            for m, piece in enumerate(results)
        ]
        return gather_columns(turn, back)
    still = jnp.zeros((1,), jnp.int32)
    extra = -row_count % 16
    chunk = jnp.pad(spectrum, ((0, extra), (0, 0)))
    before, after = from_sides(chunk, DEEP)
    wide = jnp.concatenate([before, chunk, after], axis=1)
    before, after = from_sides(table, DEEP)
    table = jnp.concatenate([before, table, after], axis=1)
    tiles = []
    for start in range(0, columns, DEEP):
        sides = [wide[:, start + j * DEEP : start + (j + 1) * DEEP] for j in range(3)]
        tables = [table[:, start + j * DEEP : start + (j + 1) * DEEP] for j in range(3)]
        tiles += propagate(still, rows, tables, sides, 0, 0, row_count + extra)
    grid = jnp.concatenate(tiles, axis=1)[:row_count].reshape(row_count, peers, columns // peers).swapaxes(0, 1)
    arrived = lax.all_to_all(grid, "comp", 0, 0, tiled=True)
    arrived = arrived.reshape(NF * ND, columns // peers)
    (results,) = source_term(still, [arrived], [[0]], quad_index, strength, blocks, turned, 1)
    results = results.reshape(peers, row_count, columns // peers)
    back = lax.all_to_all(results, "comp", 0, 0, tiled=True)
    return back.swapaxes(0, 1).reshape(row_count, columns)


def solution(mesh):
    in_specs = (
        P("comp", ("grp", "space")),
        P(),
        P(("grp", "space")),
        P(("grp", "space")),
        P(),
        P(None, ("grp", "space")),
        P(),
        P(),
        P(),
    )
    out_specs = P("comp", ("grp", "space"))
    return jax.shard_map(shards, mesh=mesh, in_specs=in_specs, out_specs=out_specs, check_vma=False)
```

time: 121 us -> 136 us (1.12); the launches traced: 119 us -> 136 us
  Pallas kernels: 35.1 us -> 60.8 us
  starting transfers between devices: 28.1 us -> 18.8 us
  waiting for transfers between devices: 45 us -> 48.9 us
  local copies, waits for them, and re-layouts: 9.5 us -> 5.82 us
    pallas_call x1, Pallas kernels: 2.4 us -> 36.9 us  [gather_columns(): pl.pallas_call(gather_kernel, out_shape=jax.ShapeDtypeStruct((rows, colum...]
    pallas_call x2, Pallas kernels: 26.8 us -> 17 us  [propagate(): pl.pallas_call(functools.partial(propagate_kernel, first, low), out_shape...]
    ppermute x3 -> x2, starting transfers between devices: 11 us -> 5.59 us  [from_sides(): before = lax.ppermute(tail, 'space', [(i, i + 1) for i in range(count - 1)])]
    ppermute x3 -> x2, waiting for transfers between devices: 0.61 us -> 5.01 us  [from_sides(): before = lax.ppermute(tail, 'space', [(i, i + 1) for i in range(count - 1)])]
    unnamed x43 -> x39, local copies, waits for them, and re-layouts: 6.94 us -> 3.51 us
    ppermute x9, waiting for transfers between devices: 42.3 us -> 39.5 us  [shards(): lax.ppermute(piece, 'comp', [(i, (i + m) % peers) for i in range(peers)])]
    ppermute x9, starting transfers between devices: 11.4 us -> 8.82 us  [shards(): lax.ppermute(piece, 'comp', [(i, (i + m) % peers) for i in range(peers)])]
    ppermute x3 -> x2, waiting for transfers between devices: 2.11 us -> 4.4 us  [from_sides(): after = lax.ppermute(head, 'space', [(i + 1, i) for i in range(count - 1)])]
  transfers between devices with their start and end apart: 15 -> 13, of which waited for: 7 -> 10; matrix products, arithmetic and copies ran while one was open for 4% -> 2% of each run, Pallas kernels for 23% -> 13%
where the time goes in v2:
time: 136 us
  Pallas kernels  60.8 us (45%)
  waiting for transfers between devices  48.9 us (36%)
  starting transfers between devices  18.8 us (14%)
  local copies, waits for them, and re-layouts  5.82 us (4%)
    ppermute x9, waiting for transfers between devices, shards(): lax.ppermute(piece, 'comp', [(i, (i + m) % peers) for i in range(peers)])  39.5 us
    pallas_call x1, Pallas kernels, gather_columns(): pl.pallas_call(gather_kernel, out_shape=jax.ShapeDtypeStruct((rows, colum...  36.9 us
    pallas_call x2, Pallas kernels, propagate(): pl.pallas_call(functools.partial(propagate_kernel, first, low), out_shape...  17 us
    ppermute x9, starting transfers between devices, shards(): lax.ppermute(piece, 'comp', [(i, (i + m) % peers) for i in range(peers)])  8.82 us
    pallas_call x1, Pallas kernels, source_term(): pl.pallas_call(functools.partial(source_kernel, starts, step, len(pieces)...  6.87 us
    ppermute x2, starting transfers between devices, from_sides(): before = lax.ppermute(tail, 'space', [(i, i + 1) for i in range(count - 1)])  5.59 us
    ppermute x2, waiting for transfers between devices, from_sides(): before = lax.ppermute(tail, 'space', [(i, i + 1) for i in range(count - 1)])  5.01 us
    ppermute x2, waiting for transfers between devices, from_sides(): after = lax.ppermute(head, 'space', [(i + 1, i) for i in range(count - 1)])  4.4 us
  transfers between devices with their start and end apart: 13, of which 10 were waited for; matrix products, arithmetic and copies ran while one was open for 2% of the time, Pallas kernels for 13%

profile of v2, /device:TPU:13, one launch (start us, length us, event | category | flops | bytes accessed | tf_op | source)
XLA Modules:
  0.0 135.6 jit_solution(5625504445165077179)
XLA Ops:
  0.0 0.9 add_convert_fusion
  0.9 0.0 copy-start.16
  0.9 0.0 copy-start.17
  0.9 1.3 fusion.8
  2.2 0.0 copy-start.18
  2.2 0.0 copy-start.15
  2.3 0.0 copy-done.16
  2.3 0.0 copy-done.17
  2.3 0.2 concatenate.3.refs_1_.refs_4_
  2.5 3.7 %collective-permute-start = (f32[296,512]{1,0:T(8,128)S(1)}, f32[296,512]{1,0:T(8,128)S(1)}, u32[]{:S(2)}, u32[]{:S(2)}) collective-permute-start(f32[296,512]{1,0:T(8,128)S(1)} %concatenate.3.refs_1_.refs_4_), channel_id=1, source_target_pairs={{0,1},{1,2},{2,3},{4,5},{5,6},{6,7},{8,9},{9,10},{10,11},{12,13},{... | collective-permute-start | bytes 1818632 | tf_op jit(solution)/shard_map/ppermute | solution.py:204
  6.2 1.9 %collective-permute-start.1 = (f32[296,512]{1,0:T(8,128)S(1)}, f32[296,512]{1,0:T(8,128)S(1)}, u32[]{:S(2)}, u32[]{:S(2)}) collective-permute-start(f32[296,512]{1,0:T(8,128)S(1)} %concatenate.3.refs_1_.refs_4_), channel_id=1, source_target_pairs={{1,0},{2,1},{3,2},{5,4},{6,5},{7,6},{9,8},{10,9},{11,10},{13,12},{... | collective-permute-start | bytes 1818632 | tf_op jit(solution)/shard_map/ppermute | solution.py:205
  8.2 5.0 %collective-permute-done.refs_0_.refs_3_ = f32[296,512]{1,0:T(8,128)S(1)} collective-permute-done((f32[296,512]{1,0:T(8,128)S(1)}, f32[296,512]{1,0:T(8,128)S(1)}, u32[]{:S(2)}, u32[]{:S(2)}) %collective-permute-start) | collective-permute-done | bytes 606240 | tf_op jit(solution)/shard_map/ppermute | solution.py:204
  13.2 4.4 %collective-permute-done.1.refs_2_.refs_5_ = f32[296,512]{1,0:T(8,128)S(1)} collective-permute-done((f32[296,512]{1,0:T(8,128)S(1)}, f32[296,512]{1,0:T(8,128)S(1)}, u32[]{:S(2)}, u32[]{:S(2)}) %collective-permute-start.1) | collective-permute-done | bytes 606240 | tf_op jit(solution)/shard_map/ppermute | solution.py:205
  17.6 1.9 %collective-permute-start.2 = (f32[288,512]{1,0:T(8,128)S(1)}, f32[288,512]{1,0:T(8,128)S(1)}, u32[]{:S(2)}, u32[]{:S(2)}) collective-permute-start(f32[288,512]{1,0:T(8,128)S(1)} %get-tuple-element.32.refs_4_), channel_id=1, source_target_pairs={{0,1},{1,2},{2,3},{4,5},{5,6},{6,7},{8,9},{9,10},{10,11},{12,13},{... | collective-permute-start | bytes 1769480 | tf_op jit(solution)/shard_map/ppermute | solution.py:204
  19.5 2.4 %collective-permute-start.3 = (f32[288,512]{1,0:T(8,128)S(1)}, f32[288,512]{1,0:T(8,128)}, u32[]{:S(2)}, u32[]{:S(2)}) collective-permute-start(f32[288,512]{1,0:T(8,128)S(1)} %get-tuple-element.32.refs_4_), channel_id=1, source_target_pairs={{1,0},{2,1},{3,2},{5,4},{6,5},{7,6},{9,8},{10,9},{11,10},{13,12},{... | collective-permute-start | bytes 1769480 | tf_op jit(solution)/shard_map/ppermute | solution.py:205
  21.9 0.1 broadcast_multiply_fusion
  22.0 0.1 mul.80
  22.1 0.1 mul.84
  22.3 0.1 fusion.2
  22.4 0.6 pad.4.rows
  23.0 8.5 %propagate.2 = (f32[288,128]{1,0:T(8,128)}, f32[288,128]{1,0:T(8,128)}, f32[288,128]{1,0:T(8,128)}, f32[288,128]{1,0:T(8,128)}) custom-call(s32[1]{0:T(128)} %bitcast.turn, f32[8,640]{1,0:T(8,128)} %pad.4.rows, f32[296,512]{1,0:T(8,128)} %copy-done.1, f32[296,512]{1,0:T(8,128)} %copy-done, f32[296,512]{1,0:T(8,128)} %copy-done.2, f32[296,512]{1,0:T(8,128)} %copy-done.1, ...), custom_call_target="tpu_custom_call" | custom-call | tf_op jit(solution)/shard_map/propagate/pallas_call | solution.py:98
  31.5 1.4 collective-permute-start.4
  32.9 1.1 collective-permute-start.5
  34.0 1.4 %collective-permute-start.6 = (f32[288,128]{1,0:T(8,128)}, f32[288,128]{1,0:T(8,128)S(1)}, u32[]{:S(2)}, u32[]{:S(2)}) collective-permute-start(f32[288,128]{1,0:T(8,128)} %get-tuple-element.39), channel_id=1, source_target_pairs={{0,12},{4,0},{8,4},{12,8},{1,13},{5,1},{9,5},{13,9},{2,14},{6,2},{... | collective-permute-start | bytes 442376 | tf_op jit(solution)/shard_map/ppermute | solution.py:284
  35.4 0.0 collective-permute-done.2.refs_3_
  35.4 0.0 collective-permute-done.3.refs_5_
  35.4 0.8 copy-done.5
  36.2 8.5 %propagate.3 = (f32[288,128]{1,0:T(8,128)}, f32[288,128]{1,0:T(8,128)}, f32[288,128]{1,0:T(8,128)}, f32[288,128]{1,0:T(8,128)}) custom-call(s32[1]{0:T(128)} %bitcast.turn, f32[8,640]{1,0:T(8,128)} %pad.4.rows, f32[296,512]{1,0:T(8,128)} %copy-done.1, f32[296,512]{1,0:T(8,128)} %copy-done, f32[296,512]{1,0:T(8,128)} %copy-done.2, f32[288,512]{1,0:T(8,128)} %copy-done.5, ...), custom_call_target="tpu_custom_call" | custom-call | tf_op jit(solution)/shard_map/propagate/pallas_call | solution.py:98
  44.7 0.0 collective-permute-done.4.refs_2_
  44.7 1.5 %collective-permute-done.5.refs_4_ = f32[288,128]{1,0:T(8,128)S(1)} collective-permute-done((f32[288,128]{1,0:T(8,128)}, f32[288,128]{1,0:T(8,128)S(1)}, u32[]{:S(2)}, u32[]{:S(2)}) %collective-permute-start.5) | collective-permute-done | bytes 147488 | tf_op jit(solution)/shard_map/ppermute | solution.py:284
  46.2 1.6 %collective-permute-done.6.refs_6_ = f32[288,128]{1,0:T(8,128)S(1)} collective-permute-done((f32[288,128]{1,0:T(8,128)}, f32[288,128]{1,0:T(8,128)S(1)}, u32[]{:S(2)}, u32[]{:S(2)}) %collective-permute-start.6) | collective-permute-done | bytes 147488 | tf_op jit(solution)/shard_map/ppermute | solution.py:284
  47.7 0.0 collective-permute-start.7
  47.8 1.4 %collective-permute-start.8 = (f32[288,128]{1,0:T(8,128)}, f32[288,128]{1,0:T(8,128)S(1)}, u32[]{:S(2)}, u32[]{:S(2)}) collective-permute-start(f32[288,128]{1,0:T(8,128)} %get-tuple-element.44), channel_id=1, source_target_pairs={{0,8},{4,12},{8,0},{12,4},{1,9},{5,13},{9,1},{13,5},{2,10},{6,14},... | collective-permute-start | bytes 442376 | tf_op jit(solution)/shard_map/ppermute | solution.py:284
  49.1 1.4 %collective-permute-start.9 = (f32[288,128]{1,0:T(8,128)}, f32[288,128]{1,0:T(8,128)S(1)}, u32[]{:S(2)}, u32[]{:S(2)}) collective-permute-start(f32[288,128]{1,0:T(8,128)} %get-tuple-element.46), channel_id=1, source_target_pairs={{0,12},{4,0},{8,4},{12,8},{1,13},{5,1},{9,5},{13,9},{2,14},{6,2},{... | collective-permute-start | bytes 442376 | tf_op jit(solution)/shard_map/ppermute | solution.py:284
  50.5 1.3 copy.10
  51.8 1.1 collective-permute-done.7.refs_3_
  53.0 7.7 %collective-permute-done.8.refs_5_ = f32[288,128]{1,0:T(8,128)S(1)} collective-permute-done((f32[288,128]{1,0:T(8,128)}, f32[288,128]{1,0:T(8,128)S(1)}, u32[]{:S(2)}, u32[]{:S(2)}) %collective-permute-start.8) | collective-permute-done | bytes 147488 | tf_op jit(solution)/shard_map/ppermute | solution.py:284
  60.7 2.4 %collective-permute-done.9.refs_7_ = f32[288,128]{1,0:T(8,128)S(1)} collective-permute-done((f32[288,128]{1,0:T(8,128)}, f32[288,128]{1,0:T(8,128)S(1)}, u32[]{:S(2)}, u32[]{:S(2)}) %collective-permute-start.9) | collective-permute-done | bytes 147488 | tf_op jit(solution)/shard_map/ppermute | solution.py:284
  63.1 0.6 copy-done.14
  63.7 6.9 %source.1 = (f32[576,128]{1,0:T(8,128)}, f32[576,128]{1,0:T(8,128)}, f32[576,128]{1,0:T(8,128)}, f32[576,128]{1,0:T(8,128)}) custom-call(s32[4,64]{1,0:T(4,128)} %quad.1, f32[64]{0:T(128)} %strength.1, s32[1]{0:T(128)} %bitcast.turn, bf16[64,64,64]{2,1,0:T(8,128)(2,1)} %blocks.1, bf16[64,64,64]{2,1,0:T(8,128)(2,1)} %bitcast.4, ...), custom_call_target="tpu_custom_call" | custom-call | tf_op jit(solution)/shard_map/source/pallas_call | solution.py:164
  70.6 0.1 collective-permute-start.10
  70.6 0.8 collective-permute-start.11
  71.4 1.4 %collective-permute-start.12 = (f32[576,128]{1,0:T(8,128)}, f32[576,128]{1,0:T(8,128)S(1)}, u32[]{:S(2)}, u32[]{:S(2)}) collective-permute-start(f32[576,128]{1,0:T(8,128)} %get-tuple-element.50), channel_id=1, source_target_pairs={{0,12},{4,0},{8,4},{12,8},{1,13},{5,1},{9,5},{13,9},{2,14},{6,2},{... | collective-permute-start | bytes 884744 | tf_op jit(solution)/shard_map/ppermute | solution.py:290
  72.8 6.1 %collective-permute-done.10.refs_1_ = f32[576,128]{1,0:T(8,128)S(1)} collective-permute-done((f32[576,128]{1,0:T(8,128)}, f32[576,128]{1,0:T(8,128)S(1)}, u32[]{:S(2)}, u32[]{:S(2)}) %collective-permute-start.10) | collective-permute-done | bytes 294944 | tf_op jit(solution)/shard_map/ppermute | solution.py:290
  78.9 17.2 %collective-permute-done.11.refs_2_ = f32[576,128]{1,0:T(8,128)S(1)} collective-permute-done((f32[576,128]{1,0:T(8,128)}, f32[576,128]{1,0:T(8,128)S(1)}, u32[]{:S(2)}, u32[]{:S(2)}) %collective-permute-start.11) | collective-permute-done | bytes 294944 | tf_op jit(solution)/shard_map/ppermute | solution.py:290
  96.1 1.9 %collective-permute-done.12.refs_3_ = f32[576,128]{1,0:T(8,128)S(1)} collective-permute-done((f32[576,128]{1,0:T(8,128)}, f32[576,128]{1,0:T(8,128)S(1)}, u32[]{:S(2)}, u32[]{:S(2)}) %collective-permute-start.12) | collective-permute-done | bytes 294944 | tf_op jit(solution)/shard_map/ppermute | solution.py:290
  98.0 0.7 copy-done.8
  98.7 36.9 %columns.1 = f32[576,512]{1,0:T(8,128)} custom-call(s32[1]{0:T(128)} %bitcast.turn, f32[576,128]{1,0:T(8,128)} %get-tuple-element.47.refs_0_, f32[576,128]{1,0:T(8,128)} %copy-done.6, f32[576,128]{1,0:T(8,128)} %copy-done.7, f32[576,128]{1,0:T(8,128)} %copy-done.8), custom_call_target="tpu_custom_call" | custom-call | tf_op jit(solution)/shard_map/columns/pallas_call | solution.py:190
  (38 shorter events, 0.2 us)
Async XLA Ops:
  0.9 1.4 %copy-start.16 = (f32[512]{0:T(512)S(1)}, f32[512]{0:T(512)}, u32[]{:S(2)}) copy-start(f32[512]{0:T(512)} %param.11) | copy-start | bytes 6148
  0.9 1.4 %copy-start.17 = (f32[512]{0:T(512)S(1)}, f32[512]{0:T(512)}, u32[]{:S(2)}) copy-start(f32[512]{0:T(512)} %param.12) | copy-start | bytes 6148
  2.2 29.3 %copy-start.4 = (f32[288,512]{1,0:T(8,128)}, f32[288,512]{1,0:T(8,128)S(1)}, u32[]{:S(2)}) copy-start(f32[288,512]{1,0:T(8,128)S(1)} %get-tuple-element.32.refs_4_) | copy-start | bytes 1769476
  2.2 19.7 %copy-start.18 = (f32[36]{0:T(128)S(1)}, f32[36]{0:T(128)}, u32[]{:S(2)}) copy-start(f32[36]{0:T(128)} %param.10) | copy-start | bytes 436
  2.2 19.9 %copy-start.15 = (s32[2304]{0:T(1024)S(1)}, s32[2304]{0:T(1024)}, u32[]{:S(2)}) copy-start(s32[2304]{0:T(1024)} %param.13) | copy-start | bytes 27652
  2.5 20.5 %copy-start = (f32[296,512]{1,0:T(8,128)}, f32[296,512]{1,0:T(8,128)S(1)}, u32[]{:S(2)}) copy-start(f32[296,512]{1,0:T(8,128)S(1)} %concatenate.3.refs_1_.refs_4_) | copy-start | bytes 1818628
  2.5 10.7 %collective-permute-start = (f32[296,512]{1,0:T(8,128)S(1)}, f32[296,512]{1,0:T(8,128)S(1)}, u32[]{:S(2)}, u32[]{:S(2)}) collective-permute-start(f32[296,512]{1,0:T(8,128)S(1)} %concatenate.3.refs_1_.refs_4_), channel_id=1, source_target_pairs={{0,1},{1,2},{2,3},{4,5},{5,6},{6,7},{8,9},{9,10},{10,11},{12,13},{... | collective-permute-start | bytes 1818632 | tf_op jit(solution)/shard_map/ppermute | solution.py:204
  6.2 11.4 %collective-permute-start.1 = (f32[296,512]{1,0:T(8,128)S(1)}, f32[296,512]{1,0:T(8,128)S(1)}, u32[]{:S(2)}, u32[]{:S(2)}) collective-permute-start(f32[296,512]{1,0:T(8,128)S(1)} %concatenate.3.refs_1_.refs_4_), channel_id=1, source_target_pairs={{1,0},{2,1},{3,2},{5,4},{6,5},{7,6},{9,8},{10,9},{11,10},{13,12},{... | collective-permute-start | bytes 1818632 | tf_op jit(solution)/shard_map/ppermute | solution.py:205
  13.2 9.8 %copy-start.1 = (f32[296,512]{1,0:T(8,128)}, f32[296,512]{1,0:T(8,128)S(1)}, u32[]{:S(2)}) copy-start(f32[296,512]{1,0:T(8,128)S(1)} %collective-permute-done.refs_0_.refs_3_) | copy-start | bytes 1818628
  17.6 5.4 %copy-start.2 = (f32[296,512]{1,0:T(8,128)}, f32[296,512]{1,0:T(8,128)S(1)}, u32[]{:S(2)}) copy-start(f32[296,512]{1,0:T(8,128)S(1)} %collective-permute-done.1.refs_2_.refs_5_) | copy-start | bytes 1818628
  17.6 17.8 %collective-permute-start.2 = (f32[288,512]{1,0:T(8,128)S(1)}, f32[288,512]{1,0:T(8,128)S(1)}, u32[]{:S(2)}, u32[]{:S(2)}) collective-permute-start(f32[288,512]{1,0:T(8,128)S(1)} %get-tuple-element.32.refs_4_), channel_id=1, source_target_pairs={{0,1},{1,2},{2,3},{4,5},{5,6},{6,7},{8,9},{9,10},{10,11},{12,13},{... | collective-permute-start | bytes 1769480 | tf_op jit(solution)/shard_map/ppermute | solution.py:204
  19.5 15.9 %collective-permute-start.3 = (f32[288,512]{1,0:T(8,128)S(1)}, f32[288,512]{1,0:T(8,128)}, u32[]{:S(2)}, u32[]{:S(2)}) collective-permute-start(f32[288,512]{1,0:T(8,128)S(1)} %get-tuple-element.32.refs_4_), channel_id=1, source_target_pairs={{1,0},{2,1},{3,2},{5,4},{6,5},{7,6},{9,8},{10,9},{11,10},{13,12},{... | collective-permute-start | bytes 1769480 | tf_op jit(solution)/shard_map/ppermute | solution.py:205
  31.5 13.2 %collective-permute-start.4 = (f32[288,128]{1,0:T(8,128)}, f32[288,128]{1,0:T(8,128)S(1)}, u32[]{:S(2)}, u32[]{:S(2)}) collective-permute-start(f32[288,128]{1,0:T(8,128)} %get-tuple-element.37), channel_id=1, source_target_pairs={{0,4},{4,8},{8,12},{12,0},{1,5},{5,9},{9,13},{13,1},{2,6},{6,10},{... | collective-permute-start | bytes 442376 | tf_op jit(solution)/shard_map/ppermute | solution.py:284
  32.9 13.3 %collective-permute-start.5 = (f32[288,128]{1,0:T(8,128)}, f32[288,128]{1,0:T(8,128)S(1)}, u32[]{:S(2)}, u32[]{:S(2)}) collective-permute-start(f32[288,128]{1,0:T(8,128)} %get-tuple-element.38), channel_id=1, source_target_pairs={{0,8},{4,12},{8,0},{12,4},{1,9},{5,13},{9,1},{13,5},{2,10},{6,14},... | collective-permute-start | bytes 442376 | tf_op jit(solution)/shard_map/ppermute | solution.py:284
  34.0 16.6 %copy-start.3 = (bf16[64,64,64]{2,1,0:T(8,128)(2,1)S(1)}, bf16[64,64,64]{2,1,0:T(8,128)(2,1)}, u32[]{:S(2)}) copy-start(bf16[64,64,64]{2,1,0:T(8,128)(2,1)} %blocks.1) | copy-start | bytes 1572868
  34.0 13.8 %collective-permute-start.6 = (f32[288,128]{1,0:T(8,128)}, f32[288,128]{1,0:T(8,128)S(1)}, u32[]{:S(2)}, u32[]{:S(2)}) collective-permute-start(f32[288,128]{1,0:T(8,128)} %get-tuple-element.39), channel_id=1, source_target_pairs={{0,12},{4,0},{8,4},{12,8},{1,13},{5,1},{9,5},{13,9},{2,14},{6,2},{... | collective-permute-start | bytes 442376 | tf_op jit(solution)/shard_map/ppermute | solution.py:284
  35.4 0.8 copy-start.5
  44.7 18.4 %copy-start.9 = (f32[288,128]{1,0:T(8,128)}, f32[288,128]{1,0:T(8,128)S(1)}, u32[]{:S(2)}) copy-start(f32[288,128]{1,0:T(8,128)S(1)} %collective-permute-done.4.refs_2_) | copy-start | bytes 442372
  46.2 16.9 %copy-start.10 = (f32[288,128]{1,0:T(8,128)}, f32[288,128]{1,0:T(8,128)S(1)}, u32[]{:S(2)}) copy-start(f32[288,128]{1,0:T(8,128)S(1)} %collective-permute-done.5.refs_4_) | copy-start | bytes 442372
  47.7 15.3 %copy-start.11 = (f32[288,128]{1,0:T(8,128)}, f32[288,128]{1,0:T(8,128)S(1)}, u32[]{:S(2)}) copy-start(f32[288,128]{1,0:T(8,128)S(1)} %collective-permute-done.6.refs_6_) | copy-start | bytes 442372
  47.7 5.2 %collective-permute-start.7 = (f32[288,128]{1,0:T(8,128)}, f32[288,128]{1,0:T(8,128)S(1)}, u32[]{:S(2)}, u32[]{:S(2)}) collective-permute-start(f32[288,128]{1,0:T(8,128)} %get-tuple-element.42), channel_id=1, source_target_pairs={{0,4},{4,8},{8,12},{12,0},{1,5},{5,9},{9,13},{13,1},{2,6},{6,10},{... | collective-permute-start | bytes 442376 | tf_op jit(solution)/shard_map/ppermute | solution.py:284
  47.8 12.9 %collective-permute-start.8 = (f32[288,128]{1,0:T(8,128)}, f32[288,128]{1,0:T(8,128)S(1)}, u32[]{:S(2)}, u32[]{:S(2)}) collective-permute-start(f32[288,128]{1,0:T(8,128)} %get-tuple-element.44), channel_id=1, source_target_pairs={{0,8},{4,12},{8,0},{12,4},{1,9},{5,13},{9,1},{13,5},{2,10},{6,14},... | collective-permute-start | bytes 442376 | tf_op jit(solution)/shard_map/ppermute | solution.py:284
  49.1 13.9 %collective-permute-start.9 = (f32[288,128]{1,0:T(8,128)}, f32[288,128]{1,0:T(8,128)S(1)}, u32[]{:S(2)}, u32[]{:S(2)}) collective-permute-start(f32[288,128]{1,0:T(8,128)} %get-tuple-element.46), channel_id=1, source_target_pairs={{0,12},{4,0},{8,4},{12,8},{1,13},{5,1},{9,5},{13,9},{2,14},{6,2},{... | collective-permute-start | bytes 442376 | tf_op jit(solution)/shard_map/ppermute | solution.py:284
  53.0 10.1 %copy-start.12 = (f32[288,128]{1,0:T(8,128)}, f32[288,128]{1,0:T(8,128)S(1)}, u32[]{:S(2)}) copy-start(f32[288,128]{1,0:T(8,128)S(1)} %collective-permute-done.7.refs_3_) | copy-start | bytes 442372
  60.7 2.4 %copy-start.13 = (f32[288,128]{1,0:T(8,128)}, f32[288,128]{1,0:T(8,128)S(1)}, u32[]{:S(2)}) copy-start(f32[288,128]{1,0:T(8,128)S(1)} %collective-permute-done.8.refs_5_) | copy-start | bytes 442372
  63.1 0.6 copy-start.14
  70.6 8.3 %collective-permute-start.10 = (f32[576,128]{1,0:T(8,128)}, f32[576,128]{1,0:T(8,128)S(1)}, u32[]{:S(2)}, u32[]{:S(2)}) collective-permute-start(f32[576,128]{1,0:T(8,128)} %get-tuple-element.48), channel_id=1, source_target_pairs={{0,4},{4,8},{8,12},{12,0},{1,5},{5,9},{9,13},{13,1},{2,6},{6,10},{... | collective-permute-start | bytes 884744 | tf_op jit(solution)/shard_map/ppermute | solution.py:290
  70.6 25.5 %collective-permute-start.11 = (f32[576,128]{1,0:T(8,128)}, f32[576,128]{1,0:T(8,128)S(1)}, u32[]{:S(2)}, u32[]{:S(2)}) collective-permute-start(f32[576,128]{1,0:T(8,128)} %get-tuple-element.49), channel_id=1, source_target_pairs={{0,8},{4,12},{8,0},{12,4},{1,9},{5,13},{9,1},{13,5},{2,10},{6,14},... | collective-permute-start | bytes 884744 | tf_op jit(solution)/shard_map/ppermute | solution.py:290
  71.4 26.6 %collective-permute-start.12 = (f32[576,128]{1,0:T(8,128)}, f32[576,128]{1,0:T(8,128)S(1)}, u32[]{:S(2)}, u32[]{:S(2)}) collective-permute-start(f32[576,128]{1,0:T(8,128)} %get-tuple-element.50), channel_id=1, source_target_pairs={{0,12},{4,0},{8,4},{12,8},{1,13},{5,1},{9,5},{13,9},{2,14},{6,2},{... | collective-permute-start | bytes 884744 | tf_op jit(solution)/shard_map/ppermute | solution.py:290
  78.9 19.1 %copy-start.6 = (f32[576,128]{1,0:T(8,128)}, f32[576,128]{1,0:T(8,128)S(1)}, u32[]{:S(2)}) copy-start(f32[576,128]{1,0:T(8,128)S(1)} %collective-permute-done.10.refs_1_) | copy-start | bytes 884740
  96.1 1.9 %copy-start.7 = (f32[576,128]{1,0:T(8,128)}, f32[576,128]{1,0:T(8,128)S(1)}, u32[]{:S(2)}) copy-start(f32[576,128]{1,0:T(8,128)S(1)} %collective-permute-done.11.refs_2_) | copy-start | bytes 884740
  98.0 0.7 copy-start.8

commit v3 on v2

--- a/solution.py
+++ b/solution.py
@@ -22,8 +22,11 @@
 
 VMEM = pl.BlockSpec(memory_space=pltpu.VMEM)
 SMEM = pl.BlockSpec(memory_space=pltpu.SMEM)
-ANY = pl.BlockSpec(memory_space=pl.ANY)
-PARAMS = pltpu.CompilerParams(vmem_limit_bytes=56 << 20)
+PARAMS = pltpu.CompilerParams(vmem_limit_bytes=40 << 20)
+
+
+def in_vmem(values):
+    return pltpu.with_memory_space_constraint(values, pltpu.VMEM)
 
 
 def split(values):
@@ -37,40 +40,46 @@
     return pl.ds(pl.multiple_of(t * LANES, LANES), width * LANES)
 
 
-def copy_all(pairs, flags):
-    copies = [pltpu.make_async_copy(source, target, flags.at[i]) for i, (source, target) in enumerate(pairs)]
-    for copy in copies:
-        copy.start()
-    return copies
-
-
-def propagate_kernel(first, low, turn, rows, *refs):
+def propagate_kernel(first, low, turn, odd, rows, *refs):
     tables, sides, outs = refs[:3], refs[3:6], refs[6 : 6 + TILES]
-    table, field, parts_a, parts_b, along_x, along_y, behind_pick, ahead_pick, flags = refs[6 + TILES :]
+    field, parts_a, parts_b, along_x, along_y, behind_pick, ahead_pick = refs[6 + TILES :]
     parts = (parts_a, parts_b)
     count = field.shape[0]
     total = 3 * TILES
-    pairs = [(ref.at[0:8, :], table.at[:, j * DEEP : (j + 1) * DEEP]) for j, ref in enumerate(tables)]
-    pairs += [(ref.at[first : first + count, :], field.at[:, j * DEEP : (j + 1) * DEEP]) for j, ref in enumerate(sides)]
-    copies = copy_all(pairs, flags)
+    turned = odd[0] == 1
     columns = jnp.transpose(rows[...])[low : low + count]
     east, north, inverse, substeps = (jnp.broadcast_to(columns[:, c : c + 1], (count, LANES)) for c in range(4))
     position = lax.broadcasted_iota(jnp.int32, (2 * LANES, LANES), 0).astype(jnp.float32)
-    for copy in copies:
-        copy.wait()
-    parts_a[:count], parts_a[count:] = split(field[...])
+
+    def region(group, taken, t):
+        cols = lane_tile(t % TILES)
+        near, own, far = (ref[taken, cols] for ref in group)
+        if t < TILES:
+            return jnp.where(turned, near, far)
+        return own if t < 2 * TILES else jnp.where(turned, far, near)
+
+    def prepare(t):
+        values = region(sides, slice(first, first + count), t)
+        field[:, lane_tile(t)] = values
+        parts_a[:count, lane_tile(t)], parts_a[count:, lane_tile(t)] = split(values)
+        if 0 < t < total - 1:
+            table = region(tables, slice(0, 8), t)
+            for pick, side in ((behind_pick, 0), (ahead_pick, 1)):
+                for d in range(2):
+                    chosen = position == table[2 * d + side : 2 * d + side + 1]
+                    pick[t, :, lane_tile(d)] = jnp.where(chosen, 1.0, 0.0).astype(jnp.bfloat16)
+            limit = table[6:7]
+            along_x[t] = jnp.clip(east + inverse * table[4:5], -limit, limit)
+            along_y[t] = jnp.clip(north + inverse * table[5:6], -limit, limit)
+
+    prepare(0)
+    prepare(1)
     for s in range(SUB):
         source, target = parts[s % 2], parts[1 - s % 2]
         for t in range(s + 1, total - 1 - s):
             cols = lane_tile(t)
             if s == 0:
-                for pick, side in ((behind_pick, 0), (ahead_pick, 1)):
-                    for d in range(2):
-                        chosen = position == table[2 * d + side : 2 * d + side + 1, cols]
-                        pick[t, :, lane_tile(d)] = jnp.where(chosen, 1.0, 0.0).astype(jnp.bfloat16)
-                limit = table[6:7, cols]
-                along_x[t] = jnp.clip(east + inverse * table[4:5, cols], -limit, limit)
-                along_y[t] = jnp.clip(north + inverse * table[5:6, cols], -limit, limit)
+                prepare(t + 1)
             behind = jnp.dot(source[:, lane_tile(t - 1, 2)], behind_pick[t], preferred_element_type=jnp.float32)
             ahead = jnp.dot(source[:, lane_tile(t, 2)], ahead_pick[t], preferred_element_type=jnp.float32)
             behind = behind[:count] + behind[count:]
@@ -86,22 +95,18 @@
             field[:, cols] = updated
             if s < SUB - 1:
                 target[:count, cols], target[count:, cols] = split(updated)
-    pairs = [
-        (field.at[:, lane_tile(lax.rem(turn[0] + m, TILES) + TILES)], out) for m, out in enumerate(outs)
-    ]
-    for copy in copy_all(pairs, flags):
-        copy.wait()
-
-
-def propagate(turn, rows, tables, sides, first, low, count):
+    for m, out in enumerate(outs):
+        out[...] = field[:, lane_tile(lax.rem(turn[0] + m, TILES) + TILES)]
+
+
+def propagate(turn, odd, rows, tables, sides, first, low, count):
     total = 3 * TILES
     return pl.pallas_call(
         functools.partial(propagate_kernel, first, low),
-        out_shape=[jax.ShapeDtypeStruct((count, LANES), jnp.float32)] * TILES,
-        in_specs=[SMEM, VMEM] + [ANY] * 6,
-        out_specs=[ANY] * TILES,
+        out_shape=[pltpu.VMEM((count, LANES), jnp.float32)] * TILES,
+        in_specs=[SMEM] * 2 + [VMEM] * 7,
+        out_specs=[VMEM] * TILES,
         scratch_shapes=[
-            pltpu.VMEM((8, 3 * DEEP), jnp.float32),
             pltpu.VMEM((count, 3 * DEEP), jnp.float32),
             pltpu.VMEM((2 * count, 3 * DEEP), jnp.bfloat16),
             pltpu.VMEM((2 * count, 3 * DEEP), jnp.bfloat16),
@@ -109,27 +114,24 @@
             pltpu.VMEM((total, count, LANES), jnp.float32),
             pltpu.VMEM((total, 2 * LANES, 2 * LANES), jnp.bfloat16),
             pltpu.VMEM((total, 2 * LANES, 2 * LANES), jnp.bfloat16),
-            pltpu.SemaphoreType.DMA((6,)),
         ],
         compiler_params=PARAMS,
         name="propagate",
-    )(turn, rows, *tables, *sides)
+    )(turn, odd, in_vmem(rows), *map(in_vmem, tables), *map(in_vmem, sides))
 
 
 def source_kernel(starts, step, arrived, quad, strength, turn, blocks, turned, *refs):
-    ins, outs, (field, rounded, total, flags) = refs[:arrived], refs[arrived:-4], refs[-4:]
+    ins, outs, (field, rounded, total) = refs[:arrived], refs[arrived:-3], refs[-3:]
     peers = len(outs)
     row_count = field.shape[0] // peers
-    pairs = []
     for m, group in enumerate(starts):
         base = lax.rem(turn[0] + peers - m, peers) * row_count
         for offset, ref in zip(group, ins[m * len(group) : (m + 1) * len(group)]):
-            pairs.append((ref, field.at[pl.ds(pl.multiple_of(base + offset, 8), ref.shape[0]), :]))
-    for copy in copy_all(pairs, flags):
-        copy.wait()
-    values = field[...]
-    total[...] = values
-    rounded[...] = values.astype(jnp.bfloat16)
+            rows = pl.ds(pl.multiple_of(base + offset, 16), ref.shape[0])
+            values = ref[...]
+            field[rows, :] = values
+            total[rows, :] = values
+            rounded[rows, :] = values.astype(jnp.bfloat16)
 
     def rows_of(f):
         return pl.ds(pl.multiple_of(f * ND, ND), ND)
@@ -149,40 +151,35 @@
         return carry
 
     lax.fori_loop(0, blocks.shape[0] // step, some, 0)
-    pairs = []
     for m, out in enumerate(outs):
         base = lax.rem(turn[0] + m, peers) * row_count
-        pairs.append((total.at[pl.ds(pl.multiple_of(base, 8), row_count), :], out))
-    for copy in copy_all(pairs, flags):
-        copy.wait()
+        out[...] = total[pl.ds(pl.multiple_of(base, 8), row_count), :]
 
 
 def source_term(turn, pieces, starts, quad_index, strength, blocks, turned, peers):
     columns = pieces[0].shape[1]
     row_count = NF * ND // peers
-    step = math.gcd(blocks.shape[0], 8)
+    step = math.gcd(blocks.shape[0], 16)
     return pl.pallas_call(
         functools.partial(source_kernel, starts, step, len(pieces)),
-        out_shape=[jax.ShapeDtypeStruct((row_count, columns), jnp.float32)] * peers,
-        in_specs=[SMEM] * 3 + [VMEM] * 2 + [ANY] * len(pieces),
-        out_specs=[ANY] * peers,
+        out_shape=[pltpu.VMEM((row_count, columns), jnp.float32)] * peers,
+        in_specs=[SMEM] * 3 + [VMEM] * (2 + len(pieces)),
+        out_specs=[VMEM] * peers,
         scratch_shapes=[
             pltpu.VMEM((NF * ND, columns), jnp.float32),
             pltpu.VMEM((NF * ND, columns), jnp.bfloat16),
             pltpu.VMEM((NF * ND, columns), jnp.float32),
-            pltpu.SemaphoreType.DMA((max(len(pieces), peers),)),
         ],
         compiler_params=PARAMS,
         name="source",
-    )(quad_index, strength, turn, blocks, turned, *pieces)
+    )(quad_index, strength, turn, in_vmem(blocks), in_vmem(turned), *map(in_vmem, pieces))
 
 
 def gather_kernel(turn, *refs):
-    ins, out, flags = refs[:-2], refs[-2], refs[-1]
+    ins, out = refs[:-1], refs[-1]
     peers = len(ins)
-    pairs = [(ref, out.at[:, lane_tile(lax.rem(turn[0] + peers - m, peers))]) for m, ref in enumerate(ins)]
-    for copy in copy_all(pairs, flags):
-        copy.wait()
+    for m, ref in enumerate(ins):
+        out[:, lane_tile(lax.rem(turn[0] + peers - m, peers))] = ref[...]
 
 
 def gather_columns(turn, pieces):
@@ -190,12 +187,11 @@
     return pl.pallas_call(
         gather_kernel,
         out_shape=jax.ShapeDtypeStruct((rows, columns * len(pieces)), jnp.float32),
-        in_specs=[SMEM] + [ANY] * len(pieces),
-        out_specs=ANY,
-        scratch_shapes=[pltpu.SemaphoreType.DMA((len(pieces),))],
+        in_specs=[SMEM] + [VMEM] * len(pieces),
+        out_specs=VMEM,
         compiler_params=PARAMS,
         name="columns",
-    )(turn, *pieces)
+    )(turn, *map(in_vmem, pieces))
 
 
 def from_sides(cells, width):
@@ -204,6 +200,16 @@
     before = lax.ppermute(tail, "space", [(i, i + 1) for i in range(count - 1)])
     after = lax.ppermute(head, "space", [(i + 1, i) for i in range(count - 1)])
     return before, after
+
+
+def from_pairs(cells):
+    count = lax.axis_size("space")
+    pairs = [[], []]
+    for i in range(count - 1):
+        pairs[i % 2] += [(i, i + 1), (i + 1, i)]
+    far = lax.ppermute(cells, "space", pairs[1])
+    near = lax.ppermute(cells, "space", pairs[0])
+    return near, cells, far
 
 
 def point_table(neighbours, current_east, current_north):
@@ -254,6 +260,7 @@
     row_count, columns = spectrum.shape
     own_index = lax.axis_index("comp").astype(jnp.int32)
     turn = own_index.reshape(1)
+    odd = lax.rem(lax.axis_index("space").astype(jnp.int32), 2).reshape(1)
     table = point_table(neighbours, current_east, current_north)
     rows = row_table(own_index * row_count, row_count, substeps, wave_speed)
     turned = blocks.swapaxes(1, 2)
@@ -267,17 +274,13 @@
                 chunk = jnp.concatenate([table, chunk])
             else:
                 chunk, *tables = lax.optimization_barrier((chunk, *tables))
-            before, after = from_sides(chunk, DEEP)
-            sides = (before, chunk, after)
+            sides = from_pairs(chunk)
             first = 0 if tables else 8
             tables = tables or sides
-            moved = propagate(turn, rows, tables, sides, first, low, high - low)
+            moved = propagate(turn, odd, rows, tables, sides, first, low, high - low)
             if sent[1]:
-                arrived = [group[-1] for group in sent[1:]]
-                held = lax.optimization_barrier((*moved, *arrived))
-                moved = held[:peers]
-                for group, piece in zip(sent[1:], held[peers:]):
-                    group[-1] = piece
+                arrived = [group[-1][:8] for group in sent[1:]]
+                moved = lax.optimization_barrier((*moved, *arrived))[:peers]
             for m in range(peers):
                 piece = moved[m]
                 if m:
@@ -302,7 +305,7 @@
     for start in range(0, columns, DEEP):
         sides = [wide[:, start + j * DEEP : start + (j + 1) * DEEP] for j in range(3)]
         tables = [table[:, start + j * DEEP : start + (j + 1) * DEEP] for j in range(3)]
-        tiles += propagate(still, rows, tables, sides, 0, 0, row_count + extra)
+        tiles += propagate(still, still + 1, rows, tables, sides, 0, 0, row_count + extra)
     grid = jnp.concatenate(tiles, axis=1)[:row_count].reshape(row_count, peers, columns // peers).swapaxes(0, 1)
     arrived = lax.all_to_all(grid, "comp", 0, 0, tiled=True)
     arrived = arrived.reshape(NF * ND, columns // peers)

time: 136 us -> 85.3 us (0.63)
  Pallas kernels: 60.8 us -> 18.2 us
  waiting for transfers between devices: 48.9 us -> 45.1 us
  starting transfers between devices: 18.8 us -> 16.1 us
  local copies, waits for them, and re-layouts: 5.82 us -> 4.38 us
    pallas_call x1, Pallas kernels: 36.9 us -> 1.17 us  [gather_columns(): pl.pallas_call(gather_kernel, out_shape=jax.ShapeDtypeStruct((rows, colum...]
    pallas_call x1, Pallas kernels: 6.87 us -> 2.94 us  [source_term(): pl.pallas_call(functools.partial(source_kernel, starts, step, len(pieces)...]
    ppermute x4, starting transfers between devices: 9.95 us -> 6.78 us  [the longest x2 6.04 us: from_pairs(): far = lax.ppermute(cells, 'space', pairs[1])]
    pallas_call x2, Pallas kernels: 17 us -> 14 us  [propagate(): pl.pallas_call(functools.partial(propagate_kernel, first, low), out_shape...]
    ppermute x9, waiting for transfers between devices: 39.5 us -> 36.8 us  [shards(): lax.ppermute(piece, 'comp', [(i, (i + m) % peers) for i in range(peers)])]
    unnamed x39 -> x27, local copies, waits for them, and re-layouts: 3.51 us -> 2.66 us
  transfers between devices with their start and end apart: 13 -> 13, of which waited for: 10 -> 7; matrix products, arithmetic and copies ran while one was open for 2% -> 1% of each run, Pallas kernels for 13% -> 16%
where the time goes in v3:
time: 85.3 us; the launch traced here: 85.1 us
  waiting for transfers between devices  45.1 us (53%)
  Pallas kernels  18.2 us (21%)
  starting transfers between devices  16.1 us (19%)
  local copies, waits for them, and re-layouts  4.38 us (5%)
  other arithmetic  1.08 us (1%)
    ppermute x9, waiting for transfers between devices, shards(): lax.ppermute(piece, 'comp', [(i, (i + m) % peers) for i in range(peers)])  36.8 us
    pallas_call x2, Pallas kernels, propagate(): pl.pallas_call(functools.partial(propagate_kernel, first, low), out_shape...  14 us
    ppermute x9, starting transfers between devices, shards(): lax.ppermute(piece, 'comp', [(i, (i + m) % peers) for i in range(peers)])  9.3 us
    ppermute x2, waiting for transfers between devices, from_pairs(): far = lax.ppermute(cells, 'space', pairs[1])  8.29 us
    ppermute x2, starting transfers between devices, from_pairs(): far = lax.ppermute(cells, 'space', pairs[1])  6.04 us
    pallas_call x1, Pallas kernels, source_term(): pl.pallas_call(functools.partial(source_kernel, starts, step, len(pieces)...  2.94 us
    unnamed x27, local copies, waits for them, and re-layouts  2.66 us
  transfers between devices with their start and end apart: 13, of which 7 were waited for; matrix products, arithmetic and copies ran while one was open for 1% of the time, Pallas kernels for 16%

profile of v3, /device:TPU:13, one launch (start us, length us, event | category | flops | bytes accessed | tf_op | source)
XLA Modules:
  0.0 85.1 jit_solution(15389464875695917038)
XLA Ops:
  0.0 0.9 %add_convert_fusion = (f32[1,512]{1,0:T(1,128)S(1)}, f32[1,512]{1,0:T(1,128)S(1)}, f32[1,512]{1,0:T(1,128)S(1)}, f32[1,512]{1,0:T(1,128)S(1)}) fusion(s32[4,512]{1,0:T(4,128)} %param.14), kind=kLoop, calls=%fused_computation.15 | loop fusion | flops 9728 | bytes 16384 | tf_op jit(solution)/shard_map/convert_element_type | solution.py:224
  0.9 0.0 copy-start.10
  0.9 0.0 copy-start.11
  0.9 1.3 %fusion.8 = (f32[288,512]{1,0:T(8,128)S(1)}, f32[288,512]{1,0:T(8,128)S(1)}) fusion(f32[576,512]{1,0:T(8,128)} %param.9), kind=kLoop, calls=%fused_computation.24 | loop fusion | bytes 2359296 | tf_op jit(solution)/shard_map/slice | solution.py:272
  2.2 0.0 copy-start.12
  2.2 0.0 copy-start.9
  2.3 0.0 copy-done.10
  2.3 0.2 concatenate.3.refs_1_.refs_4_
  2.5 0.7 collective-permute-start
  3.2 3.0 %collective-permute-start.1 = (f32[296,512]{1,0:T(8,128)S(1)}, f32[296,512]{1,0:T(8,128)S(1)}, u32[]{:S(2)}, u32[]{:S(2)}) collective-permute-start(f32[296,512]{1,0:T(8,128)S(1)} %concatenate.3.refs_1_.refs_4_), channel_id=1, source_target_pairs={{1,2},{2,1},{5,6},{6,5},{9,10},{10,9},{13,14},{14,13},{17,18},{18,... | collective-permute-start | bytes 1818632 | tf_op jit(solution)/shard_map/ppermute | solution.py:210
  6.3 0.0 collective-permute-done.refs_0_.refs_3_
  6.3 8.3 %collective-permute-done.1.refs_2_.refs_5_ = f32[296,512]{1,0:T(8,128)S(1)} collective-permute-done((f32[296,512]{1,0:T(8,128)S(1)}, f32[296,512]{1,0:T(8,128)S(1)}, u32[]{:S(2)}, u32[]{:S(2)}) %collective-permute-start.1) | collective-permute-done | bytes 606240 | tf_op jit(solution)/shard_map/ppermute | solution.py:210
  14.6 0.0 collective-permute-start.2
  14.6 3.0 %collective-permute-start.3 = (f32[288,512]{1,0:T(8,128)S(1)}, f32[288,512]{1,0:T(8,128)}, u32[]{:S(2)}, u32[]{:S(2)}) collective-permute-start(f32[288,512]{1,0:T(8,128)S(1)} %get-tuple-element.25.refs_4_), channel_id=1, source_target_pairs={{1,2},{2,1},{5,6},{6,5},{9,10},{10,9},{13,14},{14,13},{17,18},{18,... | collective-permute-start | bytes 1769480 | tf_op jit(solution)/shard_map/ppermute | solution.py:210
  17.6 0.1 broadcast_multiply_fusion
  17.7 0.1 mul.80
  17.8 0.1 mul.84
  17.9 0.1 fusion.2
  18.1 6.3 %propagate.2 = (f32[288,128]{1,0:T(8,128)S(1)}, f32[288,128]{1,0:T(8,128)S(1)}, f32[288,128]{1,0:T(8,128)}, f32[288,128]{1,0:T(8,128)}) custom-call(s32[1]{0:T(128)} %bitcast.turn, s32[1]{0:T(128)} %bitcast.2.odd, f32[8,640]{1,0:T(8,128)S(1)} %pad.4.rows, f32[296,512]{1,0:T(8,128)S(1)} %collective-permute-done.refs_0_.refs_3_, ...), custom_call_target="tpu_custom_call" | custom-call | tf_op jit(solution)/shard_map/propagate/pallas_call | solution.py:104
  24.4 0.7 copy-done.1
  25.1 1.3 %collective-permute-start.4 = (f32[288,128]{1,0:T(8,128)S(1)}, f32[288,128]{1,0:T(8,128)S(1)}, u32[]{:S(2)}, u32[]{:S(2)}) collective-permute-start(f32[288,128]{1,0:T(8,128)S(1)} %get-tuple-element.27), channel_id=1, source_target_pairs={{0,4},{4,8},{8,12},{12,0},{1,5},{5,9},{9,13},{13,1},{2,6},{6,10},{... | collective-permute-start | bytes 442376 | tf_op jit(solution)/shard_map/ppermute | solution.py:287
  26.4 1.0 %collective-permute-start.6 = (f32[288,128]{1,0:T(8,128)}, f32[288,128]{1,0:T(8,128)}, u32[]{:S(2)}, u32[]{:S(2)}) collective-permute-start(f32[288,128]{1,0:T(8,128)} %get-tuple-element.29), channel_id=1, source_target_pairs={{0,8},{4,12},{8,0},{12,4},{1,9},{5,13},{9,1},{13,5},{2,10},{6,14},... | collective-permute-start | bytes 442376 | tf_op jit(solution)/shard_map/ppermute | solution.py:287
  27.4 1.5 %collective-permute-start.8 = (f32[288,128]{1,0:T(8,128)}, f32[288,128]{1,0:T(8,128)}, u32[]{:S(2)}, u32[]{:S(2)}) collective-permute-start(f32[288,128]{1,0:T(8,128)} %get-tuple-element.31), channel_id=1, source_target_pairs={{0,12},{4,0},{8,4},{12,8},{1,13},{5,1},{9,5},{13,9},{2,14},{6,2},{... | collective-permute-start | bytes 442376 | tf_op jit(solution)/shard_map/ppermute | solution.py:287
  28.8 0.0 collective-permute-done.2.refs_3_
  28.8 0.0 collective-permute-done.3.refs_5_
  28.9 7.7 %propagate.3 = (f32[288,128]{1,0:T(8,128)S(1)}, f32[288,128]{1,0:T(8,128)}, f32[288,128]{1,0:T(8,128)}, f32[288,128]{1,0:T(8,128)}) custom-call(s32[1]{0:T(128)} %bitcast.turn, s32[1]{0:T(128)} %bitcast.2.odd, f32[8,640]{1,0:T(8,128)S(1)} %pad.4.rows, f32[296,512]{1,0:T(8,128)S(1)} %collective-permute-done.refs_0_.refs_3_, ...), custom_call_target="tpu_custom_call" | custom-call | tf_op jit(solution)/shard_map/propagate/pallas_call | solution.py:104
  36.6 0.6 copy-done.5
  37.2 0.1 collective-permute-start.5
  37.3 3.2 %collective-permute-start.7 = (f32[288,128]{1,0:T(8,128)}, f32[288,128]{1,0:T(8,128)S(1)}, u32[]{:S(2)}, u32[]{:S(2)}) collective-permute-start(f32[288,128]{1,0:T(8,128)} %get-tuple-element.30), channel_id=1, source_target_pairs={{0,8},{4,12},{8,0},{12,4},{1,9},{5,13},{9,1},{13,5},{2,10},{6,14},... | collective-permute-start | bytes 442376 | tf_op jit(solution)/shard_map/ppermute | solution.py:287
  40.4 0.0 collective-permute-done.4.refs_2_
  40.4 0.6 copy-done.3
  41.1 0.0 collective-permute-start.9
  41.1 0.7 copy.10
  41.8 0.0 collective-permute-done.6.refs_4_
  41.8 0.0 collective-permute-done.8.refs_6_
  41.8 1.3 %collective-permute-done.5.refs_3_ = f32[288,128]{1,0:T(8,128)S(1)} collective-permute-done((f32[288,128]{1,0:T(8,128)}, f32[288,128]{1,0:T(8,128)S(1)}, u32[]{:S(2)}, u32[]{:S(2)}) %collective-permute-start.5) | collective-permute-done | bytes 147488 | tf_op jit(solution)/shard_map/ppermute | solution.py:287
  43.1 8.6 %collective-permute-done.7.refs_5_ = f32[288,128]{1,0:T(8,128)S(1)} collective-permute-done((f32[288,128]{1,0:T(8,128)}, f32[288,128]{1,0:T(8,128)S(1)}, u32[]{:S(2)}, u32[]{:S(2)}) %collective-permute-start.7) | collective-permute-done | bytes 147488 | tf_op jit(solution)/shard_map/ppermute | solution.py:287
  51.7 1.9 %collective-permute-done.9.refs_7_ = f32[288,128]{1,0:T(8,128)S(1)} collective-permute-done((f32[288,128]{1,0:T(8,128)}, f32[288,128]{1,0:T(8,128)S(1)}, u32[]{:S(2)}, u32[]{:S(2)}) %collective-permute-start.9) | collective-permute-done | bytes 147488 | tf_op jit(solution)/shard_map/ppermute | solution.py:287
  53.6 0.0 copy-done.6
  53.6 0.0 copy-done.4
  53.6 2.9 %source.1 = (f32[576,128]{1,0:T(8,128)S(1)}, f32[576,128]{1,0:T(8,128)S(1)}, f32[576,128]{1,0:T(8,128)S(1)}, f32[576,128]{1,0:T(8,128)S(1)}) custom-call(s32[4,64]{1,0:T(4,128)S(1)} %copy-done.7, f32[64]{0:T(128)S(1)} %copy-done.8, s32[1]{0:T(128)} %bitcast.turn, bf16[64,64,64]{2,1,0:T(8,128)(2,1)S(1)} %copy-done, bf16[64,64,64]{2,1,0:T(8,128)(2,1)S(1)} %bitcast.5, ...), custom_call_target="tpu_custom_call" | custom-call | tf_op jit(solution)/shard_map/source/pallas_call | solution.py:163
  56.6 0.1 collective-permute-start.10
  56.6 0.9 %collective-permute-start.11 = (f32[576,128]{1,0:T(8,128)S(1)}, f32[576,128]{1,0:T(8,128)S(1)}, u32[]{:S(2)}, u32[]{:S(2)}) collective-permute-start(f32[576,128]{1,0:T(8,128)S(1)} %get-tuple-element.35), channel_id=1, source_target_pairs={{0,8},{4,12},{8,0},{12,4},{1,9},{5,13},{9,1},{13,5},{2,10},{6,14},... | collective-permute-start | bytes 884744 | tf_op jit(solution)/shard_map/ppermute | solution.py:293
  57.5 1.4 %collective-permute-start.12 = (f32[576,128]{1,0:T(8,128)S(1)}, f32[576,128]{1,0:T(8,128)S(1)}, u32[]{:S(2)}, u32[]{:S(2)}) collective-permute-start(f32[576,128]{1,0:T(8,128)S(1)} %get-tuple-element.36), channel_id=1, source_target_pairs={{0,12},{4,0},{8,4},{12,8},{1,13},{5,1},{9,5},{13,9},{2,14},{6,2},{... | collective-permute-start | bytes 884744 | tf_op jit(solution)/shard_map/ppermute | solution.py:293
  58.9 5.4 %collective-permute-done.10.refs_1_ = f32[576,128]{1,0:T(8,128)S(1)} collective-permute-done((f32[576,128]{1,0:T(8,128)S(1)}, f32[576,128]{1,0:T(8,128)S(1)}, u32[]{:S(2)}, u32[]{:S(2)}) %collective-permute-start.10) | collective-permute-done | bytes 294944 | tf_op jit(solution)/shard_map/ppermute | solution.py:293
  64.3 17.1 %collective-permute-done.11.refs_2_ = f32[576,128]{1,0:T(8,128)S(1)} collective-permute-done((f32[576,128]{1,0:T(8,128)S(1)}, f32[576,128]{1,0:T(8,128)S(1)}, u32[]{:S(2)}, u32[]{:S(2)}) %collective-permute-start.11) | collective-permute-done | bytes 294944 | tf_op jit(solution)/shard_map/ppermute | solution.py:293
  81.4 2.5 %collective-permute-done.12.refs_3_ = f32[576,128]{1,0:T(8,128)S(1)} collective-permute-done((f32[576,128]{1,0:T(8,128)S(1)}, f32[576,128]{1,0:T(8,128)S(1)}, u32[]{:S(2)}, u32[]{:S(2)}) %collective-permute-start.12) | collective-permute-done | bytes 294944 | tf_op jit(solution)/shard_map/ppermute | solution.py:293
  83.9 1.2 %columns.1 = f32[576,512]{1,0:T(8,128)} custom-call(s32[1]{0:T(128)} %bitcast.turn, f32[576,128]{1,0:T(8,128)S(1)} %get-tuple-element.33.refs_0_, f32[576,128]{1,0:T(8,128)S(1)} %collective-permute-done.10.refs_1_, f32[576,128]{1,0:T(8,128)S(1)} %collective-permute-done.11.refs_2_, f32[576,128]{1,0:T(8,128)S(1)} %collective-permute-done.12.refs_3_), custom_call_target="tpu_custom_call" | custom-call | tf_op jit(solution)/shard_map/columns/pallas_call | solution.py:187
  (26 shorter events, 0.1 us)
Async XLA Ops:
  0.9 1.4 %copy-start.10 = (f32[512]{0:T(512)S(1)}, f32[512]{0:T(512)}, u32[]{:S(2)}) copy-start(f32[512]{0:T(512)} %param.11) | copy-start | bytes 6148
  0.9 1.4 %copy-start.11 = (f32[512]{0:T(512)S(1)}, f32[512]{0:T(512)}, u32[]{:S(2)}) copy-start(f32[512]{0:T(512)} %param.12) | copy-start | bytes 6148
  2.2 15.4 %copy-start.12 = (f32[36]{0:T(128)S(1)}, f32[36]{0:T(128)}, u32[]{:S(2)}) copy-start(f32[36]{0:T(128)} %param.10) | copy-start | bytes 436
  2.2 15.6 %copy-start.9 = (s32[2304]{0:T(1024)S(1)}, s32[2304]{0:T(1024)}, u32[]{:S(2)}) copy-start(s32[2304]{0:T(1024)} %param.13) | copy-start | bytes 27652
  2.5 3.8 %collective-permute-start = (f32[296,512]{1,0:T(8,128)S(1)}, f32[296,512]{1,0:T(8,128)S(1)}, u32[]{:S(2)}, u32[]{:S(2)}) collective-permute-start(f32[296,512]{1,0:T(8,128)S(1)} %concatenate.3.refs_1_.refs_4_), channel_id=1, source_target_pairs={{0,1},{1,0},{2,3},{3,2},{4,5},{5,4},{6,7},{7,6},{8,9},{9,8},{10,11... | collective-permute-start | bytes 1818632 | tf_op jit(solution)/shard_map/ppermute | solution.py:211
  3.2 11.4 %collective-permute-start.1 = (f32[296,512]{1,0:T(8,128)S(1)}, f32[296,512]{1,0:T(8,128)S(1)}, u32[]{:S(2)}, u32[]{:S(2)}) collective-permute-start(f32[296,512]{1,0:T(8,128)S(1)} %concatenate.3.refs_1_.refs_4_), channel_id=1, source_target_pairs={{1,2},{2,1},{5,6},{6,5},{9,10},{10,9},{13,14},{14,13},{17,18},{18,... | collective-permute-start | bytes 1818632 | tf_op jit(solution)/shard_map/ppermute | solution.py:210
  14.6 14.3 %collective-permute-start.2 = (f32[288,512]{1,0:T(8,128)S(1)}, f32[288,512]{1,0:T(8,128)}, u32[]{:S(2)}, u32[]{:S(2)}) collective-permute-start(f32[288,512]{1,0:T(8,128)S(1)} %get-tuple-element.25.refs_4_), channel_id=1, source_target_pairs={{0,1},{1,0},{2,3},{3,2},{4,5},{5,4},{6,7},{7,6},{8,9},{9,8},{10,11... | collective-permute-start | bytes 1769480 | tf_op jit(solution)/shard_map/ppermute | solution.py:211
  14.6 14.3 %collective-permute-start.3 = (f32[288,512]{1,0:T(8,128)S(1)}, f32[288,512]{1,0:T(8,128)}, u32[]{:S(2)}, u32[]{:S(2)}) collective-permute-start(f32[288,512]{1,0:T(8,128)S(1)} %get-tuple-element.25.refs_4_), channel_id=1, source_target_pairs={{1,2},{2,1},{5,6},{6,5},{9,10},{10,9},{13,14},{14,13},{17,18},{18,... | collective-permute-start | bytes 1769480 | tf_op jit(solution)/shard_map/ppermute | solution.py:210
  24.4 0.7 copy-start.1
  25.1 15.4 %collective-permute-start.4 = (f32[288,128]{1,0:T(8,128)S(1)}, f32[288,128]{1,0:T(8,128)S(1)}, u32[]{:S(2)}, u32[]{:S(2)}) collective-permute-start(f32[288,128]{1,0:T(8,128)S(1)} %get-tuple-element.27), channel_id=1, source_target_pairs={{0,4},{4,8},{8,12},{12,0},{1,5},{5,9},{9,13},{13,1},{2,6},{6,10},{... | collective-permute-start | bytes 442376 | tf_op jit(solution)/shard_map/ppermute | solution.py:287
  26.4 15.4 %collective-permute-start.6 = (f32[288,128]{1,0:T(8,128)}, f32[288,128]{1,0:T(8,128)}, u32[]{:S(2)}, u32[]{:S(2)}) collective-permute-start(f32[288,128]{1,0:T(8,128)} %get-tuple-element.29), channel_id=1, source_target_pairs={{0,8},{4,12},{8,0},{12,4},{1,9},{5,13},{9,1},{13,5},{2,10},{6,14},... | collective-permute-start | bytes 442376 | tf_op jit(solution)/shard_map/ppermute | solution.py:287
  27.4 13.7 %copy-start = (bf16[64,64,64]{2,1,0:T(8,128)(2,1)S(1)}, bf16[64,64,64]{2,1,0:T(8,128)(2,1)}, u32[]{:S(2)}) copy-start(bf16[64,64,64]{2,1,0:T(8,128)(2,1)} %blocks.1) | copy-start | bytes 1572868
  27.4 14.4 %collective-permute-start.8 = (f32[288,128]{1,0:T(8,128)}, f32[288,128]{1,0:T(8,128)}, u32[]{:S(2)}, u32[]{:S(2)}) collective-permute-start(f32[288,128]{1,0:T(8,128)} %get-tuple-element.31), channel_id=1, source_target_pairs={{0,12},{4,0},{8,4},{12,8},{1,13},{5,1},{9,5},{13,9},{2,14},{6,2},{... | collective-permute-start | bytes 442376 | tf_op jit(solution)/shard_map/ppermute | solution.py:287
  36.5 0.7 copy-start.5
  37.2 16.4 %copy-start.2 = (f32[288,128]{1,0:T(8,128)S(1)}, f32[288,128]{1,0:T(8,128)}, u32[]{:S(2)}) copy-start(f32[288,128]{1,0:T(8,128)} %copy-done.1) | copy-start | bytes 442372
  37.2 16.4 %copy-start.7 = (s32[4,64]{1,0:T(4,128)S(1)}, s32[4,64]{1,0:T(4,128)}, u32[]{:S(2)}) copy-start(s32[4,64]{1,0:T(4,128)} %quad.1) | copy-start | bytes 3076
  37.2 16.4 %copy-start.8 = (f32[64]{0:T(128)S(1)}, f32[64]{0:T(128)}, u32[]{:S(2)}) copy-start(f32[64]{0:T(128)} %strength.1) | copy-start | bytes 772
  37.2 16.4 %copy-start.6 = (f32[288,128]{1,0:T(8,128)S(1)}, f32[288,128]{1,0:T(8,128)}, u32[]{:S(2)}) copy-start(f32[288,128]{1,0:T(8,128)} %copy-done.5) | copy-start | bytes 442372
  37.2 5.9 %collective-permute-start.5 = (f32[288,128]{1,0:T(8,128)}, f32[288,128]{1,0:T(8,128)S(1)}, u32[]{:S(2)}, u32[]{:S(2)}) collective-permute-start(f32[288,128]{1,0:T(8,128)} %get-tuple-element.28), channel_id=1, source_target_pairs={{0,4},{4,8},{8,12},{12,0},{1,5},{5,9},{9,13},{13,1},{2,6},{6,10},{... | collective-permute-start | bytes 442376 | tf_op jit(solution)/shard_map/ppermute | solution.py:287
  37.3 14.4 %collective-permute-start.7 = (f32[288,128]{1,0:T(8,128)}, f32[288,128]{1,0:T(8,128)S(1)}, u32[]{:S(2)}, u32[]{:S(2)}) collective-permute-start(f32[288,128]{1,0:T(8,128)} %get-tuple-element.30), channel_id=1, source_target_pairs={{0,8},{4,12},{8,0},{12,4},{1,9},{5,13},{9,1},{13,5},{2,10},{6,14},... | collective-permute-start | bytes 442376 | tf_op jit(solution)/shard_map/ppermute | solution.py:287
  40.4 0.6 copy-start.3
  41.1 12.5 %copy-start.4 = (f32[288,128]{1,0:T(8,128)S(1)}, f32[288,128]{1,0:T(8,128)}, u32[]{:S(2)}) copy-start(f32[288,128]{1,0:T(8,128)} %copy-done.3) | copy-start | bytes 442372
  41.1 12.5 %collective-permute-start.9 = (f32[288,128]{1,0:T(8,128)}, f32[288,128]{1,0:T(8,128)S(1)}, u32[]{:S(2)}, u32[]{:S(2)}) collective-permute-start(f32[288,128]{1,0:T(8,128)} %get-tuple-element.32), channel_id=1, source_target_pairs={{0,12},{4,0},{8,4},{12,8},{1,13},{5,1},{9,5},{13,9},{2,14},{6,2},{... | collective-permute-start | bytes 442376 | tf_op jit(solution)/shard_map/ppermute | solution.py:287
  56.6 7.7 %collective-permute-start.10 = (f32[576,128]{1,0:T(8,128)S(1)}, f32[576,128]{1,0:T(8,128)S(1)}, u32[]{:S(2)}, u32[]{:S(2)}) collective-permute-start(f32[576,128]{1,0:T(8,128)S(1)} %get-tuple-element.34), channel_id=1, source_target_pairs={{0,4},{4,8},{8,12},{12,0},{1,5},{5,9},{9,13},{13,1},{2,6},{6,10},{... | collective-permute-start | bytes 884744 | tf_op jit(solution)/shard_map/ppermute | solution.py:293
  56.6 24.7 %collective-permute-start.11 = (f32[576,128]{1,0:T(8,128)S(1)}, f32[576,128]{1,0:T(8,128)S(1)}, u32[]{:S(2)}, u32[]{:S(2)}) collective-permute-start(f32[576,128]{1,0:T(8,128)S(1)} %get-tuple-element.35), channel_id=1, source_target_pairs={{0,8},{4,12},{8,0},{12,4},{1,9},{5,13},{9,1},{13,5},{2,10},{6,14},... | collective-permute-start | bytes 884744 | tf_op jit(solution)/shard_map/ppermute | solution.py:293
  57.5 26.4 %collective-permute-start.12 = (f32[576,128]{1,0:T(8,128)S(1)}, f32[576,128]{1,0:T(8,128)S(1)}, u32[]{:S(2)}, u32[]{:S(2)}) collective-permute-start(f32[576,128]{1,0:T(8,128)S(1)} %get-tuple-element.36), channel_id=1, source_target_pairs={{0,12},{4,0},{8,4},{12,8},{1,13},{5,1},{9,5},{13,9},{2,14},{6,2},{... | collective-permute-start | bytes 884744 | tf_op jit(solution)/shard_map/ppermute | solution.py:293

commit v4 on v3

--- a/solution.py
+++ b/solution.py
@@ -27,6 +27,10 @@
 
 def in_vmem(values):
     return pltpu.with_memory_space_constraint(values, pltpu.VMEM)
+
+
+def in_hbm(values):
+    return pltpu.with_memory_space_constraint(values, pltpu.HBM)
 
 
 def split(values):
@@ -103,7 +107,7 @@
     total = 3 * TILES
     return pl.pallas_call(
         functools.partial(propagate_kernel, first, low),
-        out_shape=[pltpu.VMEM((count, LANES), jnp.float32)] * TILES,
+        out_shape=[jax.ShapeDtypeStruct((count, LANES), jnp.float32)] + [pltpu.VMEM((count, LANES), jnp.float32)] * (TILES - 1),
         in_specs=[SMEM] * 2 + [VMEM] * 7,
         out_specs=[VMEM] * TILES,
         scratch_shapes=[
@@ -230,6 +234,35 @@
     )
 
 
+def pack_kernel(neighbours, east, north, cells, out):
+    columns = out.shape[1]
+    tile = lax.broadcasted_iota(jnp.int32, (4, columns), 1) // LANES * LANES
+    ahead = lax.broadcasted_iota(jnp.int32, (4, columns), 0) % 2 * LANES
+    out[0:4] = (neighbours[...] - tile - ahead).astype(jnp.float32)
+    out[4:5] = east[...].reshape(1, columns)
+    out[5:6] = north[...].reshape(1, columns)
+    out[6:8] = jnp.full((2, columns), courant_limit, jnp.float32)
+    out[8:] = cells[...]
+
+
+def pack(neighbours, east, north, spectrum, count):
+    columns = spectrum.shape[1]
+    return pl.pallas_call(
+        pack_kernel,
+        grid=(1,),
+        out_shape=pltpu.VMEM((8 + count, columns), jnp.float32),
+        in_specs=[
+            pl.BlockSpec((4, columns), lambda i: (0, 0)),
+            pl.BlockSpec((1, columns), lambda i: (0, 0)),
+            pl.BlockSpec((1, columns), lambda i: (0, 0)),
+            pl.BlockSpec((count, columns), lambda i: (0, 0)),
+        ],
+        out_specs=pl.BlockSpec((8 + count, columns), lambda i: (0, 0)),
+        compiler_params=PARAMS,
+        name="pack",
+    )(*map(in_hbm, (neighbours, east[None], north[None], spectrum)))
+
+
 def row_table(first_comp, row_count, substeps, wave_speed):
     angles = (jnp.arange(ND, dtype=jnp.float32) + 0.5) * (2.0 * math.pi / ND)
     inverse = courant_scale / substeps.astype(jnp.float32)
@@ -261,7 +294,6 @@
     own_index = lax.axis_index("comp").astype(jnp.int32)
     turn = own_index.reshape(1)
     odd = lax.rem(lax.axis_index("space").astype(jnp.int32), 2).reshape(1)
-    table = point_table(neighbours, current_east, current_north)
     rows = row_table(own_index * row_count, row_count, substeps, wave_speed)
     turned = blocks.swapaxes(1, 2)
     if columns == DEEP and peers == TILES and row_count % 16 == 0:
@@ -269,18 +301,15 @@
         sent = [[] for _ in range(peers)]
         tables, moved = None, None
         for low, high in cuts:
-            chunk = spectrum[low:high]
             if tables is None:
-                chunk = jnp.concatenate([table, chunk])
+                chunk = pack(neighbours, current_east, current_north, spectrum, high)
             else:
-                chunk, *tables = lax.optimization_barrier((chunk, *tables))
+                chunk, near = lax.optimization_barrier((spectrum[low:high], tables[0]))
+                tables = (near, *tables[1:])
             sides = from_pairs(chunk)
             first = 0 if tables else 8
             tables = tables or sides
             moved = propagate(turn, odd, rows, tables, sides, first, low, high - low)
-            if sent[1]:
-                arrived = [group[-1][:8] for group in sent[1:]]
-                moved = lax.optimization_barrier((*moved, *arrived))[:peers]
             for m in range(peers):
                 piece = moved[m]
                 if m:
@@ -299,6 +328,7 @@
     chunk = jnp.pad(spectrum, ((0, extra), (0, 0)))
     before, after = from_sides(chunk, DEEP)
     wide = jnp.concatenate([before, chunk, after], axis=1)
+    table = point_table(neighbours, current_east, current_north)
     before, after = from_sides(table, DEEP)
     table = jnp.concatenate([before, table, after], axis=1)
     tiles = []

time: 85.3 us -> 75.4 us (0.88)
  waiting for transfers between devices: 45.1 us -> 37.6 us
  local copies, waits for them, and re-layouts: 4.38 us -> 2.22 us
  Pallas kernels: 18.2 us -> 19.5 us
    ppermute x9, waiting for transfers between devices: 36.8 us -> 32.5 us  [shards(): lax.ppermute(piece, 'comp', [(i, (i + m) % peers) for i in range(peers)])]
    ppermute x2, waiting for transfers between devices: 8.29 us -> 5.17 us  [from_pairs(): far = lax.ppermute(cells, 'space', pairs[1])]
    slice x1, local copies, waits for them, and re-layouts: 1.33 us -> 0.04 us  [shards(): chunk, near = lax.optimization_barrier((spectrum[low:high], tables[0]))]
    pallas_call x0 -> x1, Pallas kernels: none -> 1.25 us  [pack(): pl.pallas_call(pack_kernel, grid=(1,), out_shape=pltpu.VMEM((8 + count, c...]
    convert_element_type x1 -> x0, other arithmetic: 0.86 us -> none  [point_table(): (north - tile - LANES).astype(jnp.float32)]
    unnamed x27 -> x25, local copies, waits for them, and re-layouts: 2.66 us -> 2 us
  transfers between devices with their start and end apart: 13 -> 13, of which waited for: 7 -> 7; matrix products, arithmetic and copies ran while one was open for 1% -> 1% of each run, Pallas kernels for 16% -> 19%
where the time goes in v4:
time: 75.4 us; the launch traced here: 75.2 us
  waiting for transfers between devices  37.6 us (50%)
  Pallas kernels  19.5 us (26%)
  starting transfers between devices  15.5 us (21%)
  local copies, waits for them, and re-layouts  2.22 us (3%)
    ppermute x9, waiting for transfers between devices, shards(): lax.ppermute(piece, 'comp', [(i, (i + m) % peers) for i in range(peers)])  32.5 us
    pallas_call x2, Pallas kernels, propagate(): pl.pallas_call(functools.partial(propagate_kernel, first, low), out_shape...  14.1 us
    ppermute x9, starting transfers between devices, shards(): lax.ppermute(piece, 'comp', [(i, (i + m) % peers) for i in range(peers)])  9.1 us
    ppermute x2, starting transfers between devices, from_pairs(): far = lax.ppermute(cells, 'space', pairs[1])  5.55 us
    ppermute x2, waiting for transfers between devices, from_pairs(): far = lax.ppermute(cells, 'space', pairs[1])  5.17 us
    pallas_call x1, Pallas kernels, source_term(): pl.pallas_call(functools.partial(source_kernel, starts, step, len(pieces)...  2.95 us
    unnamed x25, local copies, waits for them, and re-layouts  2 us
  transfers between devices with their start and end apart: 13, of which 7 were waited for; matrix products, arithmetic and copies ran while one was open for 1% of the time, Pallas kernels for 19%

profile of v4, /device:TPU:13, one launch (start us, length us, event | category | flops | bytes accessed | tf_op | source)
XLA Modules:
  0.0 75.2 jit_solution(16788766839179262779)
XLA Ops:
  0.0 1.3 %pack.1.refs_1_.refs_4_ = f32[296,512]{1,0:T(8,128)S(1)} custom-call(s32[4,512]{1,0:T(4,128)} %neighbours.1, f32[1,512]{1,0:T(1,128)} %bitcast.6, f32[1,512]{1,0:T(1,128)} %bitcast.7, f32[576,512]{1,0:T(8,128)} %cells.1), custom_call_target="tpu_custom_call" | custom-call | tf_op jit(solution)/shard_map/pack/pallas_call | solution.py:250
  1.3 0.7 collective-permute-start
  2.0 3.0 %collective-permute-start.1 = (f32[296,512]{1,0:T(8,128)S(1)}, f32[296,512]{1,0:T(8,128)S(1)}, u32[]{:S(2)}, u32[]{:S(2)}) collective-permute-start(f32[296,512]{1,0:T(8,128)S(1)} %pack.1.refs_1_.refs_4_), channel_id=1, source_target_pairs={{1,2},{2,1},{5,6},{6,5},{9,10},{10,9},{13,14},{14,13},{17,18},{18,... | collective-permute-start | bytes 1818632 | tf_op jit(solution)/shard_map/ppermute | solution.py:214
  5.1 0.0 copy-done.9
  5.1 0.0 collective-permute-done.refs_0_.refs_3_
  5.1 0.1 collective-permute-start.2
  5.2 2.5 %collective-permute-start.3 = (f32[288,512]{1,0:T(8,128)S(1)}, f32[288,512]{1,0:T(8,128)}, u32[]{:S(2)}, u32[]{:S(2)}) collective-permute-start(f32[288,512]{1,0:T(8,128)S(1)} %slice.3.refs_4_), channel_id=1, source_target_pairs={{1,2},{2,1},{5,6},{6,5},{9,10},{10,9},{13,14},{14,13},{17,18},{18,... | collective-permute-start | bytes 1769480 | tf_op jit(solution)/shard_map/ppermute | solution.py:214
  7.8 0.0 copy-done.11
  7.8 0.1 broadcast_multiply_fusion
  7.9 0.1 mul.61
  7.9 0.1 mul.65
  8.0 0.0 copy-done.10
  8.1 0.1 fusion.2
  8.2 5.2 %collective-permute-done.1.refs_2_.refs_5_ = f32[296,512]{1,0:T(8,128)S(1)} collective-permute-done((f32[296,512]{1,0:T(8,128)S(1)}, f32[296,512]{1,0:T(8,128)S(1)}, u32[]{:S(2)}, u32[]{:S(2)}) %collective-permute-start.1) | collective-permute-done | bytes 606240 | tf_op jit(solution)/shard_map/ppermute | solution.py:214
  13.4 6.4 %propagate.2 = (f32[288,128]{1,0:T(8,128)S(1)}, f32[288,128]{1,0:T(8,128)S(1)}, f32[288,128]{1,0:T(8,128)}, f32[288,128]{1,0:T(8,128)}) custom-call(s32[1]{0:T(128)} %bitcast.turn, s32[1]{0:T(128)} %bitcast.2.odd, f32[8,640]{1,0:T(8,128)S(1)} %pad.4.rows, f32[296,512]{1,0:T(8,128)S(1)} %collective-permute-done.refs_0_.refs_3_, ...), custom_call_target="tpu_custom_call" | custom-call | tf_op jit(solution)/shard_map/propagate/pallas_call | solution.py:108
  19.7 1.3 %collective-permute-start.4 = (f32[288,128]{1,0:T(8,128)S(1)}, f32[288,128]{1,0:T(8,128)S(1)}, u32[]{:S(2)}, u32[]{:S(2)}) collective-permute-start(f32[288,128]{1,0:T(8,128)S(1)} %get-tuple-element.23), channel_id=1, source_target_pairs={{0,4},{4,8},{8,12},{12,0},{1,5},{5,9},{9,13},{13,1},{2,6},{6,10},{... | collective-permute-start | bytes 442376 | tf_op jit(solution)/shard_map/ppermute | solution.py:316
  21.0 1.0 %collective-permute-start.6 = (f32[288,128]{1,0:T(8,128)}, f32[288,128]{1,0:T(8,128)}, u32[]{:S(2)}, u32[]{:S(2)}) collective-permute-start(f32[288,128]{1,0:T(8,128)} %get-tuple-element.25), channel_id=1, source_target_pairs={{0,8},{4,12},{8,0},{12,4},{1,9},{5,13},{9,1},{13,5},{2,10},{6,14},... | collective-permute-start | bytes 442376 | tf_op jit(solution)/shard_map/ppermute | solution.py:316
  22.1 1.5 %collective-permute-start.8 = (f32[288,128]{1,0:T(8,128)}, f32[288,128]{1,0:T(8,128)}, u32[]{:S(2)}, u32[]{:S(2)}) collective-permute-start(f32[288,128]{1,0:T(8,128)} %get-tuple-element.27), channel_id=1, source_target_pairs={{0,12},{4,0},{8,4},{12,8},{1,13},{5,1},{9,5},{13,9},{2,14},{6,2},{... | collective-permute-start | bytes 442376 | tf_op jit(solution)/shard_map/ppermute | solution.py:316
  23.5 0.0 collective-permute-done.2.refs_3_
  23.5 0.0 collective-permute-done.3.refs_5_
  23.5 7.7 %propagate.3 = (f32[288,128]{1,0:T(8,128)S(1)}, f32[288,128]{1,0:T(8,128)}, f32[288,128]{1,0:T(8,128)}, f32[288,128]{1,0:T(8,128)}) custom-call(s32[1]{0:T(128)} %bitcast.turn, s32[1]{0:T(128)} %bitcast.2.odd, f32[8,640]{1,0:T(8,128)S(1)} %pad.4.rows, f32[296,512]{1,0:T(8,128)S(1)} %collective-permute-done.refs_0_.refs_3_, ...), custom_call_target="tpu_custom_call" | custom-call | tf_op jit(solution)/shard_map/propagate/pallas_call | solution.py:108
  31.2 0.0 copy-done.1
  31.2 0.7 copy-done.5
  31.9 0.1 collective-permute-start.5
  32.0 3.1 %collective-permute-start.7 = (f32[288,128]{1,0:T(8,128)}, f32[288,128]{1,0:T(8,128)S(1)}, u32[]{:S(2)}, u32[]{:S(2)}) collective-permute-start(f32[288,128]{1,0:T(8,128)} %get-tuple-element.26), channel_id=1, source_target_pairs={{0,8},{4,12},{8,0},{12,4},{1,9},{5,13},{9,1},{13,5},{2,10},{6,14},... | collective-permute-start | bytes 442376 | tf_op jit(solution)/shard_map/ppermute | solution.py:316
  35.1 0.0 collective-permute-done.4.refs_2_
  35.1 0.7 copy-done.3
  35.8 0.0 collective-permute-start.9
  35.8 0.0 copy-done
  35.8 0.7 copy.10
  36.4 0.0 collective-permute-done.6.refs_4_
  36.4 0.0 collective-permute-done.8.refs_6_
  36.5 4.2 %collective-permute-done.5.refs_3_ = f32[288,128]{1,0:T(8,128)S(1)} collective-permute-done((f32[288,128]{1,0:T(8,128)}, f32[288,128]{1,0:T(8,128)S(1)}, u32[]{:S(2)}, u32[]{:S(2)}) %collective-permute-start.5) | collective-permute-done | bytes 147488 | tf_op jit(solution)/shard_map/ppermute | solution.py:316
  40.6 1.6 %collective-permute-done.7.refs_5_ = f32[288,128]{1,0:T(8,128)S(1)} collective-permute-done((f32[288,128]{1,0:T(8,128)}, f32[288,128]{1,0:T(8,128)S(1)}, u32[]{:S(2)}, u32[]{:S(2)}) %collective-permute-start.7) | collective-permute-done | bytes 147488 | tf_op jit(solution)/shard_map/ppermute | solution.py:316
  42.2 2.1 %collective-permute-done.9.refs_7_ = f32[288,128]{1,0:T(8,128)S(1)} collective-permute-done((f32[288,128]{1,0:T(8,128)}, f32[288,128]{1,0:T(8,128)S(1)}, u32[]{:S(2)}, u32[]{:S(2)}) %collective-permute-start.9) | collective-permute-done | bytes 147488 | tf_op jit(solution)/shard_map/ppermute | solution.py:316
  44.3 0.0 copy-done.7
  44.3 0.0 copy-done.8
  44.3 0.0 copy-done.2
  44.3 0.0 copy-done.6
  44.3 0.0 copy-done.4
  44.3 2.9 %source.1 = (f32[576,128]{1,0:T(8,128)S(1)}, f32[576,128]{1,0:T(8,128)S(1)}, f32[576,128]{1,0:T(8,128)S(1)}, f32[576,128]{1,0:T(8,128)S(1)}) custom-call(s32[4,64]{1,0:T(4,128)S(1)} %copy-done.7, f32[64]{0:T(128)S(1)} %copy-done.8, s32[1]{0:T(128)} %bitcast.turn, bf16[64,64,64]{2,1,0:T(8,128)(2,1)S(1)} %copy-done, bf16[64,64,64]{2,1,0:T(8,128)(2,1)S(1)} %bitcast.5, ...), custom_call_target="tpu_custom_call" | custom-call | tf_op jit(solution)/shard_map/source/pallas_call | solution.py:167
  47.2 0.1 collective-permute-start.10
  47.3 1.2 %collective-permute-start.11 = (f32[576,128]{1,0:T(8,128)S(1)}, f32[576,128]{1,0:T(8,128)S(1)}, u32[]{:S(2)}, u32[]{:S(2)}) collective-permute-start(f32[576,128]{1,0:T(8,128)S(1)} %get-tuple-element.31), channel_id=1, source_target_pairs={{0,8},{4,12},{8,0},{12,4},{1,9},{5,13},{9,1},{13,5},{2,10},{6,14},... | collective-permute-start | bytes 884744 | tf_op jit(solution)/shard_map/ppermute | solution.py:322
  48.5 0.9 %collective-permute-start.12 = (f32[576,128]{1,0:T(8,128)S(1)}, f32[576,128]{1,0:T(8,128)S(1)}, u32[]{:S(2)}, u32[]{:S(2)}) collective-permute-start(f32[576,128]{1,0:T(8,128)S(1)} %get-tuple-element.32), channel_id=1, source_target_pairs={{0,12},{4,0},{8,4},{12,8},{1,13},{5,1},{9,5},{13,9},{2,14},{6,2},{... | collective-permute-start | bytes 884744 | tf_op jit(solution)/shard_map/ppermute | solution.py:322
  49.4 6.8 %collective-permute-done.10.refs_1_ = f32[576,128]{1,0:T(8,128)S(1)} collective-permute-done((f32[576,128]{1,0:T(8,128)S(1)}, f32[576,128]{1,0:T(8,128)S(1)}, u32[]{:S(2)}, u32[]{:S(2)}) %collective-permute-start.10) | collective-permute-done | bytes 294944 | tf_op jit(solution)/shard_map/ppermute | solution.py:322
  56.2 16.7 %collective-permute-done.11.refs_2_ = f32[576,128]{1,0:T(8,128)S(1)} collective-permute-done((f32[576,128]{1,0:T(8,128)S(1)}, f32[576,128]{1,0:T(8,128)S(1)}, u32[]{:S(2)}, u32[]{:S(2)}) %collective-permute-start.11) | collective-permute-done | bytes 294944 | tf_op jit(solution)/shard_map/ppermute | solution.py:322
  72.9 1.1 %collective-permute-done.12.refs_3_ = f32[576,128]{1,0:T(8,128)S(1)} collective-permute-done((f32[576,128]{1,0:T(8,128)S(1)}, f32[576,128]{1,0:T(8,128)S(1)}, u32[]{:S(2)}, u32[]{:S(2)}) %collective-permute-start.12) | collective-permute-done | bytes 294944 | tf_op jit(solution)/shard_map/ppermute | solution.py:322
  74.0 1.2 %columns.1 = f32[576,512]{1,0:T(8,128)} custom-call(s32[1]{0:T(128)} %bitcast.turn, f32[576,128]{1,0:T(8,128)S(1)} %get-tuple-element.29.refs_0_, f32[576,128]{1,0:T(8,128)S(1)} %collective-permute-done.10.refs_1_, f32[576,128]{1,0:T(8,128)S(1)} %collective-permute-done.11.refs_2_, f32[576,128]{1,0:T(8,128)S(1)} %collective-permute-done.12.refs_3_), custom_call_target="tpu_custom_call" | custom-call | tf_op jit(solution)/shard_map/columns/pallas_call | solution.py:191
  (21 shorter events, 0.2 us)
Async XLA Ops:
  0.0 5.1 %copy-start.9 = (f32[576,512]{1,0:T(8,128)S(1)}, f32[576,512]{1,0:T(8,128)}, u32[]{:S(2)}) copy-start(f32[576,512]{1,0:T(8,128)} %cells.1) | copy-start | bytes 3538948
  0.0 7.8 %copy-start.11 = (f32[36]{0:T(128)S(1)}, f32[36]{0:T(128)}, u32[]{:S(2)}) copy-start(f32[36]{0:T(128)} %param.10) | copy-start | bytes 436
  0.0 8.0 %copy-start.10 = (s32[2304]{0:T(1024)S(1)}, s32[2304]{0:T(1024)}, u32[]{:S(2)}) copy-start(s32[2304]{0:T(1024)} %param.13) | copy-start | bytes 27652
  1.3 3.9 %collective-permute-start = (f32[296,512]{1,0:T(8,128)S(1)}, f32[296,512]{1,0:T(8,128)S(1)}, u32[]{:S(2)}, u32[]{:S(2)}) collective-permute-start(f32[296,512]{1,0:T(8,128)S(1)} %pack.1.refs_1_.refs_4_), channel_id=1, source_target_pairs={{0,1},{1,0},{2,3},{3,2},{4,5},{5,4},{6,7},{7,6},{8,9},{9,8},{10,11... | collective-permute-start | bytes 1818632 | tf_op jit(solution)/shard_map/ppermute | solution.py:215
  2.0 11.4 %collective-permute-start.1 = (f32[296,512]{1,0:T(8,128)S(1)}, f32[296,512]{1,0:T(8,128)S(1)}, u32[]{:S(2)}, u32[]{:S(2)}) collective-permute-start(f32[296,512]{1,0:T(8,128)S(1)} %pack.1.refs_1_.refs_4_), channel_id=1, source_target_pairs={{1,2},{2,1},{5,6},{6,5},{9,10},{10,9},{13,14},{14,13},{17,18},{18,... | collective-permute-start | bytes 1818632 | tf_op jit(solution)/shard_map/ppermute | solution.py:214
  5.1 18.4 %collective-permute-start.2 = (f32[288,512]{1,0:T(8,128)S(1)}, f32[288,512]{1,0:T(8,128)}, u32[]{:S(2)}, u32[]{:S(2)}) collective-permute-start(f32[288,512]{1,0:T(8,128)S(1)} %slice.3.refs_4_), channel_id=1, source_target_pairs={{0,1},{1,0},{2,3},{3,2},{4,5},{5,4},{6,7},{7,6},{8,9},{9,8},{10,11... | collective-permute-start | bytes 1769480 | tf_op jit(solution)/shard_map/ppermute | solution.py:215
  5.2 18.3 %collective-permute-start.3 = (f32[288,512]{1,0:T(8,128)S(1)}, f32[288,512]{1,0:T(8,128)}, u32[]{:S(2)}, u32[]{:S(2)}) collective-permute-start(f32[288,512]{1,0:T(8,128)S(1)} %slice.3.refs_4_), channel_id=1, source_target_pairs={{1,2},{2,1},{5,6},{6,5},{9,10},{10,9},{13,14},{14,13},{17,18},{18,... | collective-permute-start | bytes 1769480 | tf_op jit(solution)/shard_map/ppermute | solution.py:214
  19.7 11.5 %copy-start.1 = (f32[288,128]{1,0:T(8,128)}, f32[288,128]{1,0:T(8,128)S(1)}, u32[]{:S(2)}) copy-start(f32[288,128]{1,0:T(8,128)S(1)} %get-tuple-element.19.refs_0_) | copy-start | bytes 442372
  19.7 15.4 %collective-permute-start.4 = (f32[288,128]{1,0:T(8,128)S(1)}, f32[288,128]{1,0:T(8,128)S(1)}, u32[]{:S(2)}, u32[]{:S(2)}) collective-permute-start(f32[288,128]{1,0:T(8,128)S(1)} %get-tuple-element.23), channel_id=1, source_target_pairs={{0,4},{4,8},{8,12},{12,0},{1,5},{5,9},{9,13},{13,1},{2,6},{6,10},{... | collective-permute-start | bytes 442376 | tf_op jit(solution)/shard_map/ppermute | solution.py:316
  21.0 15.4 %collective-permute-start.6 = (f32[288,128]{1,0:T(8,128)}, f32[288,128]{1,0:T(8,128)}, u32[]{:S(2)}, u32[]{:S(2)}) collective-permute-start(f32[288,128]{1,0:T(8,128)} %get-tuple-element.25), channel_id=1, source_target_pairs={{0,8},{4,12},{8,0},{12,4},{1,9},{5,13},{9,1},{13,5},{2,10},{6,14},... | collective-permute-start | bytes 442376 | tf_op jit(solution)/shard_map/ppermute | solution.py:316
  22.1 13.7 %copy-start = (bf16[64,64,64]{2,1,0:T(8,128)(2,1)S(1)}, bf16[64,64,64]{2,1,0:T(8,128)(2,1)}, u32[]{:S(2)}) copy-start(bf16[64,64,64]{2,1,0:T(8,128)(2,1)} %blocks.1) | copy-start | bytes 1572868
  22.1 14.4 %collective-permute-start.8 = (f32[288,128]{1,0:T(8,128)}, f32[288,128]{1,0:T(8,128)}, u32[]{:S(2)}, u32[]{:S(2)}) collective-permute-start(f32[288,128]{1,0:T(8,128)} %get-tuple-element.27), channel_id=1, source_target_pairs={{0,12},{4,0},{8,4},{12,8},{1,13},{5,1},{9,5},{13,9},{2,14},{6,2},{... | collective-permute-start | bytes 442376 | tf_op jit(solution)/shard_map/ppermute | solution.py:316
  31.2 0.7 copy-start.5
  31.9 12.4 %copy-start.7 = (s32[4,64]{1,0:T(4,128)S(1)}, s32[4,64]{1,0:T(4,128)}, u32[]{:S(2)}) copy-start(s32[4,64]{1,0:T(4,128)} %quad.1) | copy-start | bytes 3076
  31.9 12.4 %copy-start.8 = (f32[64]{0:T(128)S(1)}, f32[64]{0:T(128)}, u32[]{:S(2)}) copy-start(f32[64]{0:T(128)} %strength.1) | copy-start | bytes 772
  31.9 12.4 %copy-start.2 = (f32[288,128]{1,0:T(8,128)S(1)}, f32[288,128]{1,0:T(8,128)}, u32[]{:S(2)}) copy-start(f32[288,128]{1,0:T(8,128)} %copy-done.1) | copy-start | bytes 442372
  31.9 12.4 %copy-start.6 = (f32[288,128]{1,0:T(8,128)S(1)}, f32[288,128]{1,0:T(8,128)}, u32[]{:S(2)}) copy-start(f32[288,128]{1,0:T(8,128)} %copy-done.5) | copy-start | bytes 442372
  31.9 8.7 %collective-permute-start.5 = (f32[288,128]{1,0:T(8,128)}, f32[288,128]{1,0:T(8,128)S(1)}, u32[]{:S(2)}, u32[]{:S(2)}) collective-permute-start(f32[288,128]{1,0:T(8,128)} %get-tuple-element.24), channel_id=1, source_target_pairs={{0,4},{4,8},{8,12},{12,0},{1,5},{5,9},{9,13},{13,1},{2,6},{6,10},{... | collective-permute-start | bytes 442376 | tf_op jit(solution)/shard_map/ppermute | solution.py:316
  32.0 10.2 %collective-permute-start.7 = (f32[288,128]{1,0:T(8,128)}, f32[288,128]{1,0:T(8,128)S(1)}, u32[]{:S(2)}, u32[]{:S(2)}) collective-permute-start(f32[288,128]{1,0:T(8,128)} %get-tuple-element.26), channel_id=1, source_target_pairs={{0,8},{4,12},{8,0},{12,4},{1,9},{5,13},{9,1},{13,5},{2,10},{6,14},... | collective-permute-start | bytes 442376 | tf_op jit(solution)/shard_map/ppermute | solution.py:316
  35.1 0.7 copy-start.3
  35.8 8.5 %copy-start.4 = (f32[288,128]{1,0:T(8,128)S(1)}, f32[288,128]{1,0:T(8,128)}, u32[]{:S(2)}) copy-start(f32[288,128]{1,0:T(8,128)} %copy-done.3) | copy-start | bytes 442372
  35.8 8.5 %collective-permute-start.9 = (f32[288,128]{1,0:T(8,128)}, f32[288,128]{1,0:T(8,128)S(1)}, u32[]{:S(2)}, u32[]{:S(2)}) collective-permute-start(f32[288,128]{1,0:T(8,128)} %get-tuple-element.28), channel_id=1, source_target_pairs={{0,12},{4,0},{8,4},{12,8},{1,13},{5,1},{9,5},{13,9},{2,14},{6,2},{... | collective-permute-start | bytes 442376 | tf_op jit(solution)/shard_map/ppermute | solution.py:316
  47.2 9.0 %collective-permute-start.10 = (f32[576,128]{1,0:T(8,128)S(1)}, f32[576,128]{1,0:T(8,128)S(1)}, u32[]{:S(2)}, u32[]{:S(2)}) collective-permute-start(f32[576,128]{1,0:T(8,128)S(1)} %get-tuple-element.30), channel_id=1, source_target_pairs={{0,4},{4,8},{8,12},{12,0},{1,5},{5,9},{9,13},{13,1},{2,6},{6,10},{... | collective-permute-start | bytes 884744 | tf_op jit(solution)/shard_map/ppermute | solution.py:322
  47.3 25.6 %collective-permute-start.11 = (f32[576,128]{1,0:T(8,128)S(1)}, f32[576,128]{1,0:T(8,128)S(1)}, u32[]{:S(2)}, u32[]{:S(2)}) collective-permute-start(f32[576,128]{1,0:T(8,128)S(1)} %get-tuple-element.31), channel_id=1, source_target_pairs={{0,8},{4,12},{8,0},{12,4},{1,9},{5,13},{9,1},{13,5},{2,10},{6,14},... | collective-permute-start | bytes 884744 | tf_op jit(solution)/shard_map/ppermute | solution.py:322
  48.5 25.6 %collective-permute-start.12 = (f32[576,128]{1,0:T(8,128)S(1)}, f32[576,128]{1,0:T(8,128)S(1)}, u32[]{:S(2)}, u32[]{:S(2)}) collective-permute-start(f32[576,128]{1,0:T(8,128)S(1)} %get-tuple-element.32), channel_id=1, source_target_pairs={{0,12},{4,0},{8,4},{12,8},{1,13},{5,1},{9,5},{13,9},{2,14},{6,2},{... | collective-permute-start | bytes 884744 | tf_op jit(solution)/shard_map/ppermute | solution.py:322

commit v5 on v4

--- a/solution.py
+++ b/solution.py
@@ -22,7 +22,7 @@
 
 VMEM = pl.BlockSpec(memory_space=pltpu.VMEM)
 SMEM = pl.BlockSpec(memory_space=pltpu.SMEM)
-PARAMS = pltpu.CompilerParams(vmem_limit_bytes=40 << 20)
+PARAMS = pltpu.CompilerParams(vmem_limit_bytes=24 << 20)
 
 
 def in_vmem(values):
@@ -45,8 +45,8 @@
 
 
 def propagate_kernel(first, low, turn, odd, rows, *refs):
-    tables, sides, outs = refs[:3], refs[3:6], refs[6 : 6 + TILES]
-    field, parts_a, parts_b, along_x, along_y, behind_pick, ahead_pick = refs[6 + TILES :]
+    table, sides, outs = refs[0], refs[1:4], refs[4 : 4 + TILES]
+    field, parts_a, parts_b, along_x, along_y, behind_pick, ahead_pick = refs[-7:]
     parts = (parts_a, parts_b)
     count = field.shape[0]
     total = 3 * TILES
@@ -67,15 +67,19 @@
         field[:, lane_tile(t)] = values
         parts_a[:count, lane_tile(t)], parts_a[count:, lane_tile(t)] = split(values)
         if 0 < t < total - 1:
-            table = region(tables, slice(0, 8), t)
+            near_table = table[:, lane_tile(t)]
             for pick, side in ((behind_pick, 0), (ahead_pick, 1)):
                 for d in range(2):
-                    chosen = position == table[2 * d + side : 2 * d + side + 1]
+                    chosen = position == near_table[2 * d + side : 2 * d + side + 1]
                     pick[t, :, lane_tile(d)] = jnp.where(chosen, 1.0, 0.0).astype(jnp.bfloat16)
-            limit = table[6:7]
-            along_x[t] = jnp.clip(east + inverse * table[4:5], -limit, limit)
-            along_y[t] = jnp.clip(north + inverse * table[5:6], -limit, limit)
-
+            limit = near_table[6:7]
+            along_x[t] = jnp.clip(east + inverse * near_table[4:5], -limit, limit)
+            along_y[t] = jnp.clip(north + inverse * near_table[5:6], -limit, limit)
+
+    if first:
+        table = refs[4 + TILES]
+        for t in range(total):
+            table[:, lane_tile(t)] = region(sides, slice(0, 8), t)
     prepare(0)
     prepare(1)
     for s in range(SUB):
@@ -103,13 +107,14 @@
         out[...] = field[:, lane_tile(lax.rem(turn[0] + m, TILES) + TILES)]
 
 
-def propagate(turn, odd, rows, tables, sides, first, low, count):
+def propagate(turn, odd, rows, table, sides, first, low, count):
     total = 3 * TILES
+    shapes = [(count, LANES)] * (TILES - 1) + [(8, 3 * DEEP)] * (first > 0)
     return pl.pallas_call(
         functools.partial(propagate_kernel, first, low),
-        out_shape=[jax.ShapeDtypeStruct((count, LANES), jnp.float32)] + [pltpu.VMEM((count, LANES), jnp.float32)] * (TILES - 1),
-        in_specs=[SMEM] * 2 + [VMEM] * 7,
-        out_specs=[VMEM] * TILES,
+        out_shape=[pltpu.HBM((count, LANES), jnp.float32)] + [pltpu.VMEM(shape, jnp.float32) for shape in shapes],
+        in_specs=[SMEM] * 2 + [VMEM] * 5,
+        out_specs=[VMEM] * (1 + len(shapes)),
         scratch_shapes=[
             pltpu.VMEM((count, 3 * DEEP), jnp.float32),
             pltpu.VMEM((2 * count, 3 * DEEP), jnp.bfloat16),
@@ -121,7 +126,7 @@
         ],
         compiler_params=PARAMS,
         name="propagate",
-    )(turn, odd, in_vmem(rows), *map(in_vmem, tables), *map(in_vmem, sides))
+    )(turn, odd, *map(in_vmem, (rows, table, *sides)))
 
 
 def source_kernel(starts, step, arrived, quad, strength, turn, blocks, turned, *refs):
@@ -263,6 +268,24 @@
     )(*map(in_hbm, (neighbours, east[None], north[None], spectrum)))
 
 
+def rows_kernel(low, cells, out, flag):
+    copy = pltpu.make_async_copy(cells.at[low : low + out.shape[0], :], out, flag)
+    copy.start()
+    copy.wait()
+
+
+def rows_from(spectrum, low, high):
+    return pl.pallas_call(
+        functools.partial(rows_kernel, low),
+        out_shape=pltpu.VMEM((high - low, spectrum.shape[1]), jnp.float32),
+        in_specs=[pl.BlockSpec(memory_space=pl.ANY)],
+        out_specs=VMEM,
+        scratch_shapes=[pltpu.SemaphoreType.DMA],
+        compiler_params=PARAMS,
+        name="rest",
+    )(in_hbm(spectrum))
+
+
 def row_table(first_comp, row_count, substeps, wave_speed):
     angles = (jnp.arange(ND, dtype=jnp.float32) + 0.5) * (2.0 * math.pi / ND)
     inverse = courant_scale / substeps.astype(jnp.float32)
@@ -274,7 +297,7 @@
 
 
 def cuts_of(row_count):
-    middle = row_count // 2 // 16 * 16
+    middle = row_count * 5 // 8 // 32 * 32
     return [(0, middle), (middle, row_count)]
 
 
@@ -299,17 +322,17 @@
     if columns == DEEP and peers == TILES and row_count % 16 == 0:
         cuts = cuts_of(row_count)
         sent = [[] for _ in range(peers)]
-        tables, moved = None, None
+        chunk = pack(neighbours, current_east, current_north, spectrum, cuts[0][1])
+        sides, table = from_pairs(chunk), rows
         for low, high in cuts:
-            if tables is None:
-                chunk = pack(neighbours, current_east, current_north, spectrum, high)
-            else:
-                chunk, near = lax.optimization_barrier((spectrum[low:high], tables[0]))
-                tables = (near, *tables[1:])
-            sides = from_pairs(chunk)
-            first = 0 if tables else 8
-            tables = tables or sides
-            moved = propagate(turn, odd, rows, tables, sides, first, low, high - low)
+            first = 0 if low else 8
+            coming = None
+            if high < row_count:
+                chunk, near = lax.optimization_barrier((rows_from(spectrum, high, row_count), sides[0]))
+                sides = (near, *sides[1:])
+                coming = from_pairs(chunk)
+            moved = propagate(turn, odd, rows, table, sides, first, low, high - low)
+            sides, table = coming, moved[-1]
             for m in range(peers):
                 piece = moved[m]
                 if m:
@@ -334,8 +357,8 @@
     tiles = []
     for start in range(0, columns, DEEP):
         sides = [wide[:, start + j * DEEP : start + (j + 1) * DEEP] for j in range(3)]
-        tables = [table[:, start + j * DEEP : start + (j + 1) * DEEP] for j in range(3)]
-        tiles += propagate(still, still + 1, rows, tables, sides, 0, 0, row_count + extra)
+        near = table[:, start : start + 3 * DEEP]
+        tiles += propagate(still, still + 1, rows, near, sides, 0, 0, row_count + extra)
     grid = jnp.concatenate(tiles, axis=1)[:row_count].reshape(row_count, peers, columns // peers).swapaxes(0, 1)
     arrived = lax.all_to_all(grid, "comp", 0, 0, tiled=True)
     arrived = arrived.reshape(NF * ND, columns // peers)

time: 75.4 us -> 77.6 us (1.029)
  waiting for transfers between devices: 37.6 us -> 40 us
  local copies, waits for them, and re-layouts: 2.22 us -> 0.87 us
    ppermute x9, waiting for transfers between devices: 32.5 us -> 34.4 us  [shards(): lax.ppermute(piece, 'comp', [(i, (i + m) % peers) for i in range(peers)])]
    unnamed x25 -> x15, local copies, waits for them, and re-layouts: 2 us -> 0.69 us
    pallas_call x0 -> x1, Pallas kernels: none -> 1.03 us  [rows_from(): pl.pallas_call(functools.partial(rows_kernel, low), out_shape=pltpu.VMEM(...]
  transfers between devices with their start and end apart: 13 -> 13, of which waited for: 7 -> 8; matrix products, arithmetic and copies ran while one was open for 1% -> 1% of each run, Pallas kernels for 19% -> 19%
where the time goes in v5:
time: 77.6 us; the launch traced here: 77.3 us
  waiting for transfers between devices  40 us (52%)
  Pallas kernels  19.8 us (26%)
  starting transfers between devices  16.2 us (21%)
  local copies, waits for them, and re-layouts  0.87 us (1%)
    ppermute x9, waiting for transfers between devices, shards(): lax.ppermute(piece, 'comp', [(i, (i + m) % peers) for i in range(peers)])  34.4 us
    pallas_call x2, Pallas kernels, propagate(): pl.pallas_call(functools.partial(propagate_kernel, first, low), out_shape...  13.9 us
    ppermute x9, starting transfers between devices, shards(): lax.ppermute(piece, 'comp', [(i, (i + m) % peers) for i in range(peers)])  9.87 us
    ppermute x2, waiting for transfers between devices, from_pairs(): far = lax.ppermute(cells, 'space', pairs[1])  5.58 us
    ppermute x2, starting transfers between devices, from_pairs(): far = lax.ppermute(cells, 'space', pairs[1])  5.54 us
    pallas_call x1, Pallas kernels, source_term(): pl.pallas_call(functools.partial(source_kernel, starts, step, len(pieces)...  2.51 us
  transfers between devices with their start and end apart: 13, of which 8 were waited for; matrix products, arithmetic and copies ran while one was open for 1% of the time, Pallas kernels for 19%

profile of v5, /device:TPU:13, one launch (start us, length us, event | category | flops | bytes accessed | tf_op | source)
XLA Modules:
  0.0 77.3 jit_solution(2991633827966438924)
XLA Ops:
  0.0 1.2 %pack.1.refs_2_ = f32[360,512]{1,0:T(8,128)S(1)} custom-call(s32[4,512]{1,0:T(4,128)} %neighbours.1, f32[1,512]{1,0:T(1,128)} %bitcast.6, f32[1,512]{1,0:T(1,128)} %bitcast.7, f32[576,512]{1,0:T(8,128)} %cells.3), custom_call_target="tpu_custom_call" | custom-call | tf_op jit(solution)/shard_map/pack/pallas_call | solution.py:255
  1.2 0.0 copy-start.5
  1.2 0.0 copy-start.6
  1.2 0.7 collective-permute-start
  2.0 3.0 %collective-permute-start.1 = (f32[360,512]{1,0:T(8,128)S(1)}, f32[360,512]{1,0:T(8,128)S(1)}, u32[]{:S(2)}, u32[]{:S(2)}) collective-permute-start(f32[360,512]{1,0:T(8,128)S(1)} %pack.1.refs_2_), channel_id=1, source_target_pairs={{1,2},{2,1},{5,6},{6,5},{9,10},{10,9},{13,14},{14,13},{17,18},{18,... | collective-permute-start | bytes 2211848 | tf_op jit(solution)/shard_map/ppermute | solution.py:219
  5.0 1.0 %rest.1.refs_2_ = f32[224,512]{1,0:T(8,128)S(1)} custom-call(f32[576,512]{1,0:T(8,128)} %cells.3), custom_call_target="tpu_custom_call" | custom-call | tf_op jit(solution)/shard_map/rest/pallas_call | solution.py:278
  6.1 0.0 copy-done.5
  6.1 0.0 copy-done.6
  6.1 0.1 broadcast_multiply_fusion
  6.2 0.1 mul.65
  6.3 0.1 mul.61
  6.4 0.0 collective-permute-done.refs_1_
  6.4 2.5 %collective-permute-start.3 = (f32[224,512]{1,0:T(8,128)S(1)}, f32[224,512]{1,0:T(8,128)S(1)}, u32[]{:S(2)}, u32[]{:S(2)}) collective-permute-start(f32[224,512]{1,0:T(8,128)S(1)} %rest.1.refs_2_), channel_id=1, source_target_pairs={{1,2},{2,1},{5,6},{6,5},{9,10},{10,9},{13,14},{14,13},{17,18},{18,... | collective-permute-start | bytes 1376264 | tf_op jit(solution)/shard_map/ppermute | solution.py:219
  8.9 0.1 collective-permute-start.2
  9.1 0.1 fusion.2
  9.2 5.6 %collective-permute-done.1.refs_3_ = f32[360,512]{1,0:T(8,128)S(1)} collective-permute-done((f32[360,512]{1,0:T(8,128)S(1)}, f32[360,512]{1,0:T(8,128)S(1)}, u32[]{:S(2)}, u32[]{:S(2)}) %collective-permute-start.1) | collective-permute-done | bytes 737312 | tf_op jit(solution)/shard_map/ppermute | solution.py:219
  14.8 7.5 %propagate.2 = (f32[352,128]{1,0:T(8,128)}, f32[352,128]{1,0:T(8,128)S(1)}, f32[352,128]{1,0:T(8,128)}, f32[352,128]{1,0:T(8,128)}, f32[8,1536]{1,0:T(8,128)S(1)}) custom-call(s32[1]{0:T(128)} %bitcast.turn, s32[1]{0:T(128)} %bitcast.2.odd, f32[8,640]{1,0:T(8,128)S(1)} %pad.4.rows.refs_0_, f32[8,640]{1,0:T(8,128)S(1)} %pad.4.rows.refs_0_, ...), custom_call_target="tpu_custom_call" | custom-call | tf_op jit(solution)/shard_map/propagate/pallas_call | solution.py:113
  22.3 0.0 copy-start
  22.3 1.3 %collective-permute-start.4 = (f32[352,128]{1,0:T(8,128)S(1)}, f32[352,128]{1,0:T(8,128)S(1)}, u32[]{:S(2)}, u32[]{:S(2)}) collective-permute-start(f32[352,128]{1,0:T(8,128)S(1)} %get-tuple-element.25), channel_id=1, source_target_pairs={{0,4},{4,8},{8,12},{12,0},{1,5},{5,9},{9,13},{13,1},{2,6},{6,10},{... | collective-permute-start | bytes 540680 | tf_op jit(solution)/shard_map/ppermute | solution.py:339
  23.6 1.0 %collective-permute-start.6 = (f32[352,128]{1,0:T(8,128)}, f32[352,128]{1,0:T(8,128)S(1)}, u32[]{:S(2)}, u32[]{:S(2)}) collective-permute-start(f32[352,128]{1,0:T(8,128)} %get-tuple-element.27), channel_id=1, source_target_pairs={{0,8},{4,12},{8,0},{12,4},{1,9},{5,13},{9,1},{13,5},{2,10},{6,14},... | collective-permute-start | bytes 540680 | tf_op jit(solution)/shard_map/ppermute | solution.py:339
  24.6 1.5 %collective-permute-start.8 = (f32[352,128]{1,0:T(8,128)}, f32[352,128]{1,0:T(8,128)S(1)}, u32[]{:S(2)}, u32[]{:S(2)}) collective-permute-start(f32[352,128]{1,0:T(8,128)} %get-tuple-element.29), channel_id=1, source_target_pairs={{0,12},{4,0},{8,4},{12,8},{1,13},{5,1},{9,5},{13,9},{2,14},{6,2},{... | collective-permute-start | bytes 540680 | tf_op jit(solution)/shard_map/ppermute | solution.py:339
  26.0 0.0 collective-permute-done.3.refs_3_
  26.1 0.0 collective-permute-done.2.refs_1_
  26.1 6.4 %propagate.3 = (f32[224,128]{1,0:T(8,128)}, f32[224,128]{1,0:T(8,128)}, f32[224,128]{1,0:T(8,128)}, f32[224,128]{1,0:T(8,128)S(1)}) custom-call(s32[1]{0:T(128)} %bitcast.turn, s32[1]{0:T(128)} %bitcast.2.odd, f32[8,640]{1,0:T(8,128)S(1)} %pad.4.rows.refs_0_, f32[8,1536]{1,0:T(8,128)S(1)} %get-tuple-element.22.refs_0_, ...), custom_call_target="tpu_custom_call" | custom-call | tf_op jit(solution)/shard_map/propagate/pallas_call | solution.py:113
  32.4 0.0 copy-start.1
  32.4 0.1 collective-permute-start.5
  32.5 3.1 %collective-permute-start.7 = (f32[224,128]{1,0:T(8,128)}, f32[224,128]{1,0:T(8,128)S(1)}, u32[]{:S(2)}, u32[]{:S(2)}) collective-permute-start(f32[224,128]{1,0:T(8,128)} %get-tuple-element.28), channel_id=1, source_target_pairs={{0,8},{4,12},{8,0},{12,4},{1,9},{5,13},{9,1},{13,5},{2,10},{6,14},... | collective-permute-start | bytes 344072 | tf_op jit(solution)/shard_map/ppermute | solution.py:339
  35.6 0.0 collective-permute-done.4.refs_2_
  35.6 0.0 collective-permute-start.9
  35.6 0.0 copy-done
  35.6 0.7 copy.10
  36.3 6.1 %collective-permute-done.6.refs_4_ = f32[352,128]{1,0:T(8,128)S(1)} collective-permute-done((f32[352,128]{1,0:T(8,128)}, f32[352,128]{1,0:T(8,128)S(1)}, u32[]{:S(2)}, u32[]{:S(2)}) %collective-permute-start.6) | collective-permute-done | bytes 180256 | tf_op jit(solution)/shard_map/ppermute | solution.py:339
  42.4 0.0 collective-permute-done.8.refs_6_
  42.4 1.2 %collective-permute-done.5.refs_3_ = f32[224,128]{1,0:T(8,128)S(1)} collective-permute-done((f32[224,128]{1,0:T(8,128)}, f32[224,128]{1,0:T(8,128)S(1)}, u32[]{:S(2)}, u32[]{:S(2)}) %collective-permute-start.5) | collective-permute-done | bytes 114720 | tf_op jit(solution)/shard_map/ppermute | solution.py:339
  43.6 1.2 %collective-permute-done.7.refs_5_ = f32[224,128]{1,0:T(8,128)S(1)} collective-permute-done((f32[224,128]{1,0:T(8,128)}, f32[224,128]{1,0:T(8,128)S(1)}, u32[]{:S(2)}, u32[]{:S(2)}) %collective-permute-start.7) | collective-permute-done | bytes 114720 | tf_op jit(solution)/shard_map/ppermute | solution.py:339
  44.8 1.3 %collective-permute-done.9.refs_7_ = f32[224,128]{1,0:T(8,128)S(1)} collective-permute-done((f32[224,128]{1,0:T(8,128)S(1)}, f32[224,128]{1,0:T(8,128)S(1)}, u32[]{:S(2)}, u32[]{:S(2)}) %collective-permute-start.9) | collective-permute-done | bytes 114720 | tf_op jit(solution)/shard_map/ppermute | solution.py:339
  46.2 0.0 copy-done.1
  46.2 0.0 copy-done.2
  46.2 0.0 copy-done.3
  46.2 0.0 copy-done.4
  46.2 2.5 %source.1 = (f32[576,128]{1,0:T(8,128)S(1)}, f32[576,128]{1,0:T(8,128)S(1)}, f32[576,128]{1,0:T(8,128)S(1)}, f32[576,128]{1,0:T(8,128)S(1)}) custom-call(s32[4,64]{1,0:T(4,128)S(1)} %copy-done.3, f32[64]{0:T(128)S(1)} %copy-done.4, s32[1]{0:T(128)} %bitcast.turn, bf16[64,64,64]{2,1,0:T(8,128)(2,1)S(1)} %copy-done, bf16[64,64,64]{2,1,0:T(8,128)(2,1)S(1)} %bitcast.5, ...), custom_call_target="tpu_custom_call" | custom-call | tf_op jit(solution)/shard_map/source/pallas_call | solution.py:172
  48.7 0.1 collective-permute-start.10
  48.8 2.0 %collective-permute-start.11 = (f32[576,128]{1,0:T(8,128)S(1)}, f32[576,128]{1,0:T(8,128)S(1)}, u32[]{:S(2)}, u32[]{:S(2)}) collective-permute-start(f32[576,128]{1,0:T(8,128)S(1)} %get-tuple-element.33), channel_id=1, source_target_pairs={{0,8},{4,12},{8,0},{12,4},{1,9},{5,13},{9,1},{13,5},{2,10},{6,14},... | collective-permute-start | bytes 884744 | tf_op jit(solution)/shard_map/ppermute | solution.py:345
  50.7 0.9 %collective-permute-start.12 = (f32[576,128]{1,0:T(8,128)S(1)}, f32[576,128]{1,0:T(8,128)S(1)}, u32[]{:S(2)}, u32[]{:S(2)}) collective-permute-start(f32[576,128]{1,0:T(8,128)S(1)} %get-tuple-element.34), channel_id=1, source_target_pairs={{0,12},{4,0},{8,4},{12,8},{1,13},{5,1},{9,5},{13,9},{2,14},{6,2},{... | collective-permute-start | bytes 884744 | tf_op jit(solution)/shard_map/ppermute | solution.py:345
  51.6 6.2 %collective-permute-done.10.refs_1_ = f32[576,128]{1,0:T(8,128)S(1)} collective-permute-done((f32[576,128]{1,0:T(8,128)S(1)}, f32[576,128]{1,0:T(8,128)S(1)}, u32[]{:S(2)}, u32[]{:S(2)}) %collective-permute-start.10) | collective-permute-done | bytes 294944 | tf_op jit(solution)/shard_map/ppermute | solution.py:345
  57.8 16.5 %collective-permute-done.11.refs_2_ = f32[576,128]{1,0:T(8,128)S(1)} collective-permute-done((f32[576,128]{1,0:T(8,128)S(1)}, f32[576,128]{1,0:T(8,128)S(1)}, u32[]{:S(2)}, u32[]{:S(2)}) %collective-permute-start.11) | collective-permute-done | bytes 294944 | tf_op jit(solution)/shard_map/ppermute | solution.py:345
  74.3 1.8 %collective-permute-done.12.refs_3_ = f32[576,128]{1,0:T(8,128)S(1)} collective-permute-done((f32[576,128]{1,0:T(8,128)S(1)}, f32[576,128]{1,0:T(8,128)S(1)}, u32[]{:S(2)}, u32[]{:S(2)}) %collective-permute-start.12) | collective-permute-done | bytes 294944 | tf_op jit(solution)/shard_map/ppermute | solution.py:345
  76.1 1.2 %columns.1 = f32[576,512]{1,0:T(8,128)} custom-call(s32[1]{0:T(128)} %bitcast.turn, f32[576,128]{1,0:T(8,128)S(1)} %get-tuple-element.31.refs_0_, f32[576,128]{1,0:T(8,128)S(1)} %collective-permute-done.10.refs_1_, f32[576,128]{1,0:T(8,128)S(1)} %collective-permute-done.11.refs_2_, f32[576,128]{1,0:T(8,128)S(1)} %collective-permute-done.12.refs_3_), custom_call_target="tpu_custom_call" | custom-call | tf_op jit(solution)/shard_map/columns/pallas_call | solution.py:196
  (11 shorter events, 0.1 us)
Async XLA Ops:
  1.2 4.8 %copy-start.5 = (s32[2304]{0:T(1024)S(1)}, s32[2304]{0:T(1024)}, u32[]{:S(2)}) copy-start(s32[2304]{0:T(1024)} %param.13) | copy-start | bytes 27652
  1.2 4.9 %copy-start.6 = (f32[36]{0:T(128)S(1)}, f32[36]{0:T(128)}, u32[]{:S(2)}) copy-start(f32[36]{0:T(128)} %param.10) | copy-start | bytes 436
  1.2 5.1 %collective-permute-start = (f32[360,512]{1,0:T(8,128)S(1)}, f32[360,512]{1,0:T(8,128)S(1)}, u32[]{:S(2)}, u32[]{:S(2)}) collective-permute-start(f32[360,512]{1,0:T(8,128)S(1)} %pack.1.refs_2_), channel_id=1, source_target_pairs={{0,1},{1,0},{2,3},{3,2},{4,5},{5,4},{6,7},{7,6},{8,9},{9,8},{10,11... | collective-permute-start | bytes 2211848 | tf_op jit(solution)/shard_map/ppermute | solution.py:220
  2.0 12.8 %collective-permute-start.1 = (f32[360,512]{1,0:T(8,128)S(1)}, f32[360,512]{1,0:T(8,128)S(1)}, u32[]{:S(2)}, u32[]{:S(2)}) collective-permute-start(f32[360,512]{1,0:T(8,128)S(1)} %pack.1.refs_2_), channel_id=1, source_target_pairs={{1,2},{2,1},{5,6},{6,5},{9,10},{10,9},{13,14},{14,13},{17,18},{18,... | collective-permute-start | bytes 2211848 | tf_op jit(solution)/shard_map/ppermute | solution.py:219
  6.4 19.7 %collective-permute-start.3 = (f32[224,512]{1,0:T(8,128)S(1)}, f32[224,512]{1,0:T(8,128)S(1)}, u32[]{:S(2)}, u32[]{:S(2)}) collective-permute-start(f32[224,512]{1,0:T(8,128)S(1)} %rest.1.refs_2_), channel_id=1, source_target_pairs={{1,2},{2,1},{5,6},{6,5},{9,10},{10,9},{13,14},{14,13},{17,18},{18,... | collective-permute-start | bytes 1376264 | tf_op jit(solution)/shard_map/ppermute | solution.py:219
  8.9 17.1 %collective-permute-start.2 = (f32[224,512]{1,0:T(8,128)S(1)}, f32[224,512]{1,0:T(8,128)}, u32[]{:S(2)}, u32[]{:S(2)}) collective-permute-start(f32[224,512]{1,0:T(8,128)S(1)} %rest.1.refs_2_), channel_id=1, source_target_pairs={{0,1},{1,0},{2,3},{3,2},{4,5},{5,4},{6,7},{7,6},{8,9},{9,8},{10,11... | collective-permute-start | bytes 1376264 | tf_op jit(solution)/shard_map/ppermute | solution.py:220
  22.3 13.4 %copy-start = (bf16[64,64,64]{2,1,0:T(8,128)(2,1)S(1)}, bf16[64,64,64]{2,1,0:T(8,128)(2,1)}, u32[]{:S(2)}) copy-start(bf16[64,64,64]{2,1,0:T(8,128)(2,1)} %blocks.1) | copy-start | bytes 1572868
  22.3 13.4 %collective-permute-start.4 = (f32[352,128]{1,0:T(8,128)S(1)}, f32[352,128]{1,0:T(8,128)S(1)}, u32[]{:S(2)}, u32[]{:S(2)}) collective-permute-start(f32[352,128]{1,0:T(8,128)S(1)} %get-tuple-element.25), channel_id=1, source_target_pairs={{0,4},{4,8},{8,12},{12,0},{1,5},{5,9},{9,13},{13,1},{2,6},{6,10},{... | collective-permute-start | bytes 540680 | tf_op jit(solution)/shard_map/ppermute | solution.py:339
  23.6 18.8 %collective-permute-start.6 = (f32[352,128]{1,0:T(8,128)}, f32[352,128]{1,0:T(8,128)S(1)}, u32[]{:S(2)}, u32[]{:S(2)}) collective-permute-start(f32[352,128]{1,0:T(8,128)} %get-tuple-element.27), channel_id=1, source_target_pairs={{0,8},{4,12},{8,0},{12,4},{1,9},{5,13},{9,1},{13,5},{2,10},{6,14},... | collective-permute-start | bytes 540680 | tf_op jit(solution)/shard_map/ppermute | solution.py:339
  24.6 17.8 %collective-permute-start.8 = (f32[352,128]{1,0:T(8,128)}, f32[352,128]{1,0:T(8,128)S(1)}, u32[]{:S(2)}, u32[]{:S(2)}) collective-permute-start(f32[352,128]{1,0:T(8,128)} %get-tuple-element.29), channel_id=1, source_target_pairs={{0,12},{4,0},{8,4},{12,8},{1,13},{5,1},{9,5},{13,9},{2,14},{6,2},{... | collective-permute-start | bytes 540680 | tf_op jit(solution)/shard_map/ppermute | solution.py:339
  32.4 13.8 %copy-start.1 = (f32[352,128]{1,0:T(8,128)S(1)}, f32[352,128]{1,0:T(8,128)}, u32[]{:S(2)}) copy-start(f32[352,128]{1,0:T(8,128)} %get-tuple-element.21.refs_0_) | copy-start | bytes 540676
  32.4 13.8 %copy-start.2 = (f32[224,128]{1,0:T(8,128)S(1)}, f32[224,128]{1,0:T(8,128)}, u32[]{:S(2)}) copy-start(f32[224,128]{1,0:T(8,128)} %get-tuple-element.24.refs_1_) | copy-start | bytes 344068
  32.4 13.8 %copy-start.3 = (s32[4,64]{1,0:T(4,128)S(1)}, s32[4,64]{1,0:T(4,128)}, u32[]{:S(2)}) copy-start(s32[4,64]{1,0:T(4,128)} %quad.1) | copy-start | bytes 3076
  32.4 13.8 %copy-start.4 = (f32[64]{0:T(128)S(1)}, f32[64]{0:T(128)}, u32[]{:S(2)}) copy-start(f32[64]{0:T(128)} %strength.1) | copy-start | bytes 772
  32.4 11.2 %collective-permute-start.5 = (f32[224,128]{1,0:T(8,128)}, f32[224,128]{1,0:T(8,128)S(1)}, u32[]{:S(2)}, u32[]{:S(2)}) collective-permute-start(f32[224,128]{1,0:T(8,128)} %get-tuple-element.26), channel_id=1, source_target_pairs={{0,4},{4,8},{8,12},{12,0},{1,5},{5,9},{9,13},{13,1},{2,6},{6,10},{... | collective-permute-start | bytes 344072 | tf_op jit(solution)/shard_map/ppermute | solution.py:339
  32.5 12.3 %collective-permute-start.7 = (f32[224,128]{1,0:T(8,128)}, f32[224,128]{1,0:T(8,128)S(1)}, u32[]{:S(2)}, u32[]{:S(2)}) collective-permute-start(f32[224,128]{1,0:T(8,128)} %get-tuple-element.28), channel_id=1, source_target_pairs={{0,8},{4,12},{8,0},{12,4},{1,9},{5,13},{9,1},{13,5},{2,10},{6,14},... | collective-permute-start | bytes 344072 | tf_op jit(solution)/shard_map/ppermute | solution.py:339
  35.6 10.5 %collective-permute-start.9 = (f32[224,128]{1,0:T(8,128)S(1)}, f32[224,128]{1,0:T(8,128)S(1)}, u32[]{:S(2)}, u32[]{:S(2)}) collective-permute-start(f32[224,128]{1,0:T(8,128)S(1)} %get-tuple-element.30), channel_id=1, source_target_pairs={{0,12},{4,0},{8,4},{12,8},{1,13},{5,1},{9,5},{13,9},{2,14},{6,2},{... | collective-permute-start | bytes 344072 | tf_op jit(solution)/shard_map/ppermute | solution.py:339
  48.7 9.1 %collective-permute-start.10 = (f32[576,128]{1,0:T(8,128)S(1)}, f32[576,128]{1,0:T(8,128)S(1)}, u32[]{:S(2)}, u32[]{:S(2)}) collective-permute-start(f32[576,128]{1,0:T(8,128)S(1)} %get-tuple-element.32), channel_id=1, source_target_pairs={{0,4},{4,8},{8,12},{12,0},{1,5},{5,9},{9,13},{13,1},{2,6},{6,10},{... | collective-permute-start | bytes 884744 | tf_op jit(solution)/shard_map/ppermute | solution.py:345
  48.8 25.5 %collective-permute-start.11 = (f32[576,128]{1,0:T(8,128)S(1)}, f32[576,128]{1,0:T(8,128)S(1)}, u32[]{:S(2)}, u32[]{:S(2)}) collective-permute-start(f32[576,128]{1,0:T(8,128)S(1)} %get-tuple-element.33), channel_id=1, source_target_pairs={{0,8},{4,12},{8,0},{12,4},{1,9},{5,13},{9,1},{13,5},{2,10},{6,14},... | collective-permute-start | bytes 884744 | tf_op jit(solution)/shard_map/ppermute | solution.py:345
  50.7 25.4 %collective-permute-start.12 = (f32[576,128]{1,0:T(8,128)S(1)}, f32[576,128]{1,0:T(8,128)S(1)}, u32[]{:S(2)}, u32[]{:S(2)}) collective-permute-start(f32[576,128]{1,0:T(8,128)S(1)} %get-tuple-element.34), channel_id=1, source_target_pairs={{0,12},{4,0},{8,4},{12,8},{1,13},{5,1},{9,5},{13,9},{2,14},{6,2},{... | collective-permute-start | bytes 884744 | tf_op jit(solution)/shard_map/ppermute | solution.py:345

commit v6 on v5

--- a/solution.py
+++ b/solution.py
@@ -211,14 +211,17 @@
     return before, after
 
 
-def from_pairs(cells):
+def from_pairs(cells, gate=None):
     count = lax.axis_size("space")
     pairs = [[], []]
     for i in range(count - 1):
         pairs[i % 2] += [(i, i + 1), (i + 1, i)]
-    far = lax.ppermute(cells, "space", pairs[1])
     near = lax.ppermute(cells, "space", pairs[0])
-    return near, cells, far
+    held = cells
+    if gate is not None:
+        held, gate = lax.optimization_barrier((cells, gate))
+    far = lax.ppermute(held, "space", pairs[1])
+    return (near, cells, far), gate
 
 
 def point_table(neighbours, current_east, current_north):
@@ -268,24 +271,6 @@
     )(*map(in_hbm, (neighbours, east[None], north[None], spectrum)))
 
 
-def rows_kernel(low, cells, out, flag):
-    copy = pltpu.make_async_copy(cells.at[low : low + out.shape[0], :], out, flag)
-    copy.start()
-    copy.wait()
-
-
-def rows_from(spectrum, low, high):
-    return pl.pallas_call(
-        functools.partial(rows_kernel, low),
-        out_shape=pltpu.VMEM((high - low, spectrum.shape[1]), jnp.float32),
-        in_specs=[pl.BlockSpec(memory_space=pl.ANY)],
-        out_specs=VMEM,
-        scratch_shapes=[pltpu.SemaphoreType.DMA],
-        compiler_params=PARAMS,
-        name="rest",
-    )(in_hbm(spectrum))
-
-
 def row_table(first_comp, row_count, substeps, wave_speed):
     angles = (jnp.arange(ND, dtype=jnp.float32) + 0.5) * (2.0 * math.pi / ND)
     inverse = courant_scale / substeps.astype(jnp.float32)
@@ -297,7 +282,7 @@
 
 
 def cuts_of(row_count):
-    middle = row_count * 5 // 8 // 32 * 32
+    middle = row_count // 2 // 16 * 16
     return [(0, middle), (middle, row_count)]
 
 
@@ -323,14 +308,13 @@
         cuts = cuts_of(row_count)
         sent = [[] for _ in range(peers)]
         chunk = pack(neighbours, current_east, current_north, spectrum, cuts[0][1])
-        sides, table = from_pairs(chunk), rows
+        (sides, gate), table = from_pairs(chunk), rows
         for low, high in cuts:
             first = 0 if low else 8
             coming = None
             if high < row_count:
-                chunk, near = lax.optimization_barrier((rows_from(spectrum, high, row_count), sides[0]))
+                coming, near = from_pairs(spectrum[high:], sides[0])
                 sides = (near, *sides[1:])
-                coming = from_pairs(chunk)
             moved = propagate(turn, odd, rows, table, sides, first, low, high - low)
             sides, table = coming, moved[-1]
             for m in range(peers):

time: 77.6 us -> 74.4 us (0.959)
  waiting for transfers between devices: 40 us -> 38.2 us
  Pallas kernels: 19.8 us -> 18.9 us
    ppermute x9, waiting for transfers between devices: 34.4 us -> 33 us  [shards(): lax.ppermute(piece, 'comp', [(i, (i + m) % peers) for i in range(peers)])]
    pallas_call x1 -> x0, Pallas kernels: 1.03 us -> none  [rows_from(): pl.pallas_call(functools.partial(rows_kernel, low), out_shape=pltpu.VMEM(...]
  transfers between devices with their start and end apart: 13 -> 13, of which waited for: 8 -> 7; matrix products, arithmetic and copies ran while one was open for 1% -> 1% of each run, Pallas kernels for 19% -> 19%
where the time goes in v6:
time: 74.4 us; the launch traced here: 74.2 us
  waiting for transfers between devices  38.2 us (51%)
  Pallas kernels  18.9 us (25%)
  starting transfers between devices  15.8 us (21%)
  local copies, waits for them, and re-layouts  0.91 us (1%)
    ppermute x9, waiting for transfers between devices, shards(): lax.ppermute(piece, 'comp', [(i, (i + m) % peers) for i in range(peers)])  33 us
    pallas_call x2, Pallas kernels, propagate(): pl.pallas_call(functools.partial(propagate_kernel, first, low), out_shape...  14 us
    ppermute x9, starting transfers between devices, shards(): lax.ppermute(piece, 'comp', [(i, (i + m) % peers) for i in range(peers)])  9.45 us
    ppermute x2, starting transfers between devices, from_pairs(): far = lax.ppermute(held, 'space', pairs[1])  5.55 us
    ppermute x2, waiting for transfers between devices, from_pairs(): far = lax.ppermute(held, 'space', pairs[1])  5.17 us
    pallas_call x1, Pallas kernels, source_term(): pl.pallas_call(functools.partial(source_kernel, starts, step, len(pieces)...  2.51 us
  transfers between devices with their start and end apart: 13, of which 7 were waited for; matrix products, arithmetic and copies ran while one was open for 1% of the time, Pallas kernels for 19%

profile of v6, /device:TPU:13, one launch (start us, length us, event | category | flops | bytes accessed | tf_op | source)
XLA Modules:
  0.0 74.2 jit_solution(2848700249478180528)
XLA Ops:
  0.0 0.0 copy-start.5
  0.0 0.0 copy-start.7
  0.0 0.0 copy-start.6
  0.0 1.3 %pack.1.refs_2_ = f32[296,512]{1,0:T(8,128)S(1)} custom-call(s32[4,512]{1,0:T(4,128)} %neighbours.1, f32[1,512]{1,0:T(1,128)} %bitcast.6, f32[1,512]{1,0:T(1,128)} %bitcast.7, f32[576,512]{1,0:T(8,128)} %cells.1), custom_call_target="tpu_custom_call" | custom-call | tf_op jit(solution)/shard_map/pack/pallas_call | solution.py:258
  1.3 0.7 collective-permute-start
  2.0 3.0 %collective-permute-start.1 = (f32[296,512]{1,0:T(8,128)S(1)}, f32[296,512]{1,0:T(8,128)S(1)}, u32[]{:S(2)}, u32[]{:S(2)}) collective-permute-start(f32[296,512]{1,0:T(8,128)S(1)} %pack.1.refs_2_), channel_id=1, source_target_pairs={{1,2},{2,1},{5,6},{6,5},{9,10},{10,9},{13,14},{14,13},{17,18},{18,... | collective-permute-start | bytes 1818632 | tf_op jit(solution)/shard_map/ppermute | solution.py:223
  5.0 0.0 copy-done.5
  5.1 0.1 collective-permute-start.2
  5.2 0.0 collective-permute-done.refs_1_
  5.2 2.5 %collective-permute-start.3 = (f32[288,512]{1,0:T(8,128)S(1)}, f32[288,512]{1,0:T(8,128)}, u32[]{:S(2)}, u32[]{:S(2)}) collective-permute-start(f32[288,512]{1,0:T(8,128)S(1)} %slice.3.refs_2_), channel_id=1, source_target_pairs={{1,2},{2,1},{5,6},{6,5},{9,10},{10,9},{13,14},{14,13},{17,18},{18,... | collective-permute-start | bytes 1769480 | tf_op jit(solution)/shard_map/ppermute | solution.py:223
  7.8 0.0 copy-done.7
  7.8 0.1 broadcast_multiply_fusion
  7.9 0.1 mul.61
  7.9 0.1 mul.65
  8.0 0.0 copy-done.6
  8.1 0.1 fusion.2
  8.2 5.2 %collective-permute-done.1.refs_3_ = f32[296,512]{1,0:T(8,128)S(1)} collective-permute-done((f32[296,512]{1,0:T(8,128)S(1)}, f32[296,512]{1,0:T(8,128)S(1)}, u32[]{:S(2)}, u32[]{:S(2)}) %collective-permute-start.1) | collective-permute-done | bytes 606240 | tf_op jit(solution)/shard_map/ppermute | solution.py:223
  13.4 6.4 %propagate.2 = (f32[288,128]{1,0:T(8,128)}, f32[288,128]{1,0:T(8,128)S(1)}, f32[288,128]{1,0:T(8,128)}, f32[288,128]{1,0:T(8,128)}, f32[8,1536]{1,0:T(8,128)S(1)}) custom-call(s32[1]{0:T(128)} %bitcast.turn, s32[1]{0:T(128)} %bitcast.2.odd, f32[8,640]{1,0:T(8,128)S(1)} %pad.4.rows.refs_0_, f32[8,640]{1,0:T(8,128)S(1)} %pad.4.rows.refs_0_, ...), custom_call_target="tpu_custom_call" | custom-call | tf_op jit(solution)/shard_map/propagate/pallas_call | solution.py:113
  19.8 0.0 copy-start
  19.8 1.3 %collective-permute-start.4 = (f32[288,128]{1,0:T(8,128)S(1)}, f32[288,128]{1,0:T(8,128)S(1)}, u32[]{:S(2)}, u32[]{:S(2)}) collective-permute-start(f32[288,128]{1,0:T(8,128)S(1)} %get-tuple-element.25), channel_id=1, source_target_pairs={{0,4},{4,8},{8,12},{12,0},{1,5},{5,9},{9,13},{13,1},{2,6},{6,10},{... | collective-permute-start | bytes 442376 | tf_op jit(solution)/shard_map/ppermute | solution.py:323
  21.1 1.0 %collective-permute-start.6 = (f32[288,128]{1,0:T(8,128)}, f32[288,128]{1,0:T(8,128)S(1)}, u32[]{:S(2)}, u32[]{:S(2)}) collective-permute-start(f32[288,128]{1,0:T(8,128)} %get-tuple-element.27), channel_id=1, source_target_pairs={{0,8},{4,12},{8,0},{12,4},{1,9},{5,13},{9,1},{13,5},{2,10},{6,14},... | collective-permute-start | bytes 442376 | tf_op jit(solution)/shard_map/ppermute | solution.py:323
  22.1 1.5 %collective-permute-start.8 = (f32[288,128]{1,0:T(8,128)}, f32[288,128]{1,0:T(8,128)S(1)}, u32[]{:S(2)}, u32[]{:S(2)}) collective-permute-start(f32[288,128]{1,0:T(8,128)} %get-tuple-element.29), channel_id=1, source_target_pairs={{0,12},{4,0},{8,4},{12,8},{1,13},{5,1},{9,5},{13,9},{2,14},{6,2},{... | collective-permute-start | bytes 442376 | tf_op jit(solution)/shard_map/ppermute | solution.py:323
  23.5 0.0 collective-permute-done.2.refs_1_
  23.5 0.0 collective-permute-done.3.refs_3_
  23.6 7.6 %propagate.3 = (f32[288,128]{1,0:T(8,128)}, f32[288,128]{1,0:T(8,128)}, f32[288,128]{1,0:T(8,128)}, f32[288,128]{1,0:T(8,128)}) custom-call(s32[1]{0:T(128)} %bitcast.turn, s32[1]{0:T(128)} %bitcast.2.odd, f32[8,640]{1,0:T(8,128)S(1)} %pad.4.rows.refs_0_, f32[8,1536]{1,0:T(8,128)S(1)} %get-tuple-element.22.refs_0_, ...), custom_call_target="tpu_custom_call" | custom-call | tf_op jit(solution)/shard_map/propagate/pallas_call | solution.py:113
  31.2 0.1 collective-permute-start.5
  31.2 3.1 %collective-permute-start.7 = (f32[288,128]{1,0:T(8,128)}, f32[288,128]{1,0:T(8,128)S(1)}, u32[]{:S(2)}, u32[]{:S(2)}) collective-permute-start(f32[288,128]{1,0:T(8,128)} %get-tuple-element.28), channel_id=1, source_target_pairs={{0,8},{4,12},{8,0},{12,4},{1,9},{5,13},{9,1},{13,5},{2,10},{6,14},... | collective-permute-start | bytes 442376 | tf_op jit(solution)/shard_map/ppermute | solution.py:323
  34.4 0.0 collective-permute-done.4.refs_2_
  34.4 0.0 collective-permute-start.9
  34.4 0.0 copy-done
  34.4 0.7 copy.10
  35.0 0.0 collective-permute-done.6.refs_4_
  35.0 0.0 collective-permute-done.8.refs_6_
  35.1 5.1 %collective-permute-done.5.refs_3_ = f32[288,128]{1,0:T(8,128)S(1)} collective-permute-done((f32[288,128]{1,0:T(8,128)}, f32[288,128]{1,0:T(8,128)S(1)}, u32[]{:S(2)}, u32[]{:S(2)}) %collective-permute-start.5) | collective-permute-done | bytes 147488 | tf_op jit(solution)/shard_map/ppermute | solution.py:323
  40.1 1.7 %collective-permute-done.7.refs_5_ = f32[288,128]{1,0:T(8,128)S(1)} collective-permute-done((f32[288,128]{1,0:T(8,128)}, f32[288,128]{1,0:T(8,128)S(1)}, u32[]{:S(2)}, u32[]{:S(2)}) %collective-permute-start.7) | collective-permute-done | bytes 147488 | tf_op jit(solution)/shard_map/ppermute | solution.py:323
  41.8 1.8 %collective-permute-done.9.refs_7_ = f32[288,128]{1,0:T(8,128)S(1)} collective-permute-done((f32[288,128]{1,0:T(8,128)}, f32[288,128]{1,0:T(8,128)S(1)}, u32[]{:S(2)}, u32[]{:S(2)}) %collective-permute-start.9) | collective-permute-done | bytes 147488 | tf_op jit(solution)/shard_map/ppermute | solution.py:323
  43.6 0.0 copy-done.1
  43.6 0.0 copy-done.2
  43.6 0.0 copy-done.3
  43.6 0.0 copy-done.4
  43.6 2.5 %source.1 = (f32[576,128]{1,0:T(8,128)S(1)}, f32[576,128]{1,0:T(8,128)S(1)}, f32[576,128]{1,0:T(8,128)S(1)}, f32[576,128]{1,0:T(8,128)S(1)}) custom-call(s32[4,64]{1,0:T(4,128)S(1)} %copy-done.3, f32[64]{0:T(128)S(1)} %copy-done.4, s32[1]{0:T(128)} %bitcast.turn, bf16[64,64,64]{2,1,0:T(8,128)(2,1)S(1)} %copy-done, bf16[64,64,64]{2,1,0:T(8,128)(2,1)S(1)} %bitcast.5, ...), custom_call_target="tpu_custom_call" | custom-call | tf_op jit(solution)/shard_map/source/pallas_call | solution.py:172
  46.1 0.1 collective-permute-start.10
  46.2 1.1 %collective-permute-start.11 = (f32[576,128]{1,0:T(8,128)S(1)}, f32[576,128]{1,0:T(8,128)S(1)}, u32[]{:S(2)}, u32[]{:S(2)}) collective-permute-start(f32[576,128]{1,0:T(8,128)S(1)} %get-tuple-element.33), channel_id=1, source_target_pairs={{0,8},{4,12},{8,0},{12,4},{1,9},{5,13},{9,1},{13,5},{2,10},{6,14},... | collective-permute-start | bytes 884744 | tf_op jit(solution)/shard_map/ppermute | solution.py:329
  47.3 1.3 %collective-permute-start.12 = (f32[576,128]{1,0:T(8,128)S(1)}, f32[576,128]{1,0:T(8,128)S(1)}, u32[]{:S(2)}, u32[]{:S(2)}) collective-permute-start(f32[576,128]{1,0:T(8,128)S(1)} %get-tuple-element.34), channel_id=1, source_target_pairs={{0,12},{4,0},{8,4},{12,8},{1,13},{5,1},{9,5},{13,9},{2,14},{6,2},{... | collective-permute-start | bytes 884744 | tf_op jit(solution)/shard_map/ppermute | solution.py:329
  48.6 6.5 %collective-permute-done.10.refs_1_ = f32[576,128]{1,0:T(8,128)S(1)} collective-permute-done((f32[576,128]{1,0:T(8,128)S(1)}, f32[576,128]{1,0:T(8,128)S(1)}, u32[]{:S(2)}, u32[]{:S(2)}) %collective-permute-start.10) | collective-permute-done | bytes 294944 | tf_op jit(solution)/shard_map/ppermute | solution.py:329
  55.1 16.8 %collective-permute-done.11.refs_2_ = f32[576,128]{1,0:T(8,128)S(1)} collective-permute-done((f32[576,128]{1,0:T(8,128)S(1)}, f32[576,128]{1,0:T(8,128)S(1)}, u32[]{:S(2)}, u32[]{:S(2)}) %collective-permute-start.11) | collective-permute-done | bytes 294944 | tf_op jit(solution)/shard_map/ppermute | solution.py:329
  71.9 1.2 %collective-permute-done.12.refs_3_ = f32[576,128]{1,0:T(8,128)S(1)} collective-permute-done((f32[576,128]{1,0:T(8,128)S(1)}, f32[576,128]{1,0:T(8,128)S(1)}, u32[]{:S(2)}, u32[]{:S(2)}) %collective-permute-start.12) | collective-permute-done | bytes 294944 | tf_op jit(solution)/shard_map/ppermute | solution.py:329
  73.0 1.2 %columns.1 = f32[576,512]{1,0:T(8,128)} custom-call(s32[1]{0:T(128)} %bitcast.turn, f32[576,128]{1,0:T(8,128)S(1)} %get-tuple-element.31.refs_0_, f32[576,128]{1,0:T(8,128)S(1)} %collective-permute-done.10.refs_1_, f32[576,128]{1,0:T(8,128)S(1)} %collective-permute-done.11.refs_2_, f32[576,128]{1,0:T(8,128)S(1)} %collective-permute-done.12.refs_3_), custom_call_target="tpu_custom_call" | custom-call | tf_op jit(solution)/shard_map/columns/pallas_call | solution.py:196
  (13 shorter events, 0.1 us)
Async XLA Ops:
  0.0 5.0 %copy-start.5 = (f32[576,512]{1,0:T(8,128)S(1)}, f32[576,512]{1,0:T(8,128)}, u32[]{:S(2)}) copy-start(f32[576,512]{1,0:T(8,128)} %cells.1) | copy-start | bytes 3538948
  0.0 7.8 %copy-start.7 = (f32[36]{0:T(128)S(1)}, f32[36]{0:T(128)}, u32[]{:S(2)}) copy-start(f32[36]{0:T(128)} %param.10) | copy-start | bytes 436
  0.0 8.0 %copy-start.6 = (s32[2304]{0:T(1024)S(1)}, s32[2304]{0:T(1024)}, u32[]{:S(2)}) copy-start(s32[2304]{0:T(1024)} %param.13) | copy-start | bytes 27652
  1.3 4.0 %collective-permute-start = (f32[296,512]{1,0:T(8,128)S(1)}, f32[296,512]{1,0:T(8,128)S(1)}, u32[]{:S(2)}, u32[]{:S(2)}) collective-permute-start(f32[296,512]{1,0:T(8,128)S(1)} %pack.1.refs_2_), channel_id=1, source_target_pairs={{0,1},{1,0},{2,3},{3,2},{4,5},{5,4},{6,7},{7,6},{8,9},{9,8},{10,11... | collective-permute-start | bytes 1818632 | tf_op jit(solution)/shard_map/ppermute | solution.py:219
  2.0 11.4 %collective-permute-start.1 = (f32[296,512]{1,0:T(8,128)S(1)}, f32[296,512]{1,0:T(8,128)S(1)}, u32[]{:S(2)}, u32[]{:S(2)}) collective-permute-start(f32[296,512]{1,0:T(8,128)S(1)} %pack.1.refs_2_), channel_id=1, source_target_pairs={{1,2},{2,1},{5,6},{6,5},{9,10},{10,9},{13,14},{14,13},{17,18},{18,... | collective-permute-start | bytes 1818632 | tf_op jit(solution)/shard_map/ppermute | solution.py:223
  5.1 18.5 %collective-permute-start.2 = (f32[288,512]{1,0:T(8,128)S(1)}, f32[288,512]{1,0:T(8,128)S(1)}, u32[]{:S(2)}, u32[]{:S(2)}) collective-permute-start(f32[288,512]{1,0:T(8,128)S(1)} %slice.3.refs_2_), channel_id=1, source_target_pairs={{0,1},{1,0},{2,3},{3,2},{4,5},{5,4},{6,7},{7,6},{8,9},{9,8},{10,11... | collective-permute-start | bytes 1769480 | tf_op jit(solution)/shard_map/ppermute | solution.py:219
  5.2 18.3 %collective-permute-start.3 = (f32[288,512]{1,0:T(8,128)S(1)}, f32[288,512]{1,0:T(8,128)}, u32[]{:S(2)}, u32[]{:S(2)}) collective-permute-start(f32[288,512]{1,0:T(8,128)S(1)} %slice.3.refs_2_), channel_id=1, source_target_pairs={{1,2},{2,1},{5,6},{6,5},{9,10},{10,9},{13,14},{14,13},{17,18},{18,... | collective-permute-start | bytes 1769480 | tf_op jit(solution)/shard_map/ppermute | solution.py:223
  19.8 14.6 %copy-start = (bf16[64,64,64]{2,1,0:T(8,128)(2,1)S(1)}, bf16[64,64,64]{2,1,0:T(8,128)(2,1)}, u32[]{:S(2)}) copy-start(bf16[64,64,64]{2,1,0:T(8,128)(2,1)} %blocks.1) | copy-start | bytes 1572868
  19.8 14.6 %collective-permute-start.4 = (f32[288,128]{1,0:T(8,128)S(1)}, f32[288,128]{1,0:T(8,128)S(1)}, u32[]{:S(2)}, u32[]{:S(2)}) collective-permute-start(f32[288,128]{1,0:T(8,128)S(1)} %get-tuple-element.25), channel_id=1, source_target_pairs={{0,4},{4,8},{8,12},{12,0},{1,5},{5,9},{9,13},{13,1},{2,6},{6,10},{... | collective-permute-start | bytes 442376 | tf_op jit(solution)/shard_map/ppermute | solution.py:323
  21.1 14.0 %collective-permute-start.6 = (f32[288,128]{1,0:T(8,128)}, f32[288,128]{1,0:T(8,128)S(1)}, u32[]{:S(2)}, u32[]{:S(2)}) collective-permute-start(f32[288,128]{1,0:T(8,128)} %get-tuple-element.27), channel_id=1, source_target_pairs={{0,8},{4,12},{8,0},{12,4},{1,9},{5,13},{9,1},{13,5},{2,10},{6,14},... | collective-permute-start | bytes 442376 | tf_op jit(solution)/shard_map/ppermute | solution.py:323
  22.1 13.0 %collective-permute-start.8 = (f32[288,128]{1,0:T(8,128)}, f32[288,128]{1,0:T(8,128)S(1)}, u32[]{:S(2)}, u32[]{:S(2)}) collective-permute-start(f32[288,128]{1,0:T(8,128)} %get-tuple-element.29), channel_id=1, source_target_pairs={{0,12},{4,0},{8,4},{12,8},{1,13},{5,1},{9,5},{13,9},{2,14},{6,2},{... | collective-permute-start | bytes 442376 | tf_op jit(solution)/shard_map/ppermute | solution.py:323
  31.1 12.4 %copy-start.1 = (f32[288,128]{1,0:T(8,128)S(1)}, f32[288,128]{1,0:T(8,128)}, u32[]{:S(2)}) copy-start(f32[288,128]{1,0:T(8,128)} %get-tuple-element.21.refs_0_) | copy-start | bytes 442372
  31.1 12.4 %copy-start.2 = (f32[288,128]{1,0:T(8,128)S(1)}, f32[288,128]{1,0:T(8,128)}, u32[]{:S(2)}) copy-start(f32[288,128]{1,0:T(8,128)} %get-tuple-element.24.refs_1_) | copy-start | bytes 442372
  31.1 12.4 %copy-start.3 = (s32[4,64]{1,0:T(4,128)S(1)}, s32[4,64]{1,0:T(4,128)}, u32[]{:S(2)}) copy-start(s32[4,64]{1,0:T(4,128)} %quad.1) | copy-start | bytes 3076
  31.1 12.4 %copy-start.4 = (f32[64]{0:T(128)S(1)}, f32[64]{0:T(128)}, u32[]{:S(2)}) copy-start(f32[64]{0:T(128)} %strength.1) | copy-start | bytes 772
  31.2 9.0 %collective-permute-start.5 = (f32[288,128]{1,0:T(8,128)}, f32[288,128]{1,0:T(8,128)S(1)}, u32[]{:S(2)}, u32[]{:S(2)}) collective-permute-start(f32[288,128]{1,0:T(8,128)} %get-tuple-element.26), channel_id=1, source_target_pairs={{0,4},{4,8},{8,12},{12,0},{1,5},{5,9},{9,13},{13,1},{2,6},{6,10},{... | collective-permute-start | bytes 442376 | tf_op jit(solution)/shard_map/ppermute | solution.py:323
  31.2 10.6 %collective-permute-start.7 = (f32[288,128]{1,0:T(8,128)}, f32[288,128]{1,0:T(8,128)S(1)}, u32[]{:S(2)}, u32[]{:S(2)}) collective-permute-start(f32[288,128]{1,0:T(8,128)} %get-tuple-element.28), channel_id=1, source_target_pairs={{0,8},{4,12},{8,0},{12,4},{1,9},{5,13},{9,1},{13,5},{2,10},{6,14},... | collective-permute-start | bytes 442376 | tf_op jit(solution)/shard_map/ppermute | solution.py:323
  34.4 9.2 %collective-permute-start.9 = (f32[288,128]{1,0:T(8,128)}, f32[288,128]{1,0:T(8,128)S(1)}, u32[]{:S(2)}, u32[]{:S(2)}) collective-permute-start(f32[288,128]{1,0:T(8,128)} %get-tuple-element.30), channel_id=1, source_target_pairs={{0,12},{4,0},{8,4},{12,8},{1,13},{5,1},{9,5},{13,9},{2,14},{6,2},{... | collective-permute-start | bytes 442376 | tf_op jit(solution)/shard_map/ppermute | solution.py:323
  46.1 8.9 %collective-permute-start.10 = (f32[576,128]{1,0:T(8,128)S(1)}, f32[576,128]{1,0:T(8,128)S(1)}, u32[]{:S(2)}, u32[]{:S(2)}) collective-permute-start(f32[576,128]{1,0:T(8,128)S(1)} %get-tuple-element.32), channel_id=1, source_target_pairs={{0,4},{4,8},{8,12},{12,0},{1,5},{5,9},{9,13},{13,1},{2,6},{6,10},{... | collective-permute-start | bytes 884744 | tf_op jit(solution)/shard_map/ppermute | solution.py:329
  46.2 25.7 %collective-permute-start.11 = (f32[576,128]{1,0:T(8,128)S(1)}, f32[576,128]{1,0:T(8,128)S(1)}, u32[]{:S(2)}, u32[]{:S(2)}) collective-permute-start(f32[576,128]{1,0:T(8,128)S(1)} %get-tuple-element.33), channel_id=1, source_target_pairs={{0,8},{4,12},{8,0},{12,4},{1,9},{5,13},{9,1},{13,5},{2,10},{6,14},... | collective-permute-start | bytes 884744 | tf_op jit(solution)/shard_map/ppermute | solution.py:329
  47.3 25.7 %collective-permute-start.12 = (f32[576,128]{1,0:T(8,128)S(1)}, f32[576,128]{1,0:T(8,128)S(1)}, u32[]{:S(2)}, u32[]{:S(2)}) collective-permute-start(f32[576,128]{1,0:T(8,128)S(1)} %get-tuple-element.34), channel_id=1, source_target_pairs={{0,12},{4,0},{8,4},{12,8},{1,13},{5,1},{9,5},{13,9},{2,14},{6,2},{... | collective-permute-start | bytes 884744 | tf_op jit(solution)/shard_map/ppermute | solution.py:329

commit v7 on v6

--- a/solution.py
+++ b/solution.py
@@ -282,7 +282,7 @@
 
 
 def cuts_of(row_count):
-    middle = row_count // 2 // 16 * 16
+    middle = row_count * 17 // 36 // 16 * 16
     return [(0, middle), (middle, row_count)]
 
 

time: 74.4 us -> 79.4 us (1.067)
  waiting for transfers between devices: 38.2 us -> 43.5 us
    ppermute x9, waiting for transfers between devices: 33 us -> 38.6 us  [shards(): lax.ppermute(piece, 'comp', [(i, (i + m) % peers) for i in range(peers)])]
  transfers between devices with their start and end apart: 13 -> 13, of which waited for: 7 -> 6; matrix products, arithmetic and copies ran while one was open for 1% -> 1% of each run, Pallas kernels for 19% -> 18%
where the time goes in v7:
time: 79.4 us; the launch traced here: 79.2 us
  waiting for transfers between devices  43.5 us (55%)
  Pallas kernels  18.8 us (24%)
  starting transfers between devices  15.5 us (20%)
  local copies, waits for them, and re-layouts  0.91 us (1%)
    ppermute x9, waiting for transfers between devices, shards(): lax.ppermute(piece, 'comp', [(i, (i + m) % peers) for i in range(peers)])  38.6 us
    pallas_call x2, Pallas kernels, propagate(): pl.pallas_call(functools.partial(propagate_kernel, first, low), out_shape...  13.9 us
    ppermute x9, starting transfers between devices, shards(): lax.ppermute(piece, 'comp', [(i, (i + m) % peers) for i in range(peers)])  9.18 us
    ppermute x2, starting transfers between devices, from_pairs(): far = lax.ppermute(held, 'space', pairs[1])  5.55 us
    ppermute x2, waiting for transfers between devices, from_pairs(): far = lax.ppermute(held, 'space', pairs[1])  4.91 us
    pallas_call x1, Pallas kernels, source_term(): pl.pallas_call(functools.partial(source_kernel, starts, step, len(pieces)...  2.51 us
  transfers between devices with their start and end apart: 13, of which 6 were waited for; matrix products, arithmetic and copies ran while one was open for 1% of the time, Pallas kernels for 18%

profile of v7, /device:TPU:13, one launch (start us, length us, event | category | flops | bytes accessed | tf_op | source)
XLA Modules:
  0.0 79.2 jit_solution(11513810019846533430)
XLA Ops:
  0.0 0.0 copy-start.5
  0.0 0.0 copy-start.6
  0.0 0.0 copy-start.7
  0.0 1.2 %pack.1.refs_2_ = f32[280,512]{1,0:T(8,128)S(1)} custom-call(s32[4,512]{1,0:T(4,128)} %neighbours.1, f32[1,512]{1,0:T(1,128)} %bitcast.6, f32[1,512]{1,0:T(1,128)} %bitcast.7, f32[576,512]{1,0:T(8,128)} %cells.1), custom_call_target="tpu_custom_call" | custom-call | tf_op jit(solution)/shard_map/pack/pallas_call | solution.py:258
  1.3 0.7 collective-permute-start
  2.0 3.0 %collective-permute-start.1 = (f32[280,512]{1,0:T(8,128)S(1)}, f32[280,512]{1,0:T(8,128)}, u32[]{:S(2)}, u32[]{:S(2)}) collective-permute-start(f32[280,512]{1,0:T(8,128)S(1)} %pack.1.refs_2_), channel_id=1, source_target_pairs={{1,2},{2,1},{5,6},{6,5},{9,10},{10,9},{13,14},{14,13},{17,18},{18,... | collective-permute-start | bytes 1720328 | tf_op jit(solution)/shard_map/ppermute | solution.py:223
  5.0 0.0 copy-done.5
  5.1 0.1 collective-permute-start.2
  5.2 0.0 copy-done.6
  5.2 0.0 collective-permute-done.refs_1_
  5.3 2.5 %collective-permute-start.3 = (f32[304,512]{1,0:T(8,128)S(1)}, f32[304,512]{1,0:T(8,128)S(1)}, u32[]{:S(2)}, u32[]{:S(2)}) collective-permute-start(f32[304,512]{1,0:T(8,128)S(1)} %slice.3.refs_2_), channel_id=1, source_target_pairs={{1,2},{2,1},{5,6},{6,5},{9,10},{10,9},{13,14},{14,13},{17,18},{18,... | collective-permute-start | bytes 1867784 | tf_op jit(solution)/shard_map/ppermute | solution.py:223
  7.8 0.0 copy-done.7
  7.8 0.1 broadcast_multiply_fusion
  7.9 0.1 mul.65
  8.0 0.1 mul.61
  8.1 0.1 fusion.2
  8.2 4.9 %collective-permute-done.1.refs_3_ = f32[280,512]{1,0:T(8,128)} collective-permute-done((f32[280,512]{1,0:T(8,128)S(1)}, f32[280,512]{1,0:T(8,128)}, u32[]{:S(2)}, u32[]{:S(2)}) %collective-permute-start.1) | collective-permute-done | bytes 573472 | tf_op jit(solution)/shard_map/ppermute | solution.py:223
  13.1 7.2 %propagate.2 = (f32[272,128]{1,0:T(8,128)}, f32[272,128]{1,0:T(8,128)S(1)}, f32[272,128]{1,0:T(8,128)}, f32[272,128]{1,0:T(8,128)}, f32[8,1536]{1,0:T(8,128)S(1)}) custom-call(s32[1]{0:T(128)} %bitcast.turn, s32[1]{0:T(128)} %bitcast.2.odd, f32[8,640]{1,0:T(8,128)S(1)} %pad.4.rows.refs_0_, f32[8,640]{1,0:T(8,128)S(1)} %pad.4.rows.refs_0_, ...), custom_call_target="tpu_custom_call" | custom-call | tf_op jit(solution)/shard_map/propagate/pallas_call | solution.py:113
  20.3 0.0 copy-start
  20.3 1.3 %collective-permute-start.4 = (f32[272,128]{1,0:T(8,128)S(1)}, f32[272,128]{1,0:T(8,128)S(1)}, u32[]{:S(2)}, u32[]{:S(2)}) collective-permute-start(f32[272,128]{1,0:T(8,128)S(1)} %get-tuple-element.25), channel_id=1, source_target_pairs={{0,4},{4,8},{8,12},{12,0},{1,5},{5,9},{9,13},{13,1},{2,6},{6,10},{... | collective-permute-start | bytes 417800 | tf_op jit(solution)/shard_map/ppermute | solution.py:323
  21.6 0.0 collective-permute-done.2.refs_1_
  21.6 0.0 collective-permute-done.3.refs_3_
  21.6 6.7 %propagate.3 = (f32[304,128]{1,0:T(8,128)}, f32[304,128]{1,0:T(8,128)}, f32[304,128]{1,0:T(8,128)}, f32[304,128]{1,0:T(8,128)S(1)}) custom-call(s32[1]{0:T(128)} %bitcast.turn, s32[1]{0:T(128)} %bitcast.2.odd, f32[8,640]{1,0:T(8,128)S(1)} %pad.4.rows.refs_0_, f32[8,1536]{1,0:T(8,128)S(1)} %get-tuple-element.22.refs_0_, ...), custom_call_target="tpu_custom_call" | custom-call | tf_op jit(solution)/shard_map/propagate/pallas_call | solution.py:113
  28.3 1.3 %collective-permute-start.5 = (f32[304,128]{1,0:T(8,128)}, f32[304,128]{1,0:T(8,128)S(1)}, u32[]{:S(2)}, u32[]{:S(2)}) collective-permute-start(f32[304,128]{1,0:T(8,128)} %get-tuple-element.26), channel_id=1, source_target_pairs={{0,4},{4,8},{8,12},{12,0},{1,5},{5,9},{9,13},{13,1},{2,6},{6,10},{... | collective-permute-start | bytes 466952 | tf_op jit(solution)/shard_map/ppermute | solution.py:323
  29.7 0.9 %collective-permute-start.7 = (f32[304,128]{1,0:T(8,128)}, f32[304,128]{1,0:T(8,128)S(1)}, u32[]{:S(2)}, u32[]{:S(2)}) collective-permute-start(f32[304,128]{1,0:T(8,128)} %get-tuple-element.28), channel_id=1, source_target_pairs={{0,8},{4,12},{8,0},{12,4},{1,9},{5,13},{9,1},{13,5},{2,10},{6,14},... | collective-permute-start | bytes 466952 | tf_op jit(solution)/shard_map/ppermute | solution.py:323
  30.6 0.3 collective-permute-start.9
  30.9 1.3 %collective-permute-start.6 = (f32[272,128]{1,0:T(8,128)}, f32[272,128]{1,0:T(8,128)S(1)}, u32[]{:S(2)}, u32[]{:S(2)}) collective-permute-start(f32[272,128]{1,0:T(8,128)} %get-tuple-element.27), channel_id=1, source_target_pairs={{0,8},{4,12},{8,0},{12,4},{1,9},{5,13},{9,1},{13,5},{2,10},{6,14},... | collective-permute-start | bytes 417800 | tf_op jit(solution)/shard_map/ppermute | solution.py:323
  32.2 0.0 collective-permute-done.4.refs_2_
  32.2 1.1 %collective-permute-start.8 = (f32[272,128]{1,0:T(8,128)}, f32[272,128]{1,0:T(8,128)S(1)}, u32[]{:S(2)}, u32[]{:S(2)}) collective-permute-start(f32[272,128]{1,0:T(8,128)} %get-tuple-element.29), channel_id=1, source_target_pairs={{0,12},{4,0},{8,4},{12,8},{1,13},{5,1},{9,5},{13,9},{2,14},{6,2},{... | collective-permute-start | bytes 417800 | tf_op jit(solution)/shard_map/ppermute | solution.py:323
  33.3 0.0 copy-done
  33.3 0.6 copy.10
  33.9 13.4 %collective-permute-done.6.refs_4_ = f32[272,128]{1,0:T(8,128)S(1)} collective-permute-done((f32[272,128]{1,0:T(8,128)}, f32[272,128]{1,0:T(8,128)S(1)}, u32[]{:S(2)}, u32[]{:S(2)}) %collective-permute-start.6) | collective-permute-done | bytes 139296 | tf_op jit(solution)/shard_map/ppermute | solution.py:323
  47.3 1.3 %collective-permute-done.8.refs_6_ = f32[272,128]{1,0:T(8,128)S(1)} collective-permute-done((f32[272,128]{1,0:T(8,128)}, f32[272,128]{1,0:T(8,128)S(1)}, u32[]{:S(2)}, u32[]{:S(2)}) %collective-permute-start.8) | collective-permute-done | bytes 139296 | tf_op jit(solution)/shard_map/ppermute | solution.py:323
  48.6 0.0 collective-permute-done.5.refs_3_
  48.6 0.0 collective-permute-done.7.refs_5_
  48.6 0.0 collective-permute-done.9.refs_7_
  48.6 0.0 copy-done.1
  48.6 0.0 copy-done.2
  48.6 0.0 copy-done.3
  48.6 0.0 copy-done.4
  48.6 2.5 %source.1 = (f32[576,128]{1,0:T(8,128)S(1)}, f32[576,128]{1,0:T(8,128)S(1)}, f32[576,128]{1,0:T(8,128)S(1)}, f32[576,128]{1,0:T(8,128)S(1)}) custom-call(s32[4,64]{1,0:T(4,128)S(1)} %copy-done.3, f32[64]{0:T(128)S(1)} %copy-done.4, s32[1]{0:T(128)} %bitcast.turn, bf16[64,64,64]{2,1,0:T(8,128)(2,1)S(1)} %copy-done, bf16[64,64,64]{2,1,0:T(8,128)(2,1)S(1)} %bitcast.5, ...), custom_call_target="tpu_custom_call" | custom-call | tf_op jit(solution)/shard_map/source/pallas_call | solution.py:172
  51.2 0.1 collective-permute-start.10
  51.2 1.8 %collective-permute-start.11 = (f32[576,128]{1,0:T(8,128)S(1)}, f32[576,128]{1,0:T(8,128)S(1)}, u32[]{:S(2)}, u32[]{:S(2)}) collective-permute-start(f32[576,128]{1,0:T(8,128)S(1)} %get-tuple-element.33), channel_id=1, source_target_pairs={{0,8},{4,12},{8,0},{12,4},{1,9},{5,13},{9,1},{13,5},{2,10},{6,14},... | collective-permute-start | bytes 884744 | tf_op jit(solution)/shard_map/ppermute | solution.py:329
  53.0 1.1 %collective-permute-start.12 = (f32[576,128]{1,0:T(8,128)S(1)}, f32[576,128]{1,0:T(8,128)S(1)}, u32[]{:S(2)}, u32[]{:S(2)}) collective-permute-start(f32[576,128]{1,0:T(8,128)S(1)} %get-tuple-element.34), channel_id=1, source_target_pairs={{0,12},{4,0},{8,4},{12,8},{1,13},{5,1},{9,5},{13,9},{2,14},{6,2},{... | collective-permute-start | bytes 884744 | tf_op jit(solution)/shard_map/ppermute | solution.py:329
  54.1 6.1 %collective-permute-done.10.refs_1_ = f32[576,128]{1,0:T(8,128)S(1)} collective-permute-done((f32[576,128]{1,0:T(8,128)S(1)}, f32[576,128]{1,0:T(8,128)S(1)}, u32[]{:S(2)}, u32[]{:S(2)}) %collective-permute-start.10) | collective-permute-done | bytes 294944 | tf_op jit(solution)/shard_map/ppermute | solution.py:329
  60.2 15.8 %collective-permute-done.11.refs_2_ = f32[576,128]{1,0:T(8,128)S(1)} collective-permute-done((f32[576,128]{1,0:T(8,128)S(1)}, f32[576,128]{1,0:T(8,128)S(1)}, u32[]{:S(2)}, u32[]{:S(2)}) %collective-permute-start.11) | collective-permute-done | bytes 294944 | tf_op jit(solution)/shard_map/ppermute | solution.py:329
  76.0 2.0 %collective-permute-done.12.refs_3_ = f32[576,128]{1,0:T(8,128)S(1)} collective-permute-done((f32[576,128]{1,0:T(8,128)S(1)}, f32[576,128]{1,0:T(8,128)S(1)}, u32[]{:S(2)}, u32[]{:S(2)}) %collective-permute-start.12) | collective-permute-done | bytes 294944 | tf_op jit(solution)/shard_map/ppermute | solution.py:329
  78.0 1.2 %columns.1 = f32[576,512]{1,0:T(8,128)} custom-call(s32[1]{0:T(128)} %bitcast.turn, f32[576,128]{1,0:T(8,128)S(1)} %get-tuple-element.31.refs_0_, f32[576,128]{1,0:T(8,128)S(1)} %collective-permute-done.10.refs_1_, f32[576,128]{1,0:T(8,128)S(1)} %collective-permute-done.11.refs_2_, f32[576,128]{1,0:T(8,128)S(1)} %collective-permute-done.12.refs_3_), custom_call_target="tpu_custom_call" | custom-call | tf_op jit(solution)/shard_map/columns/pallas_call | solution.py:196
  (13 shorter events, 0.2 us)
Async XLA Ops:
  0.0 5.0 %copy-start.5 = (f32[576,512]{1,0:T(8,128)S(1)}, f32[576,512]{1,0:T(8,128)}, u32[]{:S(2)}) copy-start(f32[576,512]{1,0:T(8,128)} %cells.1) | copy-start | bytes 3538948
  0.0 5.2 %copy-start.6 = (s32[2304]{0:T(1024)S(1)}, s32[2304]{0:T(1024)}, u32[]{:S(2)}) copy-start(s32[2304]{0:T(1024)} %param.13) | copy-start | bytes 27652
  0.0 7.8 %copy-start.7 = (f32[36]{0:T(128)S(1)}, f32[36]{0:T(128)}, u32[]{:S(2)}) copy-start(f32[36]{0:T(128)} %param.10) | copy-start | bytes 436
  1.3 4.0 %collective-permute-start = (f32[280,512]{1,0:T(8,128)S(1)}, f32[280,512]{1,0:T(8,128)S(1)}, u32[]{:S(2)}, u32[]{:S(2)}) collective-permute-start(f32[280,512]{1,0:T(8,128)S(1)} %pack.1.refs_2_), channel_id=1, source_target_pairs={{0,1},{1,0},{2,3},{3,2},{4,5},{5,4},{6,7},{7,6},{8,9},{9,8},{10,11... | collective-permute-start | bytes 1720328 | tf_op jit(solution)/shard_map/ppermute | solution.py:219
  2.0 11.1 %collective-permute-start.1 = (f32[280,512]{1,0:T(8,128)S(1)}, f32[280,512]{1,0:T(8,128)}, u32[]{:S(2)}, u32[]{:S(2)}) collective-permute-start(f32[280,512]{1,0:T(8,128)S(1)} %pack.1.refs_2_), channel_id=1, source_target_pairs={{1,2},{2,1},{5,6},{6,5},{9,10},{10,9},{13,14},{14,13},{17,18},{18,... | collective-permute-start | bytes 1720328 | tf_op jit(solution)/shard_map/ppermute | solution.py:223
  5.1 16.5 %collective-permute-start.2 = (f32[304,512]{1,0:T(8,128)S(1)}, f32[304,512]{1,0:T(8,128)S(1)}, u32[]{:S(2)}, u32[]{:S(2)}) collective-permute-start(f32[304,512]{1,0:T(8,128)S(1)} %slice.3.refs_2_), channel_id=1, source_target_pairs={{0,1},{1,0},{2,3},{3,2},{4,5},{5,4},{6,7},{7,6},{8,9},{9,8},{10,11... | collective-permute-start | bytes 1867784 | tf_op jit(solution)/shard_map/ppermute | solution.py:219
  5.3 16.4 %collective-permute-start.3 = (f32[304,512]{1,0:T(8,128)S(1)}, f32[304,512]{1,0:T(8,128)S(1)}, u32[]{:S(2)}, u32[]{:S(2)}) collective-permute-start(f32[304,512]{1,0:T(8,128)S(1)} %slice.3.refs_2_), channel_id=1, source_target_pairs={{1,2},{2,1},{5,6},{6,5},{9,10},{10,9},{13,14},{14,13},{17,18},{18,... | collective-permute-start | bytes 1867784 | tf_op jit(solution)/shard_map/ppermute | solution.py:223
  20.3 13.0 %copy-start = (bf16[64,64,64]{2,1,0:T(8,128)(2,1)S(1)}, bf16[64,64,64]{2,1,0:T(8,128)(2,1)}, u32[]{:S(2)}) copy-start(bf16[64,64,64]{2,1,0:T(8,128)(2,1)} %blocks.1) | copy-start | bytes 1572868
  20.3 11.9 %collective-permute-start.4 = (f32[272,128]{1,0:T(8,128)S(1)}, f32[272,128]{1,0:T(8,128)S(1)}, u32[]{:S(2)}, u32[]{:S(2)}) collective-permute-start(f32[272,128]{1,0:T(8,128)S(1)} %get-tuple-element.25), channel_id=1, source_target_pairs={{0,4},{4,8},{8,12},{12,0},{1,5},{5,9},{9,13},{13,1},{2,6},{6,10},{... | collective-permute-start | bytes 417800 | tf_op jit(solution)/shard_map/ppermute | solution.py:323
  28.3 20.3 %copy-start.1 = (f32[304,128]{1,0:T(8,128)S(1)}, f32[304,128]{1,0:T(8,128)}, u32[]{:S(2)}) copy-start(f32[304,128]{1,0:T(8,128)} %get-tuple-element.24.refs_1_) | copy-start | bytes 466948
  28.3 20.3 %copy-start.2 = (f32[272,128]{1,0:T(8,128)S(1)}, f32[272,128]{1,0:T(8,128)}, u32[]{:S(2)}) copy-start(f32[272,128]{1,0:T(8,128)} %get-tuple-element.21.refs_0_) | copy-start | bytes 417796
  28.3 20.3 %copy-start.3 = (s32[4,64]{1,0:T(4,128)S(1)}, s32[4,64]{1,0:T(4,128)}, u32[]{:S(2)}) copy-start(s32[4,64]{1,0:T(4,128)} %quad.1) | copy-start | bytes 3076
  28.3 20.3 %copy-start.4 = (f32[64]{0:T(128)S(1)}, f32[64]{0:T(128)}, u32[]{:S(2)}) copy-start(f32[64]{0:T(128)} %strength.1) | copy-start | bytes 772
  28.3 20.3 %collective-permute-start.5 = (f32[304,128]{1,0:T(8,128)}, f32[304,128]{1,0:T(8,128)S(1)}, u32[]{:S(2)}, u32[]{:S(2)}) collective-permute-start(f32[304,128]{1,0:T(8,128)} %get-tuple-element.26), channel_id=1, source_target_pairs={{0,4},{4,8},{8,12},{12,0},{1,5},{5,9},{9,13},{13,1},{2,6},{6,10},{... | collective-permute-start | bytes 466952 | tf_op jit(solution)/shard_map/ppermute | solution.py:323
  29.7 18.9 %collective-permute-start.7 = (f32[304,128]{1,0:T(8,128)}, f32[304,128]{1,0:T(8,128)S(1)}, u32[]{:S(2)}, u32[]{:S(2)}) collective-permute-start(f32[304,128]{1,0:T(8,128)} %get-tuple-element.28), channel_id=1, source_target_pairs={{0,8},{4,12},{8,0},{12,4},{1,9},{5,13},{9,1},{13,5},{2,10},{6,14},... | collective-permute-start | bytes 466952 | tf_op jit(solution)/shard_map/ppermute | solution.py:323
  30.6 18.0 %collective-permute-start.9 = (f32[304,128]{1,0:T(8,128)S(1)}, f32[304,128]{1,0:T(8,128)S(1)}, u32[]{:S(2)}, u32[]{:S(2)}) collective-permute-start(f32[304,128]{1,0:T(8,128)S(1)} %get-tuple-element.30), channel_id=1, source_target_pairs={{0,12},{4,0},{8,4},{12,8},{1,13},{5,1},{9,5},{13,9},{2,14},{6,2},{... | collective-permute-start | bytes 466952 | tf_op jit(solution)/shard_map/ppermute | solution.py:323
  30.9 16.4 %collective-permute-start.6 = (f32[272,128]{1,0:T(8,128)}, f32[272,128]{1,0:T(8,128)S(1)}, u32[]{:S(2)}, u32[]{:S(2)}) collective-permute-start(f32[272,128]{1,0:T(8,128)} %get-tuple-element.27), channel_id=1, source_target_pairs={{0,8},{4,12},{8,0},{12,4},{1,9},{5,13},{9,1},{13,5},{2,10},{6,14},... | collective-permute-start | bytes 417800 | tf_op jit(solution)/shard_map/ppermute | solution.py:323
  32.2 16.4 %collective-permute-start.8 = (f32[272,128]{1,0:T(8,128)}, f32[272,128]{1,0:T(8,128)S(1)}, u32[]{:S(2)}, u32[]{:S(2)}) collective-permute-start(f32[272,128]{1,0:T(8,128)} %get-tuple-element.29), channel_id=1, source_target_pairs={{0,12},{4,0},{8,4},{12,8},{1,13},{5,1},{9,5},{13,9},{2,14},{6,2},{... | collective-permute-start | bytes 417800 | tf_op jit(solution)/shard_map/ppermute | solution.py:323
  51.2 9.0 %collective-permute-start.10 = (f32[576,128]{1,0:T(8,128)S(1)}, f32[576,128]{1,0:T(8,128)S(1)}, u32[]{:S(2)}, u32[]{:S(2)}) collective-permute-start(f32[576,128]{1,0:T(8,128)S(1)} %get-tuple-element.32), channel_id=1, source_target_pairs={{0,4},{4,8},{8,12},{12,0},{1,5},{5,9},{9,13},{13,1},{2,6},{6,10},{... | collective-permute-start | bytes 884744 | tf_op jit(solution)/shard_map/ppermute | solution.py:329
  51.2 24.8 %collective-permute-start.11 = (f32[576,128]{1,0:T(8,128)S(1)}, f32[576,128]{1,0:T(8,128)S(1)}, u32[]{:S(2)}, u32[]{:S(2)}) collective-permute-start(f32[576,128]{1,0:T(8,128)S(1)} %get-tuple-element.33), channel_id=1, source_target_pairs={{0,8},{4,12},{8,0},{12,4},{1,9},{5,13},{9,1},{13,5},{2,10},{6,14},... | collective-permute-start | bytes 884744 | tf_op jit(solution)/shard_map/ppermute | solution.py:329
  53.0 25.0 %collective-permute-start.12 = (f32[576,128]{1,0:T(8,128)S(1)}, f32[576,128]{1,0:T(8,128)S(1)}, u32[]{:S(2)}, u32[]{:S(2)}) collective-permute-start(f32[576,128]{1,0:T(8,128)S(1)} %get-tuple-element.34), channel_id=1, source_target_pairs={{0,12},{4,0},{8,4},{12,8},{1,13},{5,1},{9,5},{13,9},{2,14},{6,2},{... | collective-permute-start | bytes 884744 | tf_op jit(solution)/shard_map/ppermute | solution.py:329
